TPU v7x, 32 devices: a whole 2x2x4 slice. The times are simulated.
32 devices in a mesh: dp: 16 (over z, y, x), tensor: 2 (over core).
Axes of the slice: x: 2, y: 2, z: 4, core: 2. Of those that a mesh axis runs over, the one named last changes fastest.
Arguments:
- tokens: bfloat16 [8192, 1536], P('dp'), may hold values from -6 to 6
- cotangent: bfloat16 [8192, 1536], P('dp'), may hold values from -6 to 6
- seq_offsets: int32 [6], replicated, may hold values from 0 to 5736, as said below
- block_offsets: int32 [17], replicated, may hold values from 0 to 5736, as said below
- image_mod: float32 [5, 6, 1536], replicated, may hold values from -4 to 4
- text_mod: float32 [5, 6, 1536], replicated, may hold values from -4 to 4
- image_qkv: bfloat16 [1536, 3, 1536], P('dp', None, 'tensor'), may hold values from -0.15625 to 0.15625
- text_qkv: bfloat16 [1536, 3, 1536], P('dp', None, 'tensor'), may hold values from -0.15625 to 0.15625
- image_out: bfloat16 [1536, 1536], P('tensor', 'dp'), may hold values from -0.4375 to 0.4375
- text_out: bfloat16 [1536, 1536], P('tensor', 'dp'), may hold values from -0.4375 to 0.4375
- image_fc1: bfloat16 [1536, 6144], P('dp', 'tensor'), may hold values from -0.15625 to 0.15625
- text_fc1: bfloat16 [1536, 6144], P('dp', 'tensor'), may hold values from -0.15625 to 0.15625
- image_fc2: bfloat16 [6144, 1536], P('tensor', 'dp'), may hold values from -0.109375 to 0.109375
- text_fc2: bfloat16 [6144, 1536], P('tensor', 'dp'), may hold values from -0.109375 to 0.109375
- clip_limits: float32 [24], P('tensor'), may hold values from 2 to 20
Outputs:
- mixed: bfloat16 [8192, 1536], P('dp')
- tokens_grad: float32 [8192, 1536], P('dp')
- image_mod_grad: float32 [5, 6, 1536], P(None, None, 'dp')
- text_mod_grad: float32 [5, 6, 1536], P(None, None, 'dp')
- image_qkv_grad: float32 [1536, 3, 1536], P('dp', None, 'tensor')
- text_qkv_grad: float32 [1536, 3, 1536], P('dp', None, 'tensor')
- image_out_grad: float32 [1536, 1536], P('tensor', 'dp')
- text_out_grad: float32 [1536, 1536], P('tensor', 'dp')
- image_fc1_grad: float32 [1536, 6144], P('dp', 'tensor')
- text_fc1_grad: float32 [1536, 6144], P('dp', 'tensor')
- image_fc2_grad: float32 [6144, 1536], P('tensor', 'dp')
- text_fc2_grad: float32 [6144, 1536], P('tensor', 'dp')
- head_max: float32 [24], P('tensor')
- image_clipped: bfloat16 [1536, 2, 1536], P('dp', None, 'tensor')
- text_clipped: bfloat16 [1536, 2, 1536], P('dp', None, 'tensor')
Inputs may be any that keep to these rules, and one draw needn't show every extreme that they name: seq_offsets[0] = 0 and rises; each sequence has 1024 image tokens followed by 77 to 154 text tokens, and some sequence has exactly 154; the last entry, the stream's length, is always 5 * 1101 + 462 // 2 and equals the last entry of block_offsets. block_offsets[0] = 0 and rises; every block of dp holds 256 to 512 live rows, its first ones, and some block holds exactly 512; the last entry is the stream's length.
All inputs are finite; a program needn't handle non-finite values.
Results may differ from a plain program's by a relative error of at most 0.014.
Values may be sent and summed in bfloat16 or wider, within the bound.
No kernel may reach another device: no remote copies, remote signals or barrier semaphores. Data moves between devices by JAX's collectives and lax.ppermute only.
A program may use at most 448 MiB of HBM per device.

v0:
```python
import jax
import jax.numpy as jnp
from jax import lax
from jax.sharding import PartitionSpec as P

HEAD = 64
IMG = 1024
TXT = 154


EPSILON = 1e-06
NEGATIVE = -1e30


def from_behind(value, axis, steps):
    count = lax.axis_size(axis)
    first, last = (max(0, -steps), min(count, count - steps))
    return lax.ppermute(value, axis, [(source, source + steps) for source in range(first, last)])


def matmul(left_part, right_part):
    return jnp.dot(left_part, right_part, preferred_element_type=jnp.float32)


def matmul_back(left_part, right_part):
    return lax.dot_general(
        left_part, right_part, (((1,), (1,)), ((), ())), preferred_element_type=jnp.float32
    )


def matmul_rows(left_part, right_part):
    return lax.dot_general(
        left_part, right_part, (((0,), (0,)), ((), ())), preferred_element_type=jnp.float32
    )


def exact_dot(left_part, right_part):
    return jnp.dot(
        left_part, right_part, precision=lax.Precision.HIGHEST, preferred_element_type=jnp.float32
    )


def exact_rows(left_part, right_part):
    return lax.dot_general(
        left_part,
        right_part,
        (((0,), (0,)), ((), ())),
        precision=lax.Precision.HIGHEST,
        preferred_element_type=jnp.float32,
    )


def row_info(device, seq_offsets, block_offsets, rows_cap, n_blocks):
    inside = (device >= 0) & (device < n_blocks)
    safe_device = jnp.clip(device, 0, n_blocks - 1)
    first_row = block_offsets[safe_device]
    row_count = block_offsets[safe_device + 1] - first_row
    row_ids = jnp.arange(rows_cap, dtype=jnp.int32)
    position = first_row + row_ids
    is_live = inside & (row_ids < row_count)
    seq_id = jnp.sum((position[:, None] >= seq_offsets[None, 1:-1]).astype(jnp.int32), axis=1)
    return (position, seq_id, is_live)


def by_kind(rows_bf, image_weight, text_weight, text_start, text_rows, product):
    whole = product(rows_bf, image_weight)
    part_rows = lax.dynamic_slice_in_dim(rows_bf, text_start, TXT, 0)
    text_result = product(part_rows, text_weight)
    previous = lax.dynamic_slice_in_dim(whole, text_start, TXT, 0)
    merged = jnp.where(text_rows[:, None], text_result, previous)
    return lax.dynamic_update_slice_in_dim(whole, merged, text_start, 0)


def kind_grads(left_rows, right_rows, text_start, text_rows, is_image):
    image_grad = matmul_rows(left_rows, jnp.where(is_image[:, None], right_rows, 0))
    text_grad = matmul_rows(
        lax.dynamic_slice_in_dim(left_rows, text_start, TXT, 0),
        jnp.where(text_rows[:, None], lax.dynamic_slice_in_dim(right_rows, text_start, TXT, 0), 0),
    )
    return (image_grad, text_grad)


def layer_norm(inputs):
    centered = inputs - jnp.mean(inputs, axis=1, keepdims=True)
    inverse_std = lax.rsqrt(jnp.mean(centered * centered, axis=1, keepdims=True) + EPSILON)
    return (centered * inverse_std, inverse_std)


def norm_back(grad_normed, normed, inverse_std):
    return inverse_std * (
        grad_normed
        - jnp.mean(grad_normed, axis=1, keepdims=True)
        - normed * jnp.mean(grad_normed * normed, axis=1, keepdims=True)
    )


def smooth_gelu(inputs):
    return jax.nn.gelu(inputs, approximate=True)


def column_block(inputs, which, width):
    return inputs[:, which * width : (which + 1) * width]


def pair_logits(queries, keys_piece, scale_factor):
    return (
        jnp.einsum("qhd,khd->hqk", queries, keys_piece, preferred_element_type=jnp.float32)
        * scale_factor
    )


def fetch(key_flat, value_flat, shift_by):
    return from_behind((key_flat, value_flat), "dp", shift_by)


def return_grads(key_part, value_part, shift_by):
    return (
        from_behind(key_part.astype(jnp.bfloat16), "dp", shift_by).astype(key_part.dtype),
        from_behind(value_part.astype(jnp.bfloat16), "dp", shift_by).astype(value_part.dtype),
    )


def local(
    tokens,
    cotangent,
    seq_offsets,
    block_offsets,
    image_mod,
    text_mod,
    image_qkv,
    text_qkv,
    image_out,
    text_out,
    image_fc1,
    text_fc1,
    image_fc2,
    text_fc2,
    clip_limits,
):
    rows_cap, model_width = tokens.shape
    columns = image_qkv.shape[2]
    width_share = image_qkv.shape[0]
    heads_here = columns // HEAD
    seq_count = seq_offsets.shape[0] - 1
    n_blocks = lax.axis_size("dp")
    device = lax.axis_index("dp")
    neighbours = (IMG + TXT - 2) // (rows_cap // 2) + 1
    scale_factor = HEAD ** (-0.5)
    gathered = (
        lax.all_gather(image_qkv, "dp", axis=0, tiled=True),
        lax.all_gather(text_qkv, "dp", axis=0, tiled=True),
        lax.all_gather(image_out, "dp", axis=1, tiled=True),
        lax.all_gather(text_out, "dp", axis=1, tiled=True),
        lax.all_gather(image_fc1, "dp", axis=0, tiled=True),
        lax.all_gather(text_fc1, "dp", axis=0, tiled=True),
        lax.all_gather(image_fc2, "dp", axis=1, tiled=True),
        lax.all_gather(text_fc2, "dp", axis=1, tiled=True),
    )
    image_weight = gathered[0].reshape(model_width, 3 * columns)
    text_weight = gathered[1].reshape(model_width, 3 * columns)
    image_proj, text_proj = (gathered[2], gathered[3])
    image_upper, text_upper = (gathered[4], gathered[5])
    image_lower, text_lower = (gathered[6], gathered[7])
    position, seq_id, is_live = row_info(device, seq_offsets, block_offsets, rows_cap, n_blocks)
    seq_hits = (seq_id[:, None] == jnp.arange(seq_count)[None, :]) & is_live[:, None]
    seq_start = jnp.sum(jnp.where(seq_hits, seq_offsets[None, :seq_count], 0), axis=1)
    is_text = is_live & (position >= seq_start + IMG)
    is_image = is_live & jnp.logical_not(is_text)
    text_flag = is_text.astype(jnp.float32)[:, None]
    seq_weight = seq_hits.astype(jnp.float32)
    pick_image = seq_weight * (1.0 - text_flag)
    pick_text = seq_weight * text_flag
    modulation = exact_dot(pick_image, image_mod.reshape(seq_count, 6 * model_width)) + exact_dot(
        pick_text, text_mod.reshape(seq_count, 6 * model_width)
    )
    shift_rows = column_block(modulation, 0, model_width)
    scale_rows = column_block(modulation, 1, model_width)
    gate_rows = column_block(modulation, 2, model_width)
    shift_mlp = column_block(modulation, 3, model_width)
    scale_mlp = column_block(modulation, 4, model_width)
    gate_mlp = column_block(modulation, 5, model_width)
    text_start = jnp.clip(jnp.argmax(is_text.astype(jnp.int32)), 0, rows_cap - TXT)
    text_rows = lax.dynamic_slice_in_dim(is_text, text_start, TXT, 0)
    stream = tokens.astype(jnp.float32)
    normed, inverse_std = layer_norm(stream)
    modulated = (normed * (1.0 + scale_rows) + shift_rows).astype(jnp.bfloat16)
    qkv = by_kind(modulated, image_weight, text_weight, text_start, text_rows, matmul).astype(
        jnp.bfloat16
    )
    queries = qkv[:, :columns].reshape(rows_cap, heads_here, HEAD)
    key_flat = qkv[:, columns : 2 * columns]
    value_flat = qkv[:, 2 * columns :]
    query_tag = jnp.where(is_live, seq_id, -2)
    pieces = [(0, key_flat, value_flat, jnp.where(is_live, seq_id, -1))]
    for step in range(1, neighbours + 1):
        for offset in (step, -step):
            keys_far, values_far = fetch(key_flat, value_flat, -offset)
            far_position, far_seq, far_live = row_info(
                device + offset, seq_offsets, block_offsets, rows_cap, n_blocks
            )
            pieces.append((offset, keys_far, values_far, jnp.where(far_live, far_seq, -1)))
    head_top = jnp.full((heads_here,), NEGATIVE, jnp.float32)
    running_max = jnp.full((heads_here, rows_cap), NEGATIVE, jnp.float32)
    running_sum = jnp.zeros((heads_here, rows_cap), jnp.float32)
    for offset, keys_piece, values_piece, key_tag in pieces:
        pair_mask = (query_tag[:, None] == key_tag[None, :])[None]
        logits = pair_logits(queries, keys_piece.reshape(rows_cap, heads_here, HEAD), scale_factor)
        masked = jnp.where(pair_mask, logits, NEGATIVE)
        head_top = jnp.maximum(head_top, jnp.max(masked, axis=(1, 2)))
        new_max = jnp.maximum(running_max, jnp.max(masked, axis=2))
        running_sum = running_sum * jnp.exp(running_max - new_max) + jnp.sum(
            jnp.where(pair_mask, jnp.exp(masked - new_max[:, :, None]), 0.0), axis=2
        )
        running_max = new_max
    log_total = running_max + jnp.log(jnp.where(running_sum > 0.0, running_sum, 1.0))
    attended = jnp.zeros((rows_cap, heads_here, HEAD), jnp.float32)
    for offset, keys_piece, values_piece, key_tag in pieces:
        pair_mask = (query_tag[:, None] == key_tag[None, :])[None]
        logits = pair_logits(queries, keys_piece.reshape(rows_cap, heads_here, HEAD), scale_factor)
        probs = jnp.where(pair_mask, jnp.exp(logits - log_total[:, :, None]), 0.0).astype(
            jnp.bfloat16
        )
        attended = attended + jnp.einsum(
            "hqk,khd->qhd",
            probs,
            values_piece.reshape(rows_cap, heads_here, HEAD),
            preferred_element_type=jnp.float32,
        )
    attended_flat = attended.reshape(rows_cap, columns).astype(jnp.bfloat16)
    head_max = lax.pmax(head_top, "dp")
    branch = lax.psum(
        by_kind(attended_flat, image_proj, text_proj, text_start, text_rows, matmul).astype(
            jnp.bfloat16
        ),
        "tensor",
    ).astype(jnp.float32)
    first = stream + gate_rows * branch
    normed_mlp, inverse_mlp = layer_norm(first)
    modulated_mlp = (normed_mlp * (1.0 + scale_mlp) + shift_mlp).astype(jnp.bfloat16)
    before_act = by_kind(modulated_mlp, image_upper, text_upper, text_start, text_rows, matmul)
    hidden = smooth_gelu(before_act).astype(jnp.bfloat16)
    mlp_branch = lax.psum(
        by_kind(hidden, image_lower, text_lower, text_start, text_rows, matmul).astype(
            jnp.bfloat16
        ),
        "tensor",
    ).astype(jnp.float32)
    mixed = jnp.where(is_live[:, None], first + gate_mlp * mlp_branch, 0.0).astype(jnp.bfloat16)
    grad_stream = jnp.where(is_live[:, None], cotangent.astype(jnp.float32), 0.0)
    grad_mlp = (gate_mlp * grad_stream).astype(jnp.bfloat16)
    grad_hidden = by_kind(
        grad_mlp, image_lower, text_lower, text_start, text_rows, matmul_back
    ).astype(jnp.bfloat16)
    lower_image_turned, lower_text_turned = kind_grads(
        grad_mlp, hidden, text_start, text_rows, is_image
    )
    act_pull = jax.vjp(smooth_gelu, before_act)[1]
    grad_before = act_pull(grad_hidden.astype(jnp.float32))[0].astype(jnp.bfloat16)
    upper_image_grad, upper_text_grad = kind_grads(
        modulated_mlp, grad_before, text_start, text_rows, is_image
    )
    grad_mod_mlp = lax.psum(
        by_kind(grad_before, image_upper, text_upper, text_start, text_rows, matmul_back).astype(
            jnp.bfloat16
        ),
        "tensor",
    ).astype(jnp.float32)
    grad_first = jnp.where(
        is_live[:, None],
        grad_stream + norm_back(grad_mod_mlp * (1.0 + scale_mlp), normed_mlp, inverse_mlp),
        0.0,
    )
    grad_branch = (gate_rows * grad_first).astype(jnp.bfloat16)
    grad_attended = by_kind(
        grad_branch, image_proj, text_proj, text_start, text_rows, matmul_back
    ).astype(jnp.bfloat16)
    proj_image_turned, proj_text_turned = kind_grads(
        grad_branch, attended_flat, text_start, text_rows, is_image
    )
    grad_heads = grad_attended.reshape(rows_cap, heads_here, HEAD)
    delta = jnp.einsum("qhd,qhd->hq", grad_heads.astype(jnp.float32), attended)
    query_grad = jnp.zeros((rows_cap, heads_here, HEAD), jnp.float32)
    key_total = jnp.zeros((rows_cap, columns), jnp.float32)
    value_total = jnp.zeros((rows_cap, columns), jnp.float32)
    for offset, keys_piece, values_piece, key_tag in pieces:
        pair_mask = (query_tag[:, None] == key_tag[None, :])[None]
        keys_heads = keys_piece.reshape(rows_cap, heads_here, HEAD)
        logits = pair_logits(queries, keys_heads, scale_factor)
        probs = jnp.where(pair_mask, jnp.exp(logits - log_total[:, :, None]), 0.0)
        grad_probs = jnp.einsum(
            "qhd,khd->hqk",
            grad_heads,
            values_piece.reshape(rows_cap, heads_here, HEAD),
            preferred_element_type=jnp.float32,
        )
        grad_logits = (probs * (grad_probs - delta[:, :, None])).astype(jnp.bfloat16)
        query_grad = (
            query_grad
            + jnp.einsum(
                "hqk,khd->qhd", grad_logits, keys_heads, preferred_element_type=jnp.float32
            )
            * scale_factor
        )
        key_part = (
            jnp.einsum("hqk,qhd->khd", grad_logits, queries, preferred_element_type=jnp.float32)
            * scale_factor
        ).reshape(rows_cap, columns)
        value_part = jnp.einsum(
            "hqk,qhd->khd",
            probs.astype(jnp.bfloat16),
            grad_heads,
            preferred_element_type=jnp.float32,
        ).reshape(rows_cap, columns)
        if offset == 0:
            key_total = key_part
            value_total = value_part
        else:
            back_keys, back_values = return_grads(key_part, value_part, offset)
            key_total = key_total + back_keys
            value_total = value_total + back_values
    grad_qkv = jnp.concatenate(
        [query_grad.reshape(rows_cap, columns), key_total, value_total], axis=1
    ).astype(jnp.bfloat16)
    qkv_image_grad, qkv_text_grad = kind_grads(modulated, grad_qkv, text_start, text_rows, is_image)
    grad_modulated = lax.psum(
        by_kind(grad_qkv, image_weight, text_weight, text_start, text_rows, matmul_back).astype(
            jnp.bfloat16
        ),
        "tensor",
    ).astype(jnp.float32)
    row_terms = (
        grad_modulated,
        grad_modulated * normed,
        grad_first * branch,
        grad_mod_mlp,
        grad_mod_mlp * normed_mlp,
        grad_stream * mlp_branch,
    )
    image_mod_turned = jnp.concatenate([exact_rows(term, pick_image) for term in row_terms], axis=1)
    text_mod_turned = jnp.concatenate([exact_rows(term, pick_text) for term in row_terms], axis=1)
    tokens_grad = jnp.where(
        is_live[:, None],
        grad_first + norm_back(grad_modulated * (1.0 + scale_rows), normed, inverse_std),
        0.0,
    )
    (
        qkv_image_sum,
        qkv_text_sum,
        proj_image_sum,
        proj_text_sum,
        upper_image_sum,
        upper_text_sum,
        lower_image_sum,
        lower_text_sum,
        mod_image_sum,
        mod_text_sum,
    ) = (
        lax.psum_scatter(qkv_image_grad, "dp", scatter_dimension=0, tiled=True),
        lax.psum_scatter(qkv_text_grad, "dp", scatter_dimension=0, tiled=True),
        lax.psum_scatter(proj_image_turned, "dp", scatter_dimension=0, tiled=True),
        lax.psum_scatter(proj_text_turned, "dp", scatter_dimension=0, tiled=True),
        lax.psum_scatter(upper_image_grad, "dp", scatter_dimension=0, tiled=True),
        lax.psum_scatter(upper_text_grad, "dp", scatter_dimension=0, tiled=True),
        lax.psum_scatter(lower_image_turned, "dp", scatter_dimension=0, tiled=True),
        lax.psum_scatter(lower_text_turned, "dp", scatter_dimension=0, tiled=True),
        lax.psum_scatter(image_mod_turned, "dp", scatter_dimension=0, tiled=True),
        lax.psum_scatter(text_mod_turned, "dp", scatter_dimension=0, tiled=True),
    )
    root_factor = jnp.sqrt(clip_limits / jnp.maximum(head_max, clip_limits))
    column_scale = jnp.repeat(root_factor, HEAD)[None, None, :]
    image_clipped = (image_qkv[:, :2, :].astype(jnp.float32) * column_scale).astype(jnp.bfloat16)
    text_clipped = (text_qkv[:, :2, :].astype(jnp.float32) * column_scale).astype(jnp.bfloat16)
    image_mod_out = jnp.transpose(mod_image_sum.reshape(width_share, 6, seq_count), (2, 1, 0))
    text_mod_out = jnp.transpose(mod_text_sum.reshape(width_share, 6, seq_count), (2, 1, 0))
    return (
        mixed,
        tokens_grad,
        image_mod_out,
        text_mod_out,
        qkv_image_sum.reshape(width_share, 3, columns),
        qkv_text_sum.reshape(width_share, 3, columns),
        jnp.transpose(proj_image_sum),
        jnp.transpose(proj_text_sum),
        upper_image_sum,
        upper_text_sum,
        jnp.transpose(lower_image_sum),
        jnp.transpose(lower_text_sum),
        head_max,
        image_clipped,
        text_clipped,
    )


def solution(mesh):
    placed = (
        P("dp", None),
        P("dp", None),
        P(),
        P(),
        P(),
        P(),
        P("dp", None, "tensor"),
        P("dp", None, "tensor"),
        P("tensor", "dp"),
        P("tensor", "dp"),
        P("dp", "tensor"),
        P("dp", "tensor"),
        P("tensor", "dp"),
        P("tensor", "dp"),
        P("tensor"),
    )
    return jax.shard_map(
        local,
        mesh=mesh,
        in_specs=placed,
        out_specs=(
            P("dp", None),
            P("dp", None),
            P(None, None, "dp"),
            P(None, None, "dp"),
            P("dp", None, "tensor"),
            P("dp", None, "tensor"),
            P("tensor", "dp"),
            P("tensor", "dp"),
            P("dp", "tensor"),
            P("dp", "tensor"),
            P("tensor", "dp"),
            P("tensor", "dp"),
            P("tensor"),
            P("dp", None, "tensor"),
            P("dp", None, "tensor"),
        ),
        check_vma=False,
    )
```

profile of v0, /device:TPU:0, one launch (start us, length us, event | category | flops | bytes accessed | tf_op | source)
XLA Modules:
  0.0 3970.1 jit_solution(11799543725549656592)
XLA Ops:
  63.1 19.4 convolution_add_fusion
  89.8 25.0 all-gather.9.cloned.1.call-done
  133.2 84.0 %all-gather.11.cloned.1.call-done = bf16[1536,3,768]{2,0,1:T(8,128)(2,1)} async-done(((bf16[96,3,768]{2,0,1:T(8,128)(2,1)}), bf16[1536,3,768]{2,0,1:T(8,128)(2,1)}) %all-gather.11.cloned.1.call-update) | async-done | bytes 7077904 | tf_op jit(solution)/shard_map/all_gather | solution.py:151
  329.9 19.6 collective-permute-start.1
  381.8 18.6 collective-permute-start.17
  421.3 18.5 collective-permute-start.15
  671.6 24.8 all-reduce.5.cloned.1.call-done
  707.0 116.2 %all-gather.17.cloned.1.call-done = bf16[1536,3072]{1,0:T(8,128)(2,1)} async-done(((bf16[96,3072]{1,0:T(8,128)(2,1)}), bf16[1536,3072]{1,0:T(8,128)(2,1)}) %all-gather.17.cloned.1.call-update) | async-done | bytes 9437200 | tf_op jit(solution)/shard_map/all_gather | solution.py:154
  832.9 114.1 %all-gather.19.cloned.1.call-done = bf16[1536,3072]{1,0:T(8,128)(2,1)} async-done(((bf16[96,3072]{1,0:T(8,128)(2,1)}), bf16[1536,3072]{1,0:T(8,128)(2,1)}) %all-gather.19.cloned.1.call-update) | async-done | bytes 9437200 | tf_op jit(solution)/shard_map/all_gather | solution.py:155
  960.3 110.6 %all-gather.21.cloned.1.call-done = bf16[3072,1536]{0,1:T(8,128)(2,1)} async-done(((bf16[3072,96]{0,1:T(8,128)(2,1)}), bf16[3072,1536]{0,1:T(8,128)(2,1)}) %all-gather.21.cloned.1.call-update) | async-done | bytes 9437200 | tf_op jit(solution)/shard_map/all_gather | solution.py:156
  1080.1 114.7 %all-gather.23.cloned.1.call-done = bf16[3072,1536]{0,1:T(8,128)(2,1)} async-done(((bf16[3072,96]{0,1:T(8,128)(2,1)}), bf16[3072,1536]{0,1:T(8,128)(2,1)}) %all-gather.23.cloned.1.call-update) | async-done | bytes 9437200 | tf_op jit(solution)/shard_map/all_gather | solution.py:157
  1573.7 29.7 collective-permute-done.34
  1604.6 35.9 collective-permute-start.28
  1698.0 25.2 collective-permute-done.24
  1896.5 42.0 %pmax.7 = f32[12]{0:T(128)S(1)} all-reduce(f32[12]{0:T(128)S(1)} %maximum_maximum_fusion), channel_id=1, replica_groups=mesh['dp'=16,'tensor'=2] {'dp'}, use_global_device_ids=true, to_apply=%region_68.69 | all-reduce | flops 12 | bytes 96 | tf_op jit(solution)/shard_map/pmax | solution.py:230
  1952.3 105.9 %reduce-scatter.33.cloned.1.call-done = f32[96,30]{1,0:T(8,128)} async-done(((f32[1536,30]{1,0:T(8,128)}), f32[96,30]{1,0:T(8,128)}) %reduce-scatter.33.cloned.1.call-update) | async-done | bytes 11536
  2059.8 225.5 %reduce-scatter.15.cloned.1.call-done = f32[96,2304]{1,0:T(8,128)} async-done(((f32[1536,2304]{1,0:T(8,128)}), f32[96,2304]{1,0:T(8,128)}) %reduce-scatter.15.cloned.1.call-update) | async-done | bytes 884752 | tf_op jit(solution)/shard_map/reduce_scatter | solution.py:358
  2287.5 224.0 %reduce-scatter.17.cloned.1.call-done = f32[96,2304]{1,0:T(8,128)} async-done(((f32[1536,2304]{1,0:T(8,128)}), f32[96,2304]{1,0:T(8,128)}) %reduce-scatter.17.cloned.1.call-update) | async-done | bytes 884752 | tf_op jit(solution)/shard_map/reduce_scatter | solution.py:359
  2513.6 140.1 %reduce-scatter.19.cloned.1.call-done = f32[96,768]{1,0:T(8,128)} async-done(((f32[1536,768]{1,0:T(8,128)}), f32[96,768]{1,0:T(8,128)}) %reduce-scatter.19.cloned.1.call-update) | async-done | bytes 294928 | tf_op jit(solution)/shard_map/reduce_scatter | solution.py:360
  2653.7 141.4 %reduce-scatter.21.cloned.1.call-done = f32[96,768]{1,0:T(8,128)} async-done(((f32[1536,768]{1,0:T(8,128)}), f32[96,768]{1,0:T(8,128)}) %reduce-scatter.21.cloned.1.call-update) | async-done | bytes 294928 | tf_op jit(solution)/shard_map/reduce_scatter | solution.py:361
  2795.1 292.0 %reduce-scatter.23.cloned.1.call-done = f32[96,3072]{1,0:T(8,128)} async-done(((f32[1536,3072]{1,0:T(8,128)}), f32[96,3072]{1,0:T(8,128)}) %reduce-scatter.23.cloned.1.call-update) | async-done | bytes 1179664 | tf_op jit(solution)/shard_map/reduce_scatter | solution.py:362
  3087.1 292.1 %reduce-scatter.25.cloned.1.call-done = f32[96,3072]{1,0:T(8,128)} async-done(((f32[1536,3072]{1,0:T(8,128)}), f32[96,3072]{1,0:T(8,128)}) %reduce-scatter.25.cloned.1.call-update) | async-done | bytes 1179664 | tf_op jit(solution)/shard_map/reduce_scatter | solution.py:363
  3379.2 291.9 %reduce-scatter.27.cloned.1.call-done = f32[96,3072]{1,0:T(8,128)} async-done(((f32[1536,3072]{1,0:T(8,128)}), f32[96,3072]{1,0:T(8,128)}) %reduce-scatter.27.cloned.1.call-update) | async-done | bytes 1179664 | tf_op jit(solution)/shard_map/reduce_scatter | solution.py:364
  3671.1 291.9 %reduce-scatter.29.cloned.1.call-done = f32[96,3072]{1,0:T(8,128)} async-done(((f32[1536,3072]{1,0:T(8,128)}), f32[96,3072]{1,0:T(8,128)}) %reduce-scatter.29.cloned.1.call-update) | async-done | bytes 1179664 | tf_op jit(solution)/shard_map/reduce_scatter | solution.py:365
  (845 shorter events, 1134.9 us)
Async XLA Ops:
  7.9 209.2 %all-gather.11.cloned.1.call-start = ((), (), s32[]{:S(2)}) async-start(), calls=%async_computation.11 | async-start | bytes 7520256 | tf_op jit(solution)/shard_map/all_gather | solution.py:151
  8.7 649.9 %all-gather.13.cloned.1.call-start = ((), (), s32[]{:S(2)}) async-start(), calls=%async_computation.12 | async-start | bytes 2506752 | tf_op jit(solution)/shard_map/all_gather | solution.py:152
  9.4 652.6 %all-gather.15.cloned.1.call-start = ((), (), s32[]{:S(2)}) async-start(), calls=%async_computation.13 | async-start | bytes 2506752 | tf_op jit(solution)/shard_map/all_gather | solution.py:153
  10.0 686.5 %all-reduce.5.cloned.1.call-start = ((), (), s32[]{:S(2)}) async-start(), calls=%async_computation.14 | async-start | bytes 3145728 | tf_op jit(solution)/shard_map/psum | solution.py:231
  254.7 268.4 %collective-permute-start.19 = (bf16[512,768]{1,0:T(8,128)(2,1)S(1)}, bf16[512,768]{1,0:T(8,128)(2,1)}, u32[]{:S(2)}, u32[]{:S(2)}) collective-permute-start(bf16[512,768]{1,0:T(8,128)(2,1)S(1)} %get-tuple-element.142), channel_id=1, source_target_pairs={{0,10},{2,12},{4,14},{6,16},{8,18},{10,20},{12,22},{14,24},{16,26}... | collective-permute-start | bytes 2359304 | tf_op jit(solution)/shard_map/ppermute | solution.py:18
  370.4 155.5 %collective-permute-start.18 = (bf16[512,768]{1,0:T(8,128)(2,1)S(1)}, bf16[512,768]{1,0:T(8,128)(2,1)}, u32[]{:S(2)}, u32[]{:S(2)}) collective-permute-start(bf16[512,768]{1,0:T(8,128)(2,1)S(1)} %get-tuple-element.142), channel_id=1, source_target_pairs={{10,0},{12,2},{14,4},{16,6},{18,8},{20,10},{22,12},{24,14},{26,16}... | collective-permute-start | bytes 2359304 | tf_op jit(solution)/shard_map/ppermute | solution.py:18
  381.8 153.6 %collective-permute-start.17 = (bf16[512,768]{1,0:T(8,128)(2,1)S(1)}, bf16[512,768]{1,0:T(8,128)(2,1)}, u32[]{:S(2)}, u32[]{:S(2)}) collective-permute-start(bf16[512,768]{1,0:T(8,128)(2,1)S(1)} %get-tuple-element.142), channel_id=1, source_target_pairs={{0,8},{2,10},{4,12},{6,14},{8,16},{10,18},{12,20},{14,22},{16,24},... | collective-permute-start | bytes 2359304 | tf_op jit(solution)/shard_map/ppermute | solution.py:18
  421.3 141.7 %collective-permute-start.15 = (bf16[512,768]{1,0:T(8,128)(2,1)S(1)}, bf16[512,768]{1,0:T(8,128)(2,1)}, u32[]{:S(2)}, u32[]{:S(2)}) collective-permute-start(bf16[512,768]{1,0:T(8,128)(2,1)S(1)} %get-tuple-element.142), channel_id=1, source_target_pairs={{0,6},{2,8},{4,10},{6,12},{8,14},{10,16},{12,18},{14,20},{16,22},{... | collective-permute-start | bytes 2359304 | tf_op jit(solution)/shard_map/ppermute | solution.py:18
  668.7 154.4 %all-gather.17.cloned.1.call-start = ((), (), s32[]{:S(2)}) async-start(), calls=%async_computation.15 | async-start | bytes 10027008 | tf_op jit(solution)/shard_map/all_gather | solution.py:154
  669.3 277.7 %all-gather.19.cloned.1.call-start = ((), (), s32[]{:S(2)}) async-start(), calls=%async_computation.16 | async-start | bytes 10027008 | tf_op jit(solution)/shard_map/all_gather | solution.py:155
  670.1 400.8 %all-gather.21.cloned.1.call-start = ((), (), s32[]{:S(2)}) async-start(), calls=%async_computation.17 | async-start | bytes 10027008 | tf_op jit(solution)/shard_map/all_gather | solution.py:156
  670.8 523.9 %all-gather.23.cloned.1.call-start = ((), (), s32[]{:S(2)}) async-start(), calls=%async_computation.18 | async-start | bytes 10027008 | tf_op jit(solution)/shard_map/all_gather | solution.py:157
  671.6 584.4 %all-reduce.7.cloned.1.call-start = ((), (), s32[]{:S(2)}) async-start(), calls=%async_computation.19 | async-start | bytes 3145728 | tf_op jit(solution)/shard_map/psum | solution.py:262
  1233.5 552.7 %all-reduce.9.cloned.1.call-start = ((), (), s32[]{:S(2)}) async-start(), calls=%async_computation.30 | async-start | bytes 6291456 | tf_op jit(solution)/shard_map/psum | solution.py:242
  1752.3 198.5 %reduce-scatter.31.cloned.1.call-start = ((), (), s32[]{:S(2)}) async-start(), calls=%async_computation.28 | async-start | bytes 835584
  1807.5 250.8 %reduce-scatter.33.cloned.1.call-start = ((), (), s32[]{:S(2)}) async-start(), calls=%async_computation.29 | async-start | bytes 835584
  1818.4 466.9 %reduce-scatter.15.cloned.1.call-start = ((), (), s32[]{:S(2)}) async-start(), calls=%async_computation.20 | async-start | bytes 15040512 | tf_op jit(solution)/shard_map/reduce_scatter | solution.py:358
  1829.6 681.8 %reduce-scatter.17.cloned.1.call-start = ((), (), s32[]{:S(2)}) async-start(), calls=%async_computation.21 | async-start | bytes 15040512 | tf_op jit(solution)/shard_map/reduce_scatter | solution.py:359
  1838.3 815.4 %reduce-scatter.19.cloned.1.call-start = ((), (), s32[]{:S(2)}) async-start(), calls=%async_computation.22 | async-start | bytes 5013504 | tf_op jit(solution)/shard_map/reduce_scatter | solution.py:360
  1843.5 951.6 %reduce-scatter.21.cloned.1.call-start = ((), (), s32[]{:S(2)}) async-start(), calls=%async_computation.23 | async-start | bytes 5013504 | tf_op jit(solution)/shard_map/reduce_scatter | solution.py:361
  1849.8 1237.3 %reduce-scatter.23.cloned.1.call-start = ((), (), s32[]{:S(2)}) async-start(), calls=%async_computation.24 | async-start | bytes 20054016 | tf_op jit(solution)/shard_map/reduce_scatter | solution.py:362
  1861.1 1518.1 %reduce-scatter.25.cloned.1.call-start = ((), (), s32[]{:S(2)}) async-start(), calls=%async_computation.25 | async-start | bytes 20054016 | tf_op jit(solution)/shard_map/reduce_scatter | solution.py:363
  1871.6 1799.5 %reduce-scatter.27.cloned.1.call-start = ((), (), s32[]{:S(2)}) async-start(), calls=%async_computation.26 | async-start | bytes 20054016 | tf_op jit(solution)/shard_map/reduce_scatter | solution.py:364
  1883.0 2080.0 %reduce-scatter.29.cloned.1.call-start = ((), (), s32[]{:S(2)}) async-start(), calls=%async_computation.27 | async-start | bytes 20054016 | tf_op jit(solution)/shard_map/reduce_scatter | solution.py:365
  (262 other events, 8182.7 us)
Sparse Core Ops, SparseCore 0:
  10.7 104.0 all-gather.8
  117.5 99.6 all-gather.10
  220.0 141.2 all-gather.12
  363.9 113.3 all-gather.14
  668.9 27.5 all-reduce.4
  699.5 123.6 all-gather.16
  826.3 120.6 all-gather.18
  950.2 120.6 all-gather.20
  1074.1 120.6 all-gather.22
  1233.7 18.5 all-reduce.6
  1752.4 33.7 all-reduce.8
  1807.6 123.3 reduce-scatter.30
  1937.0 121.2 reduce-scatter.32
  2064.9 220.3 reduce-scatter.14
  2290.9 220.4 reduce-scatter.16
  2517.8 135.8 reduce-scatter.18
  2659.3 135.7 reduce-scatter.20
  2802.3 284.7 reduce-scatter.22
  3094.4 284.7 reduce-scatter.24
  3386.4 284.7 reduce-scatter.26
  3678.5 284.5 reduce-scatter.28
where the time goes:
time: 3990 us; the launch traced here: 3970 us
  waiting for transfers between devices  2710 us (68%)
  matrix products  650 us (16%)
  starting transfers between devices  210 us (5%)
  local copies, waits for them, and re-layouts  185 us (5%)
  other arithmetic  139 us (3%)
  blocking collectives  42 us (1%)
    reduce_scatter x1, waiting for transfers between devices, local(): lax.psum_scatter(upper_text_grad, 'dp', scatter_dimension=0, tiled=True)  292 us
    reduce_scatter x1, waiting for transfers between devices, local(): lax.psum_scatter(upper_image_grad, 'dp', scatter_dimension=0, tiled=True)  292 us
    reduce_scatter x1, waiting for transfers between devices, local(): lax.psum_scatter(lower_image_turned, 'dp', scatter_dimension=0, tiled=True)  292 us
    reduce_scatter x1, waiting for transfers between devices, local(): lax.psum_scatter(lower_text_turned, 'dp', scatter_dimension=0, tiled=True)  292 us
    reduce_scatter x1, waiting for transfers between devices, local(): lax.psum_scatter(qkv_image_grad, 'dp', scatter_dimension=0, tiled=True)  226 us
    reduce_scatter x1, waiting for transfers between devices, local(): lax.psum_scatter(qkv_text_grad, 'dp', scatter_dimension=0, tiled=True)  224 us
    ppermute x40, starting transfers between devices, from_behind(): lax.ppermute(value, axis, [(source, source + steps) for source in range(f...  209 us
    reduce_scatter x1, waiting for transfers between devices, local(): lax.psum_scatter(proj_text_turned, 'dp', scatter_dimension=0, tiled=True)  141 us
  transfers between devices with their start and end apart: 61, of which 26 were waited for; matrix products, arithmetic and copies ran while one was open for 17% of the time, Pallas kernels for 0%

commit v1 on v0

v1 whole, which is shorter than its diff:
```python
import jax
import jax.numpy as jnp
from jax import lax
from jax.experimental import pallas as pl
from jax.experimental.pallas import tpu as pltpu
from jax.sharding import Mesh, PartitionSpec as P

HEAD = 64
IMG = 1024
TXT = 154
EPSILON = 1e-06
NEGATIVE = -1e30
BLOCKS = 4
SUB = 128
TAIL = 1184
TAIL_PAD = 1280
EDGE = 160
CHUNK = 256
ALIGN = 16
BF = jnp.bfloat16
F32 = jnp.float32
SWAP = [(0, 1), (1, 0)]
VMEM_LIMIT = 60 * 1024 * 1024

VMEM = pl.BlockSpec(memory_space=pltpu.VMEM)
SMEM = pl.BlockSpec(memory_space=pltpu.SMEM)

COUNT, OFFSET, TEXT_FROM, TEXT_TO = 0, 4, 8, 12
CORE, TAIL_FROM, EDGE_FROM = 16, 17, 18


def dot(a, b):
    return jnp.dot(a, b, preferred_element_type=F32)


def dot_back(a, b):
    return lax.dot_general(a, b, (((1,), (1,)), ((), ())), preferred_element_type=F32)


def dot_rows(a, b):
    return lax.dot_general(a, b, (((0,), (0,)), ((), ())), preferred_element_type=F32)


def call(body, out_shape, n_in, scratch=(), flops=0, moved=0):
    return pl.pallas_call(
        body,
        out_shape=out_shape,
        in_specs=[SMEM] + [VMEM] * (n_in - 1),
        out_specs=jax.tree.map(lambda _: VMEM, out_shape),
        scratch_shapes=list(scratch),
        compiler_params=pltpu.CompilerParams(vmem_limit_bytes=VMEM_LIMIT),
        cost_estimate=pl.CostEstimate(flops=flops, bytes_accessed=moved, transcendentals=0),
    )


def for_tiles(info, half, body, empty=None):
    def step(j, carry):
        for side in (0, 1):
            base = (info[CORE] if side == 0 else 1 - info[CORE]) * half
            live = info[COUNT + j] - base

            @pl.when(live > SUB)
            def _():
                body(j, side, base, half)

            @pl.when((live > 0) & (live <= SUB))
            def _():
                body(j, side, base, SUB)

            if empty is not None:

                @pl.when(live <= 0)
                def _():
                    empty(j, side)

        return carry

    lax.fori_loop(0, BLOCKS, step, 0)


def row_ids(base, rows):
    return base + lax.broadcasted_iota(jnp.int32, (rows, 1), 0)


def for_text(info, j, base, rows, body):
    for u in range(rows // SUB):
        low = base + u * SUB

        @pl.when((info[TEXT_FROM + j] < low + SUB) & (info[TEXT_TO + j] > low))
        def _():
            ids = row_ids(low, SUB)
            body(u, (ids >= info[TEXT_FROM + j]) & (ids < info[TEXT_TO + j]))


def window(start, rows, total):
    base = jnp.minimum(lax.shift_right_logical(start, 4) * ALIGN, total - rows - ALIGN)
    return pl.ds(pl.multiple_of(base, ALIGN), rows + ALIGN), start - base


def moved(part, skip):
    rows = part.shape[0]
    shape = (rows + ALIGN, rows)
    there = lax.broadcasted_iota(jnp.int32, shape, 0) - skip
    return dot((there == lax.broadcasted_iota(jnp.int32, shape, 1)).astype(F32).astype(BF), part)


def read_rows(ref, start, rows):
    place, skip = window(start, rows, ref.shape[0])
    shape = (rows, rows + ALIGN)
    here = lax.broadcasted_iota(jnp.int32, shape, 1) - skip
    pick = (here == lax.broadcasted_iota(jnp.int32, shape, 0)).astype(F32).astype(BF)
    return dot(pick, ref[place, :]).astype(BF)


def slots_to_rows(info, own, oth, w_image, w_text, out, tile):
    half = own.shape[1]
    out[...] = jnp.zeros_like(out)

    def body(j, side, base, rows):
        x = (own, oth)[side]
        tile[:rows, :] = dot(x[j, :rows, :], w_image[...])

        def text(u, is_text):
            part = slice(u * SUB, (u + 1) * SUB)
            tile[part, :] = jnp.where(is_text, dot(x[j, part, :], w_text[...]), tile[part, :])

        for_text(info, j, base, rows, text)
        place, skip = window(info[OFFSET + j] + base, rows, out.shape[0])
        part = moved(tile[:rows, :].astype(BF), skip)
        ids = row_ids(base - skip, rows + ALIGN)
        stop = jnp.minimum(info[COUNT + j], base + rows)
        out[place, :] = jnp.where((ids >= base) & (ids < stop), part, out[place, :].astype(F32)).astype(BF)

    for_tiles(info, half, body)


def rows_to_slots(info, rows_ref, w_image, w_text, own, oth):
    half = own.shape[1]

    def body(j, side, base, rows):
        out = (own, oth)[side]
        x = read_rows(rows_ref, info[OFFSET + j] + base, rows)
        out[j, :rows, :] = dot_back(x, w_image[...]).astype(BF)
        if rows < half:
            out[j, rows:, :] = jnp.zeros((half - rows, out.shape[2]), BF)

        def text(u, is_text):
            part = slice(u * SUB, (u + 1) * SUB)
            out[j, part, :] = jnp.where(
                is_text, dot_back(x[part], w_text[...]).astype(BF), out[j, part, :]
            )

        for_text(info, j, base, rows, text)

    def empty(j, side):
        out = (own, oth)[side]
        out[j] = jnp.zeros(out.shape[1:], BF)

    for_tiles(info, half, body, empty)


def slots_to_slots(info, x_own, x_oth, w, own, oth):
    half = own.shape[1]
    cut = w.shape[1] // 2

    def body(j, side, base, rows):
        x, out = (x_own, x_oth)[side], (own, oth)[side]
        out[j, :rows, :] = dot_back(x[j, :rows, :], w[:, :cut]).astype(BF)
        if rows < half:
            out[j, rows:, :] = jnp.zeros((half - rows, out.shape[2]), BF)

        def text(u, is_text):
            part = slice(u * SUB, (u + 1) * SUB)
            out[j, part, :] = jnp.where(
                is_text, dot_back(x[j, part, :], w[:, cut:]).astype(BF), out[j, part, :]
            )

        for_text(info, j, base, rows, text)

    def empty(j, side):
        out = (own, oth)[side]
        out[j] = jnp.zeros(out.shape[1:], BF)

    for_tiles(info, half, body, empty)


def gelu_parts(v):
    k = 0.7978845608028654
    square = v * v
    t = jnp.tanh(k * v * (1.0 + 0.044715 * square))
    value = 0.5 * v * (1.0 + t)
    slope = 0.5 * (1.0 + t) + 0.5 * v * (1.0 - t * t) * k * (1.0 + 3 * 0.044715 * square)
    return value, slope


def mlp_core(
    info, x_own, x_oth, g_own, g_oth, upper, lower,
    gm_own, gm_oth, hid_own, hid_oth, gb_own, gb_oth,
    before, back,
):
    half = x_own.shape[1]
    cut = upper.shape[1] // 2

    def body(j, side, base, rows):
        x, g = (x_own, x_oth)[side], (g_own, g_oth)[side]
        gm, hid, gb = (gm_own, gm_oth)[side], (hid_own, hid_oth)[side], (gb_own, gb_oth)[side]
        before[:rows, :] = dot(x[j, :rows, :], upper[:, :cut])
        back[:rows, :] = dot(g[j, :rows, :], lower[:, :cut])

        def text(u, is_text):
            part = slice(u * SUB, (u + 1) * SUB)
            before[part, :] = jnp.where(is_text, dot(x[j, part, :], upper[:, cut:]), before[part, :])
            back[part, :] = jnp.where(is_text, dot(g[j, part, :], lower[:, cut:]), back[part, :])

        for_text(info, j, base, rows, text)
        value, slope = gelu_parts(before[:rows, :])
        hid[j, :rows, :] = value.astype(BF)
        gb[j, :rows, :] = (back[:rows, :].astype(BF).astype(F32) * slope).astype(BF)
        gm[j, :rows, :] = dot_back(gb[j, :rows, :], upper[:, :cut]).astype(BF)

        def text_back(u, is_text):
            part = slice(u * SUB, (u + 1) * SUB)
            gm[j, part, :] = jnp.where(
                is_text, dot_back(gb[j, part, :], upper[:, cut:]).astype(BF), gm[j, part, :]
            )

        for_text(info, j, base, rows, text_back)
        if rows < half:
            for ref in (gm, hid, gb):
                ref[j, rows:, :] = jnp.zeros((half - rows, ref.shape[2]), BF)

    def empty(j, side):
        for ref in ((gm_own, gm_oth)[side], (hid_own, hid_oth)[side], (gb_own, gb_oth)[side]):
            ref[j] = jnp.zeros(ref.shape[1:], BF)

    for_tiles(info, half, body, empty)


def weight_sums(info, half, left_of, right_of, acc_image, acc_text):
    acc_image[...] = jnp.zeros_like(acc_image)
    acc_text[...] = jnp.zeros_like(acc_text)

    def body(j, side, base, rows):
        left, right = left_of(j, side, base, rows), right_of(j, side, base, rows)
        ids = row_ids(base, rows)
        is_text = (ids >= info[TEXT_FROM + j]) & (ids < info[TEXT_TO + j])
        is_image = (ids < info[COUNT + j]) & jnp.logical_not(is_text)
        acc_image[...] += dot_rows(left, jnp.where(is_image, right, 0).astype(BF))

        def text(u, hit):
            part = slice(u * SUB, (u + 1) * SUB)
            acc_text[...] += dot_rows(left[part], jnp.where(hit, right[part], 0).astype(BF))

        for_text(info, j, base, rows, text)

    for_tiles(info, half, body)


def sums_of_slots(info, l_own, l_oth, r_own, r_oth, out, acc_image, acc_text):
    cut = acc_image.shape[1]
    weight_sums(
        info,
        l_own.shape[1],
        lambda j, side, base, rows: (l_own, l_oth)[side][j, :rows, :],
        lambda j, side, base, rows: (r_own, r_oth)[side][j, :rows, :].astype(F32),
        acc_image,
        acc_text,
    )
    out[:, :cut] = acc_image[...].astype(BF)
    out[:, cut:] = acc_text[...].astype(BF)


def sums_of_rows(info, l_own, l_oth, right, image, text, acc_image, acc_text):
    weight_sums(
        info,
        l_own.shape[1],
        lambda j, side, base, rows: (l_own, l_oth)[side][j, :rows, :],
        lambda j, side, base, rows: read_rows(right, info[OFFSET + j] + base, rows).astype(F32),
        acc_image,
        acc_text,
    )
    image[...] = acc_image[...].astype(BF)
    text[...] = acc_text[...].astype(BF)


def head_rows(turned, h):
    ids = lax.broadcasted_iota(jnp.int32, turned.shape, 0)
    return jnp.where((ids >= h * HEAD) & (ids < (h + 1) * HEAD), turned, 0)


def head_columns(plain, h):
    ids = lax.broadcasted_iota(jnp.int32, plain.shape, 1)
    return jnp.where((ids >= h * HEAD) & (ids < (h + 1) * HEAD), plain, 0)


def chunk_mask(chunks, i, n_chunks, q_from, q_to):
    position = chunks[i] + lax.broadcasted_iota(jnp.int32, (CHUNK, 1), 0)
    valid = (position >= chunks[n_chunks + i]) & (position < chunks[2 * n_chunks + i])
    position = jnp.where(valid, position, -1)
    return (position >= q_from) & (position < q_to)


def for_chunks(chunks, n_chunks, t, body):
    low, high = chunks[3 * n_chunks + 2 * t], chunks[3 * n_chunks + 2 * t + 1]

    def step(i, carry):
        start = jnp.maximum(chunks[i], chunks[n_chunks + i])
        stop = jnp.minimum(chunks[i] + CHUNK, chunks[2 * n_chunks + i])

        @pl.when((start < high) & (stop > low) & (start < stop))
        def _():
            body(i)

        return carry

    lax.fori_loop(0, n_chunks, step, 0)


def attend_kernel(chunks, q, k, v, q_from, q_to, out, exact, lse, top, v_turned, logits, total, high):
    t = pl.program_id(0)
    n_chunks = k.shape[0] // CHUNK
    heads = q.shape[1] // HEAD

    @pl.when(t == 0)
    def _():
        for i in range(n_chunks):
            part = slice(i * CHUNK, (i + 1) * CHUNK)
            v_turned[:, part] = v[part, :].T
        top[...] = jnp.full_like(top, NEGATIVE)

    live = chunks[3 * n_chunks + 2 * t + 1] > 0

    @pl.when(live)
    def _():
        turned = (q[...].astype(F32) * HEAD**-0.5).T
        per_head = [head_rows(turned, h).astype(BF) for h in range(heads)]
        lanes_from, lanes_to = q_from[0], q_to[0]
        total[...] = jnp.zeros_like(total)
        high[...] = jnp.full_like(high, NEGATIVE)

        def first(i):
            keys = k[pl.ds(pl.multiple_of(i * CHUNK, CHUNK), CHUNK), :]
            mask = chunk_mask(chunks, i, n_chunks, lanes_from, lanes_to)
            for h in range(heads):
                part = jnp.where(mask, dot(keys, per_head[h]), NEGATIVE)
                logits[h, i] = part
                high[h : h + 1, :] = jnp.maximum(high[h : h + 1, :], jnp.max(part, axis=0, keepdims=True))

        for_chunks(chunks, n_chunks, t, first)
        tops = [high[h : h + 1, :] for h in range(heads)]

        def second(i):
            for h in range(heads):
                part = jnp.exp(logits[h, i] - tops[h])
                high[8 + h : 9 + h, :] += jnp.sum(part, axis=0, keepdims=True)
                rows = slice(h * HEAD, (h + 1) * HEAD)
                values = v_turned[rows, pl.ds(pl.multiple_of(i * CHUNK, CHUNK), CHUNK)]
                total[rows, :] += dot(values, part.astype(BF))

        high[8:, :] = jnp.zeros((8, high.shape[1]), F32)
        for_chunks(chunks, n_chunks, t, second)
        for h in range(heads):
            rows = slice(h * HEAD, (h + 1) * HEAD)
            sums = high[8 + h : 9 + h, :]
            total[rows, :] = total[rows, :] / sums
            lse[0, h : h + 1, :] = tops[h] + jnp.log(sums)
            seen = jnp.where(lanes_to > lanes_from, tops[h], NEGATIVE)
            top[h : h + 1, :] = jnp.maximum(top[h : h + 1, :], seen)
        result = total[...].T
        exact[...] = result
        out[...] = result.astype(BF)

    @pl.when(jnp.logical_not(live))
    def _():
        exact[...] = jnp.zeros_like(exact)
        out[...] = jnp.zeros_like(out)
        lse[...] = jnp.zeros_like(lse)


def attend_back_kernel(
    chunks, q, g, attended, k, v, lse, q_from, q_to, dq, dk, dv, k_turned, q_stack, g_stack, total
):
    t = pl.program_id(0)
    n_chunks = k.shape[0] // CHUNK
    heads = q.shape[1] // HEAD
    wide = q.shape[0]

    @pl.when(t == 0)
    def _():
        for i in range(n_chunks):
            part = slice(i * CHUNK, (i + 1) * CHUNK)
            k_turned[:, part] = k[part, :].T
        dk[...] = jnp.zeros_like(dk)
        dv[...] = jnp.zeros_like(dv)

    live = chunks[3 * n_chunks + 2 * t + 1] > 0

    @pl.when(live)
    def _():
        scaled = q[...].astype(F32) * HEAD**-0.5
        grads = g[...].astype(F32)
        q_turned, g_turned = scaled.T, grads.T
        product = g_turned * attended[...].T
        q_heads, g_heads, delta, logs = [], [], [], []
        for h in range(heads):
            rows = slice(h * wide, (h + 1) * wide)
            q_stack[rows, :] = head_columns(scaled, h).astype(BF)
            g_stack[rows, :] = head_columns(grads, h).astype(BF)
            q_heads.append(head_rows(q_turned, h).astype(BF))
            g_heads.append(head_rows(g_turned, h).astype(BF))
            delta.append(jnp.sum(product[h * HEAD : (h + 1) * HEAD, :], axis=0, keepdims=True))
            logs.append(lse[0, h : h + 1, :])
        lanes_from, lanes_to = q_from[0], q_to[0]
        total[...] = jnp.zeros_like(total)

        def body(i):
            place = pl.ds(pl.multiple_of(i * CHUNK, CHUNK), CHUNK)
            keys, values = k[place, :], v[place, :]
            mask = chunk_mask(chunks, i, n_chunks, lanes_from, lanes_to)
            probs, grad_logits = [], []
            for h in range(heads):
                part = jnp.where(mask, jnp.exp(dot(keys, q_heads[h]) - logs[h]), 0.0)
                back = (part * (dot(values, g_heads[h]) - delta[h])).astype(BF)
                probs.append(part.astype(BF))
                grad_logits.append(back)
                rows = slice(h * HEAD, (h + 1) * HEAD)
                total[rows, :] += dot(k_turned[rows, place], back)
            dv[place, :] += dot(jnp.concatenate(probs, axis=1), g_stack[...])
            dk[place, :] += dot(jnp.concatenate(grad_logits, axis=1), q_stack[...])

        for_chunks(chunks, n_chunks, t, body)
        dq[...] = total[...].T * HEAD**-0.5

    @pl.when(jnp.logical_not(live))
    def _():
        dq[...] = jnp.zeros_like(dq)


def gather_grads_kernel(info, dq, dk, dv, near_back, near_on, far_back, far_on, out, keys, values):
    width = dq.shape[1]
    keys[...] = dk[...]
    values[...] = dv[...]

    def add(place, part):
        keys[place, :] += part[:, :width]
        values[place, :] += part[:, width:]

    for start, part in ((info[TAIL_FROM], near_back), (info[EDGE_FROM], far_back)):
        place, skip = window(start, part.shape[0], keys.shape[0])
        add(place, moved(part[...], skip))
    add(pl.ds(0, TAIL), near_on[...].astype(F32))
    add(pl.ds(0, EDGE), far_on[...].astype(F32))
    out[...] = jnp.concatenate([dq[...], keys[...], values[...]], axis=1).astype(BF)


def shift(value, steps):
    count = lax.axis_size("g")
    pairs = [(i, i + steps) for i in range(count) if 0 <= i + steps < count]
    if not pairs:
        return jnp.zeros_like(value)
    return lax.ppermute(value, "g", pairs)


def over_x(value):
    return lax.ppermute(value, "x", SWAP)


def over_y(value):
    return lax.ppermute(value, "y", SWAP)


def over_core(value):
    return lax.ppermute(value, "c", SWAP)


def over_xy(value):
    return lax.ppermute(value, ("y", "x"), [(0, 3), (1, 2), (2, 1), (3, 0)])


def spread(value):
    cut = value.shape[0] // 2
    from_x, from_y = over_x(value), over_y(value)
    far = jnp.concatenate([over_y(from_x[:cut]), over_x(from_y[cut:])], axis=0)
    own = jnp.stack([value, from_x, from_y, far])
    return own, over_core(own)


def add16(*parts):
    total = parts[0].astype(F32)
    for part in parts[1:]:
        total = total + part.astype(F32)
    return total


def collect(own, oth):
    cut = own.shape[1] // 2
    part = add16(own, over_core(oth)).astype(BF)
    to_x, to_y, far = part[1], part[2], part[3]
    from_x, from_y = over_x(far[:cut]), over_y(far[cut:])
    first_x = over_x(to_x[:cut])
    first_y = over_y(to_y[cut:])
    last_x = over_x(add16(to_x[cut:], from_y).astype(BF))
    last_y = over_y(add16(to_y[:cut], from_x).astype(BF))
    low = add16(part[0, :cut], first_x, last_y)
    high = add16(part[0, cut:], last_x, first_y)
    return jnp.concatenate([low, high], axis=0)


def layer_norm(inputs):
    centered = inputs - jnp.mean(inputs, axis=1, keepdims=True)
    inverse_std = lax.rsqrt(jnp.mean(centered * centered, axis=1, keepdims=True) + EPSILON)
    return (centered * inverse_std, inverse_std)


def norm_back(grad_normed, normed, inverse_std):
    return inverse_std * (
        grad_normed
        - jnp.mean(grad_normed, axis=1, keepdims=True)
        - normed * jnp.mean(grad_normed * normed, axis=1, keepdims=True)
    )


def exchange_pieces(pieces, q):
    pick = lambda j: lax.dynamic_index_in_dim(pieces, q ^ j, 0, keepdims=False)
    got = jnp.stack([pick(0), over_x(pick(1)), over_y(pick(2)), over_xy(pick(3))])
    return jnp.stack([lax.dynamic_index_in_dim(got, q ^ b, 0, keepdims=False) for b in range(BLOCKS)])


def local(
    tokens,
    cotangent,
    seq_offsets,
    block_offsets,
    image_mod,
    text_mod,
    image_qkv,
    text_qkv,
    image_out,
    text_out,
    image_fc1,
    text_fc1,
    image_fc2,
    text_fc2,
    clip_limits,
):
    rows_cap, width = tokens.shape
    half = rows_cap // 2
    share = image_qkv.shape[0]
    columns = image_qkv.shape[2]
    group_rows = BLOCKS * rows_cap
    mine = columns // BLOCKS
    heads = mine // HEAD
    seq_count = seq_offsets.shape[0] - 1
    n_groups = lax.axis_size("g")
    g, c = lax.axis_index("g"), lax.axis_index("c")
    q = 2 * lax.axis_index("y") + lax.axis_index("x")
    device = g * BLOCKS + q

    def quarter(inputs):
        return jnp.moveaxis(inputs.reshape(share, -1, BLOCKS, mine), 2, 0).reshape(BLOCKS, share, -1)

    def quarter_turned(inputs):
        return jnp.swapaxes(inputs.reshape(BLOCKS, -1, share), 1, 2)

    def quarter_wide(inputs):
        return jnp.swapaxes(inputs.reshape(share, BLOCKS, -1), 0, 1)

    pack_qkv = jnp.concatenate([quarter(image_qkv), quarter(text_qkv)], axis=2)
    pack_rest = jnp.concatenate(
        [
            quarter_wide(image_fc1),
            quarter_wide(text_fc1),
            quarter_turned(image_fc2),
            quarter_turned(text_fc2),
            quarter_turned(image_out),
            quarter_turned(text_out),
        ],
        axis=2,
    )
    fc = image_fc1.shape[1] // BLOCKS
    plane_qkv = exchange_pieces(pack_qkv, q).reshape(BLOCKS * share, -1)
    plane_rest = exchange_pieces(pack_rest, q).reshape(BLOCKS * share, -1)
    whole_qkv = lax.all_gather(plane_qkv, "g", axis=0, tiled=True)
    whole_out = lax.all_gather(plane_rest[:, 4 * fc :], "g", axis=0, tiled=True)
    whole_fc1 = lax.all_gather(plane_rest[:, : 2 * fc], "g", axis=0, tiled=True)
    whole_fc2 = lax.all_gather(plane_rest[:, 2 * fc : 4 * fc], "g", axis=0, tiled=True)
    qkv_image, qkv_text = whole_qkv[:, : 3 * mine], whole_qkv[:, 3 * mine :]
    out_image, out_text = whole_out[:, :mine], whole_out[:, mine:]

    group_from = block_offsets[:: BLOCKS]
    own_from, own_to = block_offsets[device], block_offsets[device + 1]
    start, stop = group_from[g], group_from[g + 1]
    live_rows = stop - start
    members = g * BLOCKS + (q ^ jnp.arange(BLOCKS, dtype=jnp.int32))
    member_from, member_to = block_offsets[members], block_offsets[members + 1]
    text_low = jnp.maximum(seq_offsets[None, :-1] + IMG, member_from[:, None])
    text_high = jnp.minimum(seq_offsets[None, 1:], member_to[:, None])
    has_text = text_low < text_high
    text_from = jnp.sum(jnp.where(has_text, text_low - member_from[:, None], 0), axis=1)
    text_to = jnp.sum(jnp.where(has_text, text_high - member_from[:, None], 0), axis=1)
    tail_from = jnp.maximum(live_rows - TAIL, 0)
    edge_from = jnp.maximum(live_rows - EDGE, 0)
    info = jnp.concatenate(
        [
            member_to - member_from,
            member_from - start,
            text_from,
            text_to,
            jnp.stack([c, tail_from, edge_from]),
        ]
    ).astype(jnp.int32)

    def group_span(steps):
        there = (g + steps >= 0) & (g + steps < n_groups)
        at = jnp.clip(g + steps, 0, n_groups - 1)
        return jnp.where(there, group_from[at], 0), jnp.where(there, group_from[at + 1], 0)

    def region(base, low, high, rows):
        n = rows // CHUNK
        steps = jnp.arange(n, dtype=jnp.int32) * CHUNK
        return base + steps, jnp.full((n,), 0, jnp.int32) + low, jnp.full((n,), 0, jnp.int32) + high

    spans = {steps: group_span(steps) for steps in (-2, -1, 1, 2)}
    regions = [
        region(jnp.maximum(spans[-2][1] - EDGE, spans[-2][0]), *spans[-2], CHUNK),
        region(jnp.maximum(spans[-1][1] - TAIL, spans[-1][0]), *spans[-1], TAIL_PAD),
        region(start, start, stop, group_rows),
        region(spans[1][0], spans[1][0], jnp.minimum(spans[1][1], spans[1][0] + TAIL), TAIL_PAD),
        region(spans[2][0], spans[2][0], jnp.minimum(spans[2][1], spans[2][0] + EDGE), CHUNK),
    ]
    n_tiles = group_rows // CHUNK
    position = start + jnp.arange(group_rows, dtype=jnp.int32)
    row_seq = jnp.sum((position[:, None] >= seq_offsets[None, 1:-1]).astype(jnp.int32), axis=1)
    seq_hit = row_seq[:, None] == jnp.arange(seq_count)[None, :]
    row_live = position < stop
    rows_from = jnp.where(row_live, jnp.sum(jnp.where(seq_hit, seq_offsets[None, :-1], 0), axis=1), 0)
    rows_to = jnp.where(row_live, jnp.sum(jnp.where(seq_hit, seq_offsets[None, 1:], 0), axis=1), 0)
    rows_from = rows_from.reshape(n_tiles, 1, CHUNK).astype(jnp.int32)
    rows_to = rows_to.reshape(n_tiles, 1, CHUNK).astype(jnp.int32)
    tile_span = jnp.stack([rows_from[:, 0, 0], jnp.max(rows_to[:, 0, :], axis=1)], axis=1).reshape(-1)
    chunks = jnp.concatenate([part for field in zip(*regions) for part in field] + [tile_span]).astype(jnp.int32)

    my_rows = lambda inputs: lax.dynamic_slice_in_dim(inputs, c * half, half, 0)
    ids = c * half + jnp.arange(half, dtype=jnp.int32)
    is_live = (ids < own_to - own_from)[:, None]
    my_seq = jnp.sum((own_from >= seq_offsets[1:-1]).astype(jnp.int32))
    next_seq = jnp.minimum(my_seq + 1, seq_count - 1)
    is_text = (is_live[:, 0] & (ids >= text_from[0]) & (ids < text_to[0]))[:, None]
    is_next = is_live & (own_from + ids >= seq_offsets[my_seq + 1])[:, None]
    vectors = (image_mod[my_seq], text_mod[my_seq], image_mod[next_seq])

    def modulation(which):
        return jnp.where(
            is_text, vectors[1][which][None], jnp.where(is_next, vectors[2][which][None], vectors[0][which][None])
        )

    shift_rows, scale_rows, gate_rows, shift_mlp, scale_mlp, gate_mlp = (modulation(i) for i in range(6))
    stream = my_rows(tokens).astype(F32)
    grad_stream = jnp.where(is_live, my_rows(cotangent).astype(F32), 0.0)
    normed, inverse_std = layer_norm(stream)
    modulated = (normed * (1.0 + scale_rows) + shift_rows).astype(BF)
    grad_mlp = (gate_mlp * grad_stream).astype(BF)

    slot = lambda n: jax.ShapeDtypeStruct((BLOCKS, half, n), BF)
    rows_of = lambda n, kind: jax.ShapeDtypeStruct((group_rows, n), kind)
    work = lambda n, k: 2 * (group_rows * 3 // 4) * n * k
    mod_own, mod_oth = spread(modulated)
    qkv = call(
        slots_to_rows,
        rows_of(3 * mine, BF),
        5,
        [pltpu.VMEM((half, 3 * mine), F32)],
        work(width, 3 * mine),
        12_000_000,
    )(info, mod_own, mod_oth, qkv_image, qkv_text)

    queries = qkv[:, :mine]
    pairs = qkv[:, mine:]
    tail = lax.dynamic_slice_in_dim(pairs, tail_from, TAIL, 0)
    edge = lax.dynamic_slice_in_dim(pairs, edge_from, EDGE, 0)
    near_back, near_on = shift(tail, 1), shift(pairs[:TAIL], -1)
    far_back, far_on = shift(edge, 2), shift(pairs[:EDGE], -2)
    blank = lambda n: jnp.zeros((n, 2 * mine), BF)
    around = jnp.concatenate(
        [
            far_back,
            blank(CHUNK - EDGE),
            near_back,
            blank(TAIL_PAD - TAIL),
            pairs,
            near_on,
            blank(TAIL_PAD - TAIL),
            far_on,
            blank(CHUNK - EDGE),
        ],
        axis=0,
    )
    keys, values = around[:, :mine], around[:, mine:]
    reach = keys.shape[0]
    n_chunks = reach // CHUNK

    tile_spec = pl.BlockSpec((CHUNK, mine), lambda t: (t, 0))
    all_spec = pl.BlockSpec((reach, mine), lambda t: (0, 0))
    lane_spec = pl.BlockSpec((1, 1, CHUNK), lambda t: (t, 0, 0))
    log_spec = pl.BlockSpec((1, 8, CHUNK), lambda t: (t, 0, 0))
    pair_work = 2 * heads * group_rows * 3 // 4 * 1280 * 256
    attended, attended_exact, logs, tops = pl.pallas_call(
        attend_kernel,
        grid=(n_tiles,),
        out_shape=(
            rows_of(mine, BF),
            rows_of(mine, F32),
            jax.ShapeDtypeStruct((n_tiles, 8, CHUNK), F32),
            jax.ShapeDtypeStruct((8, CHUNK), F32),
        ),
        in_specs=[SMEM, tile_spec, all_spec, all_spec, lane_spec, lane_spec],
        out_specs=(tile_spec, tile_spec, log_spec, pl.BlockSpec((8, CHUNK), lambda t: (0, 0))),
        scratch_shapes=[
            pltpu.VMEM((mine, reach), BF),
            pltpu.VMEM((heads, n_chunks, CHUNK, CHUNK), F32),
            pltpu.VMEM((mine, CHUNK), F32),
            pltpu.VMEM((16, CHUNK), F32),
        ],
        compiler_params=pltpu.CompilerParams(vmem_limit_bytes=VMEM_LIMIT),
        cost_estimate=pl.CostEstimate(flops=2 * pair_work, bytes_accessed=8_000_000, transcendentals=8_000_000),
    )(chunks, queries, keys, values, rows_from, rows_to)

    head_top = jnp.max(tops[:heads], axis=1)
    spot = jnp.arange(BLOCKS)[:, None] == q
    head_max = lax.pmax(jnp.where(spot, head_top[None, :], NEGATIVE).reshape(-1), ("g", "y", "x"))

    sent = call(rows_to_slots, (slot(width), slot(width)), 4, (), work(width, mine), 9_000_000)(
        info, attended, out_image, out_text
    )
    branch = collect(*sent)
    first = stream + gate_rows * branch
    normed_mlp, inverse_mlp = layer_norm(first)
    modulated_mlp = (normed_mlp * (1.0 + scale_mlp) + shift_mlp).astype(BF)

    gmlp_own, gmlp_oth = spread(grad_mlp)
    mm_own, mm_oth = spread(modulated_mlp)
    gm_own, gm_oth, hid_own, hid_oth, gb_own, gb_oth = call(
        mlp_core,
        (slot(width), slot(width), slot(fc), slot(fc), slot(fc), slot(fc)),
        7,
        [pltpu.VMEM((half, fc), F32), pltpu.VMEM((half, fc), F32)],
        work(width, 3 * fc),
        35_000_000,
    )(info, mm_own, mm_oth, gmlp_own, gmlp_oth, whole_fc1, whole_fc2)
    grad_mod_mlp = collect(gm_own, gm_oth)

    def slot_sums(left, right):
        return call(
            sums_of_slots,
            jax.ShapeDtypeStruct((width, 2 * fc), BF),
            5,
            [pltpu.VMEM((width, fc), F32), pltpu.VMEM((width, fc), F32)],
            work(width, fc),
            15_000_000,
        )(info, *left, *right)

    def row_sums(left, right):
        n = right.shape[1]
        return jnp.concatenate(
            call(
                sums_of_rows,
                (jax.ShapeDtypeStruct((width, n), BF), jax.ShapeDtypeStruct((width, n), BF)),
                4,
                [pltpu.VMEM((width, n), F32), pltpu.VMEM((width, n), F32)],
                work(width, n),
                12_000_000,
            )(info, *left, right),
            axis=1,
        )

    fc2_sums = slot_sums((gmlp_own, gmlp_oth), (hid_own, hid_oth))
    fc1_sums = slot_sums((mm_own, mm_oth), (gb_own, gb_oth))
    mlp_sent = call(slots_to_slots, (slot(width), slot(width)), 4, (), work(width, fc), 12_000_000)(
        info, hid_own, hid_oth, whole_fc2
    )
    mlp_branch = collect(*mlp_sent)
    mixed_rows = jnp.where(is_live, first + gate_mlp * mlp_branch, 0.0).astype(BF)

    grad_first = jnp.where(
        is_live,
        grad_stream + norm_back(grad_mod_mlp * (1.0 + scale_mlp), normed_mlp, inverse_mlp),
        0.0,
    )
    grad_branch = (gate_rows * grad_first).astype(BF)
    gbr_own, gbr_oth = spread(grad_branch)
    grad_attended = call(
        slots_to_rows,
        rows_of(mine, BF),
        5,
        [pltpu.VMEM((half, mine), F32)],
        work(width, mine),
        8_000_000,
    )(info, gbr_own, gbr_oth, out_image, out_text)
    out_sums = row_sums((gbr_own, gbr_oth), attended)

    dq, dk, dv = pl.pallas_call(
        attend_back_kernel,
        grid=(n_tiles,),
        out_shape=(
            rows_of(mine, F32),
            jax.ShapeDtypeStruct((reach, mine), F32),
            jax.ShapeDtypeStruct((reach, mine), F32),
        ),
        in_specs=[SMEM, tile_spec, tile_spec, tile_spec, all_spec, all_spec, log_spec, lane_spec, lane_spec],
        out_specs=(tile_spec, all_spec, all_spec),
        scratch_shapes=[
            pltpu.VMEM((mine, reach), BF),
            pltpu.VMEM((heads * CHUNK, mine), BF),
            pltpu.VMEM((heads * CHUNK, mine), BF),
            pltpu.VMEM((mine, CHUNK), F32),
        ],
        compiler_params=pltpu.CompilerParams(vmem_limit_bytes=VMEM_LIMIT),
        cost_estimate=pl.CostEstimate(flops=5 * pair_work, bytes_accessed=20_000_000, transcendentals=8_000_000),
    )(chunks, queries, grad_attended, attended_exact, keys, values, logs, rows_from, rows_to)

    both = lambda a, n: jnp.concatenate([dk[a : a + n], dv[a : a + n]], axis=1).astype(BF)
    at_own = CHUNK + TAIL_PAD
    at_next = at_own + group_rows
    back_near = shift(both(CHUNK, TAIL), -1)
    on_near = shift(both(at_next, TAIL), 1)
    back_far = shift(both(0, EDGE), -2)
    on_far = shift(both(at_next + TAIL_PAD, EDGE), 2)
    grad_qkv = call(
        gather_grads_kernel,
        rows_of(3 * mine, BF),
        8,
        [pltpu.VMEM((group_rows, mine), F32), pltpu.VMEM((group_rows, mine), F32)],
        0,
        20_000_000,
    )(
        info,
        dq,
        dk[at_own:at_next],
        dv[at_own:at_next],
        back_near,
        on_near,
        back_far,
        on_far,
    )
    mod_sent = call(
        rows_to_slots, (slot(width), slot(width)), 4, (), work(width, 3 * mine), 12_000_000
    )(info, grad_qkv, qkv_image, qkv_text)
    grad_modulated = collect(*mod_sent)
    qkv_sums = row_sums((mod_own, mod_oth), grad_qkv)

    tokens_grad_rows = jnp.where(
        is_live,
        grad_first + norm_back(grad_modulated * (1.0 + scale_rows), normed, inverse_std),
        0.0,
    )

    def scattered(sums):
        part = lax.psum_scatter(sums, "g", scatter_dimension=0, tiled=True)
        return exchange_pieces(part.reshape(BLOCKS, share, -1), q)

    fc2_back, fc1_back = scattered(fc2_sums), scattered(fc1_sums)
    out_back, qkv_back = scattered(out_sums), scattered(qkv_sums)

    def qkv_out(part):
        return jnp.transpose(part.reshape(BLOCKS, share, 3, mine), (1, 2, 0, 3)).reshape(share, 3, columns).astype(F32)

    def turned_out(part):
        return jnp.swapaxes(part, 1, 2).reshape(-1, share).astype(F32)

    def wide_out(part):
        return jnp.swapaxes(part, 0, 1).reshape(share, -1).astype(F32)

    picks = jnp.concatenate(
        [is_live & ~is_text & ~is_next, is_text, is_next & ~is_text, jnp.zeros((half, 5), bool)], axis=1
    ).astype(F32)
    terms = (
        grad_modulated,
        grad_modulated * normed,
        grad_first * branch,
        grad_mod_mlp,
        grad_mod_mlp * normed_mlp,
        grad_stream * mlp_branch,
    )
    sums = jnp.stack(
        [
            lax.dot_general(
                picks,
                jnp.where(is_live, term, 0.0),
                (((0,), (0,)), ((), ())),
                precision=lax.Precision.HIGHEST,
                preferred_element_type=F32,
            )
            for term in terms
        ],
        axis=1,
    )
    seq_ids = jnp.arange(seq_count)[:, None, None]
    image_part = jnp.where(seq_ids == my_seq, sums[0][None], 0.0) + jnp.where(
        (seq_ids == next_seq) & (next_seq > my_seq), sums[2][None], 0.0
    )
    text_part = jnp.where(seq_ids == my_seq, sums[1][None], 0.0)
    mod_part = jnp.concatenate([image_part, text_part], axis=0).reshape(2 * seq_count * 6, -1, share)
    mod_part = jnp.swapaxes(mod_part, 0, 1)
    mod_part = mod_part + over_core(mod_part)
    mod_sum = lax.psum_scatter(mod_part, ("g", "y", "x"), scatter_dimension=0, tiled=True)
    mod_sum = mod_sum.reshape(2, seq_count, 6, share)

    def both_halves(rows):
        other = over_core(rows)
        return jnp.where(c == 0, jnp.concatenate([rows, other], axis=0), jnp.concatenate([other, rows], axis=0))

    root_factor = jnp.sqrt(clip_limits / jnp.maximum(head_max, clip_limits))
    column_scale = jnp.repeat(root_factor, HEAD)[None, None, :]
    image_clipped = (image_qkv[:, :2, :].astype(F32) * column_scale).astype(BF)
    text_clipped = (text_qkv[:, :2, :].astype(F32) * column_scale).astype(BF)
    return (
        both_halves(mixed_rows),
        both_halves(tokens_grad_rows),
        mod_sum[0],
        mod_sum[1],
        qkv_out(qkv_back[:, :, : 3 * mine]),
        qkv_out(qkv_back[:, :, 3 * mine :]),
        turned_out(out_back[:, :, :mine]),
        turned_out(out_back[:, :, mine:]),
        wide_out(fc1_back[:, :, :fc]),
        wide_out(fc1_back[:, :, fc:]),
        turned_out(fc2_back[:, :, :fc]),
        turned_out(fc2_back[:, :, fc:]),
        head_max,
        image_clipped,
        text_clipped,
    )


def solution(mesh):
    devices = mesh.devices
    split = Mesh(devices.reshape(devices.shape[0] // BLOCKS, 2, 2, devices.shape[1]), ("g", "y", "x", "c"))
    dp = ("g", "y", "x")
    placed = (
        P(dp, None),
        P(dp, None),
        P(),
        P(),
        P(),
        P(),
        P(dp, None, "c"),
        P(dp, None, "c"),
        P("c", dp),
        P("c", dp),
        P(dp, "c"),
        P(dp, "c"),
        P("c", dp),
        P("c", dp),
        P("c"),
    )
    return jax.shard_map(
        local,
        mesh=split,
        in_specs=placed,
        out_specs=(
            P(dp, None),
            P(dp, None),
            P(None, None, dp),
            P(None, None, dp),
            P(dp, None, "c"),
            P(dp, None, "c"),
            P("c", dp),
            P("c", dp),
            P(dp, "c"),
            P(dp, "c"),
            P("c", dp),
            P("c", dp),
            P("c"),
            P(dp, None, "c"),
            P(dp, None, "c"),
        ),
        check_vma=False,
    )
```

time: 3990 us -> 1030 us (0.26)
  waiting for transfers between devices: 2710 us -> 408 us
  matrix products: 650 us -> 6.45 us
  Pallas kernels: 0 us -> 249 us
  starting transfers between devices: 210 us -> 105 us
  local copies, waits for them, and re-layouts: 185 us -> 93.4 us
  other arithmetic: 139 us -> 91.3 us
    reduce_scatter x8 -> x4, waiting for transfers between devices: 1900 us -> 65.1 us  [scattered(): part = lax.psum_scatter(sums, 'g', scatter_dimension=0, tiled=True)]
    dot_general x104 -> x6, matrix products: 650 us -> 6.45 us  [local(): lax.dot_general(picks, jnp.where(is_live, term, 0.0), (((0,), (0,)), ((),...]
    all_gather x8 -> x4, waiting for transfers between devices: 564 us -> 27.8 us  [the longest x1 27.8 us: local(): whole_fc1 = lax.all_gather(plane_rest[:, :2 * fc], 'g', axis=0, tiled=True)]
    pallas_call x0 -> x13, Pallas kernels: none -> 249 us  [the longest x1 57.1 us: local(): pl.pallas_call(attend_back_kernel, grid=(n_tiles,), out_shape=(rows_of(mi...]
    ppermute x40 -> x77, waiting for transfers between devices: 97.1 us -> 293 us  [the longest x26 107 us: over_x(): return lax.ppermute(value, 'x', SWAP)]
    ppermute x40 -> x77, starting transfers between devices: 209 us -> 104 us  [the longest x26 33.8 us: over_x(): return lax.ppermute(value, 'x', SWAP)]
    unnamed x23 -> x10, waiting for transfers between devices: 111 us -> 21.5 us
    reduce_max x11 -> x2, other arithmetic: 71.4 us -> 1.49 us  [the longest x1 1.38 us: local(): jnp.max(rows_to[:, 0, :], axis=1)]
  transfers between devices with their start and end apart: 61 -> 86, of which waited for: 26 -> 44; matrix products, arithmetic and copies ran while one was open for 17% -> 16% of each run, Pallas kernels for 0% -> 20%
where the time goes in v1:
time: 1030 us; the launch traced here: 1020 us
  waiting for transfers between devices  408 us (40%)
  Pallas kernels  249 us (24%)
  starting transfers between devices  105 us (10%)
  local copies, waits for them, and re-layouts  93.4 us (9%)
  other arithmetic  91.3 us (9%)
  blocking collectives  42.2 us (4%)
  between operations  28.2 us (3%)
    ppermute x26, waiting for transfers between devices, over_x(): return lax.ppermute(value, 'x', SWAP)  107 us
    ppermute x8, waiting for transfers between devices, shift(): return lax.ppermute(value, 'g', pairs)  94.1 us
    ppermute x26, waiting for transfers between devices, over_y(): return lax.ppermute(value, 'y', SWAP)  69.8 us
    reduce_scatter x4, waiting for transfers between devices, scattered(): part = lax.psum_scatter(sums, 'g', scatter_dimension=0, tiled=True)  65.1 us
    pallas_call x1, Pallas kernels, local(): pl.pallas_call(attend_back_kernel, grid=(n_tiles,), out_shape=(rows_of(mi...  57.1 us
    pmax x1, blocking collectives, local(): lax.pmax(jnp.where(spot, head_top[None, :], NEGATIVE).reshape(-1), ('g',...  42.2 us
    ppermute x26, starting transfers between devices, over_x(): return lax.ppermute(value, 'x', SWAP)  33.8 us
    pallas_call x1, Pallas kernels, local(): call(mlp_core, (slot(width), slot(width), slot(fc), slot(fc), slot(fc), s...  33.2 us
  transfers between devices with their start and end apart: 86, of which 44 were waited for; matrix products, arithmetic and copies ran while one was open for 16% of the time, Pallas kernels for 20%

profile of v1, /device:TPU:0, one launch (start us, length us, event | category | flops | bytes accessed | tf_op | source)
XLA Modules:
  0.0 1023.3 jit_solution(243291298620458211)
XLA Ops:
  87.3 11.0 %collective-permute-done.14 = bf16[96,3456]{1,0:T(8,128)(2,1)} collective-permute-done((bf16[96,3456]{1,0:T(8,128)(2,1)}, bf16[96,3456]{1,0:T(8,128)(2,1)}, u32[]{:S(2)}, u32[]{:S(2)}) %collective-permute-start.14) | collective-permute-done | bytes 663584 | tf_op jit(solution)/shard_map/ppermute | solution.py:477
  116.0 14.1 %shard_map.262 = bf16[2048,576]{1,0:T(8,128)(2,1)} custom-call(s32[19]{0:T(128)} %concatenate.79.info, bf16[4,256,1536]{2,1,0:T(8,128)(2,1)} %copy-done.6, bf16[4,256,1536]{2,1,0:T(8,128)(2,1)} %collective-permute-done.4.oth.l_oth, bf16[1536,576]{1,0:T(8,128)(2,1)} %get-tuple-element.96.w_image, bf16[1536,576]{1,0:T(8,128)(2,1)} %get-tuple-element.95.w_text), custom_call_target="tpu_custom_call" | custom-call | flops 2717908992 | bytes 12000000 | tf_op jit(solution)/shard_map/pallas_call | solution.py:668
  153.1 15.4 %collective-permute-done.8 = bf16[160,384]{1,0:T(8,128)(2,1)} collective-permute-done((bf16[160,384]{1,0:T(8,128)(2,1)}, bf16[160,384]{1,0:T(8,128)(2,1)}, u32[]{:S(2)}, u32[]{:S(2)}) %collective-permute-start.8) | collective-permute-done | bytes 122912 | tf_op jit(solution)/shard_map/ppermute | solution.py:461
  170.4 41.1 %collective-permute-done.10 = bf16[1184,384]{1,0:T(8,128)(2,1)S(1)} collective-permute-done((bf16[1184,384]{1,0:T(8,128)(2,1)S(1)}, bf16[1184,384]{1,0:T(8,128)(2,1)S(1)}, u32[]{:S(2)}, u32[]{:S(2)}) %collective-permute-start.10) | collective-permute-done | bytes 909344 | tf_op jit(solution)/shard_map/ppermute | solution.py:461
  211.8 14.0 %collective-permute-done.11 = bf16[160,384]{1,0:T(8,128)(2,1)S(1)} collective-permute-done((bf16[160,384]{1,0:T(8,128)(2,1)S(1)}, bf16[160,384]{1,0:T(8,128)(2,1)S(1)}, u32[]{:S(2)}, u32[]{:S(2)}) %collective-permute-start.11) | collective-permute-done | bytes 122912 | tf_op jit(solution)/shard_map/ppermute | solution.py:461
  229.5 31.8 %shard_map.263 = (bf16[2048,192]{1,0:T(8,128)(2,1)}, f32[2048,192]{1,0:T(8,128)}, f32[8,8,256]{2,1,0:T(8,128)}, f32[8,256]{1,0:T(8,128)}) custom-call(s32[76]{0:T(128)} %concatenate.80.chunks, bf16[2048,192]{1,0:T(8,128)(2,1)} %slice.566.q, bf16[5120,192]{1,0:T(8,128)(2,1)} %get-tuple-element.94.k, bf16[5120,192]{1,0:T(8,128)(2,1)} %get-tuple-element.93.v, ...), custom_call_target="tpu_custom_call" | custom-call | flops 6039797760 | bytes 8000000 | tf_op jit(solution)/shard_map/pallas_call | solution.py:707
  307.3 10.0 collective-permute-done.27
  340.1 10.2 collective-permute-done.22
  366.3 27.8 %all-gather.9.cloned.1.call-done.upper = bf16[1536,1536]{1,0:T(8,128)(2,1)} async-done(((bf16[384,1536]{1,0:T(8,128)(2,1)}), bf16[1536,1536]{1,0:T(8,128)(2,1)}) %all-gather.9.cloned.1.call-update) | async-done | bytes 4718608 | tf_op jit(solution)/shard_map/all_gather | solution.py:585
  394.1 33.2 %shard_map.265 = (bf16[4,256,1536]{2,1,0:T(8,128)(2,1)}, bf16[4,256,1536]{2,1,0:T(8,128)(2,1)}, bf16[4,256,768]{2,1,0:T(8,128)(2,1)}, bf16[4,256,768]{2,1,0:T(8,...) custom-call(s32[19]{0:T(128)} %concatenate.79.info, ...), custom_call_target="tpu_custom_call" | custom-call | flops 10871635968 | bytes 35000000 | tf_op jit(solution)/shard_map/pallas_call | solution.py:742
  427.4 14.6 %shard_map.266 = (bf16[4,256,1536]{2,1,0:T(8,128)(2,1)}, bf16[4,256,1536]{2,1,0:T(8,128)(2,1)}) custom-call(s32[19]{0:T(128)} %concatenate.79.info, bf16[4,256,768]{2,1,0:T(8,128)(2,1)} %get-tuple-element.41.x_own.r_own, bf16[4,256,768]{2,1,0:T(8,128)(2,1)} %get-tuple-element.42.x_oth.r_oth, bf16[1536,1536]{1,0:T(8,128)(2,1)} %all-gather.11.cloned.1.call-done.lower.w), custom_call_target="tpu_custom_call" | custom-call | flops 3623878656 | bytes 12000000 | tf_op jit(solution)/shard_map/pallas_call | solution.py:778
  442.5 15.1 %shard_map.274 = bf16[1536,1536]{1,0:T(8,128)(2,1)} custom-call(s32[19]{0:T(128)} %concatenate.79.info, bf16[4,256,1536]{2,1,0:T(8,128)(2,1)} %copy-done.7, bf16[4,256,1536]{2,1,0:T(8,128)(2,1)} %collective-permute-done.31.g_oth.l_oth, bf16[4,256,768]{2,1,0:T(8,128)(2,1)} %get-tuple-element.41.x_own.r_own, bf16[4,256,768]{2,1,0:T(8,128)(2,1)} %get-tuple-element.42.x_oth.r_oth), custom_call_target="tpu_custom_call" | custom-call | flops 3623878656 | bytes 15000000 | tf_op jit(solution)/shard_map/pallas_call | solution.py:753
  475.1 15.3 %collective-permute-done.42 = bf16[128,1536]{1,0:T(8,128)(2,1)S(1)} collective-permute-done((bf16[128,1536]{1,0:T(8,128)(2,1)S(1)}, bf16[128,1536]{1,0:T(8,128)(2,1)S(1)}, u32[]{:S(2)}, u32[]{:S(2)}) %collective-permute-start.42) | collective-permute-done | bytes 393248 | tf_op jit(solution)/shard_map/ppermute | solution.py:465
  510.9 14.1 %collective-permute-done.43 = bf16[128,1536]{1,0:T(8,128)(2,1)S(1)} collective-permute-done((bf16[128,1536]{1,0:T(8,128)(2,1)S(1)}, bf16[128,1536]{1,0:T(8,128)(2,1)S(1)}, u32[]{:S(2)}, u32[]{:S(2)}) %collective-permute-start.43) | collective-permute-done | bytes 393248 | tf_op jit(solution)/shard_map/ppermute | solution.py:469
  541.7 13.3 %collective-permute-done.47 = bf16[256,1536]{1,0:T(8,128)(2,1)S(1)} collective-permute-done((bf16[256,1536]{1,0:T(8,128)(2,1)S(1)}, bf16[256,1536]{1,0:T(8,128)(2,1)S(1)}, u32[]{:S(2)}, u32[]{:S(2)}) %collective-permute-start.47) | collective-permute-done | bytes 786464 | tf_op jit(solution)/shard_map/ppermute | solution.py:465
  568.7 15.2 %shard_map.273 = bf16[1536,1536]{1,0:T(8,128)(2,1)} custom-call(s32[19]{0:T(128)} %concatenate.79.info, bf16[4,256,1536]{2,1,0:T(8,128)(2,1)} %pad_maximum_fusion.2.x_own.l_own, bf16[4,256,1536]{2,1,0:T(8,128)(2,1)} %collective-permute-done.26.x_oth.l_oth, bf16[4,256,768]{2,1,0:T(8,128)(2,1)} %get-tuple-element.58.r_own, ...), custom_call_target="tpu_custom_call" | custom-call | flops 3623878656 | bytes 15000000 | tf_op jit(solution)/shard_map/pallas_call | solution.py:753
  593.2 57.1 %shard_map.268 = (f32[2048,192]{1,0:T(8,128)}, f32[5120,192]{1,0:T(8,128)}, f32[5120,192]{1,0:T(8,128)}) custom-call(s32[76]{0:T(128)} %concatenate.80.chunks, bf16[2048,192]{1,0:T(8,128)(2,1)} %slice.566.q, bf16[2048,192]{1,0:T(8,128)(2,1)} %shard_map.267.g, f32[2048,192]{1,0:T(8,128)} %get-tuple-element.47.attended, ...), custom_call_target="tpu_custom_call" | custom-call | flops 15099494400 | bytes 20000000 | tf_op jit(solution)/shard_map/pallas_call | solution.py:801
  674.9 18.3 %collective-permute-done.55.far_on = bf16[160,384]{1,0:T(8,128)(2,1)S(1)} collective-permute-done((bf16[160,384]{1,0:T(8,128)(2,1)S(1)}, bf16[160,384]{1,0:T(8,128)(2,1)S(1)}, u32[]{:S(2)}, u32[]{:S(2)}) %collective-permute-start.55) | collective-permute-done | bytes 122912 | tf_op jit(solution)/shard_map/ppermute | solution.py:461
  707.9 15.2 %shard_map.270 = (bf16[4,256,1536]{2,1,0:T(8,128)(2,1)}, bf16[4,256,1536]{2,1,0:T(8,128)(2,1)}) custom-call(s32[19]{0:T(128)} %concatenate.79.info, bf16[2048,576]{1,0:T(8,128)(2,1)} %shard_map.269.rows_ref.right, bf16[1536,576]{1,0:T(8,128)(2,1)} %get-tuple-element.96.w_image, bf16[1536,576]{1,0:T(8,128)(2,1)} %get-tuple-element.95.w_text), custom_call_target="tpu_custom_call" | custom-call | flops 2717908992 | bytes 12000000 | tf_op jit(solution)/shard_map/pallas_call | solution.py:845
  764.0 10.4 %shard_map.272 = (bf16[1536,192]{1,0:T(8,128)(2,1)}, bf16[1536,192]{1,0:T(8,128)(2,1)}) custom-call(s32[19]{0:T(128)} %concatenate.79.info, bf16[4,256,1536]{2,1,0:T(8,128)(2,1)} %pad_maximum_fusion.4.own.l_own, bf16[4,256,1536]{2,1,0:T(8,128)(2,1)} %collective-permute-done.51.oth.l_oth, bf16[2048,192]{1,0:T(8,128)(2,1)} %get-tuple-element.38.rows_ref.right), custom_call_target="tpu_custom_call" | custom-call | flops 905969664 | bytes 12000000 | tf_op jit(solution)/shard_map/pallas_call | solution.py:765
  789.0 15.6 %shard_map.271 = (bf16[1536,576]{1,0:T(8,128)(2,1)}, bf16[1536,576]{1,0:T(8,128)(2,1)}) custom-call(s32[19]{0:T(128)} %concatenate.79.info, bf16[4,256,1536]{2,1,0:T(8,128)(2,1)} %copy-done.6, bf16[4,256,1536]{2,1,0:T(8,128)(2,1)} %collective-permute-done.4.oth.l_oth, bf16[2048,576]{1,0:T(8,128)(2,1)} %shard_map.269.rows_ref.right), custom_call_target="tpu_custom_call" | custom-call | flops 2717908992 | bytes 12000000 | tf_op jit(solution)/shard_map/pallas_call | solution.py:765
  813.7 42.2 %pmax.7 = f32[12]{0:T(128)S(1)} all-reduce(f32[12]{0:T(128)S(1)} %select_n.350), channel_id=1, replica_groups=mesh['g'=4,'y'=2,'x'=2,'c'=2] {'g','y','x'}, use_global_device_ids=true, to_apply=%region_21.22 | all-reduce | flops 12 | bytes 96 | tf_op jit(solution)/shard_map/pmax | solution.py:730
  901.5 21.3 %all-reduce.3.cloned.1.call-done = f32[16,60,96]{2,0,1:T(8,128)} async-done(((f32[16,60,96]{2,0,1:T(8,128)}), f32[16,60,96]{2,0,1:T(8,128)}) %all-reduce.3.cloned.1.call-update) | async-done | bytes 368656
  925.8 65.1 %reduce-scatter.6.cloned.1.call-done = bf16[384,1152]{1,0:T(8,128)(2,1)} async-done(((bf16[1536,1152]{1,0:T(8,128)(2,1)}), bf16[384,1152]{1,0:T(8,128)(2,1)}) %reduce-scatter.6.cloned.1.call-update) | async-done | bytes 884752 | tf_op jit(solution)/shard_map/reduce_scatter | solution.py:858
  (620 shorter events, 453.6 us)
Async XLA Ops:
  7.2 103.6 %all-gather.5.cloned.1.call-start = ((), (), s32[]{:S(2)}) async-start(), calls=%async_computation.4 | async-start | bytes 4423680 | tf_op jit(solution)/shard_map/all_gather | solution.py:583
  34.0 111.5 %all-gather.7.cloned.1.call-start = ((), (), s32[]{:S(2)}) async-start(), calls=%async_computation.5 | async-start | bytes 1474560 | tf_op jit(solution)/shard_map/all_gather | solution.py:584
  64.8 33.5 %collective-permute-start.14 = (bf16[96,3456]{1,0:T(8,128)(2,1)}, bf16[96,3456]{1,0:T(8,128)(2,1)}, u32[]{:S(2)}, u32[]{:S(2)}) collective-permute-start(bf16[96,3456]{1,0:T(8,128)(2,1)} %get-tuple-element.128), channel_id=1, source_target_pairs={{0,6},{2,4},{4,2},{6,0},{1,7},{3,5},{5,3},{7,1},{8,14},{10,12},{12... | collective-permute-start | bytes 1990664 | tf_op jit(solution)/shard_map/ppermute | solution.py:477
  75.9 40.1 %collective-permute-start.4 = (bf16[4,256,1536]{2,1,0:T(8,128)(2,1)S(1)}, bf16[4,256,1536]{2,1,0:T(8,128)(2,1)}, u32[]{:S(2)}, u32[]{:S(2)}) collective-permute-start(bf16[4,256,1536]{2,1,0:T(8,128)(2,1)S(1)} %pad_maximum_fusion.1.own.l_own), channel_id=1, source_target_pairs={{0,1},{1,0},{2,3},{3,2},{4,5},{5,4},{6,7},{7,6},{8,9},{9,8},{10,11... | collective-permute-start | bytes 9437192 | tf_op jit(solution)/shard_map/ppermute | solution.py:473
  103.4 262.9 %all-gather.11.cloned.1.call-start = ((), (), s32[]{:S(2)}) async-start(), calls=%async_computation.7 | async-start | bytes 5898240 | tf_op jit(solution)/shard_map/all_gather | solution.py:586
  133.8 35.6 %collective-permute-start.9 = (bf16[1184,384]{1,0:T(8,128)(2,1)}, bf16[1184,384]{1,0:T(8,128)(2,1)S(1)}, u32[]{:S(2)}, u32[]{:S(2)}) collective-permute-start(bf16[1184,384]{1,0:T(8,128)(2,1)} %constant_dynamic-slice_fusion.41), channel_id=1, source_target_pairs={{0,8},{8,16},{16,24},{1,9},{9,17},{17,25},{2,10},{10,18},{18,26},{... | collective-permute-start | bytes 2727944 | tf_op jit(solution)/shard_map/ppermute | solution.py:461
  138.9 255.2 %all-gather.9.cloned.1.call-start = ((), (), s32[]{:S(2)}) async-start(), calls=%async_computation.6 | async-start | bytes 5898240 | tf_op jit(solution)/shard_map/all_gather | solution.py:585
  150.0 61.5 %collective-permute-start.10 = (bf16[1184,384]{1,0:T(8,128)(2,1)S(1)}, bf16[1184,384]{1,0:T(8,128)(2,1)S(1)}, u32[]{:S(2)}, u32[]{:S(2)}) collective-permute-start(bf16[1184,384]{1,0:T(8,128)(2,1)S(1)} %slice.568), channel_id=1, source_target_pairs={{8,0},{16,8},{24,16},{9,1},{17,9},{25,17},{10,2},{18,10},{26,18},{... | collective-permute-start | bytes 2727944 | tf_op jit(solution)/shard_map/ppermute | solution.py:461
  151.3 74.4 %collective-permute-start.11 = (bf16[160,384]{1,0:T(8,128)(2,1)S(1)}, bf16[160,384]{1,0:T(8,128)(2,1)S(1)}, u32[]{:S(2)}, u32[]{:S(2)}) collective-permute-start(bf16[160,384]{1,0:T(8,128)(2,1)S(1)} %slice.569), channel_id=1, source_target_pairs={{16,0},{24,8},{17,1},{25,9},{18,2},{26,10},{19,3},{27,11},{20,4},{... | collective-permute-start | bytes 368648 | tf_op jit(solution)/shard_map/ppermute | solution.py:461
  300.4 29.2 %collective-permute-start.21 = (bf16[128,1536]{1,0:T(8,128)(2,1)S(1)}, bf16[128,1536]{1,0:T(8,128)(2,1)}, u32[]{:S(2)}, u32[]{:S(2)}) collective-permute-start(bf16[128,1536]{1,0:T(8,128)(2,1)S(1)} %get-tuple-element.118), channel_id=1, source_target_pairs={{0,4},{4,0},{1,5},{5,1},{2,6},{6,2},{3,7},{7,3},{8,12},{12,8},{9,1... | collective-permute-start | bytes 1179656 | tf_op jit(solution)/shard_map/ppermute | solution.py:469
  307.2 550.3 %reduce-scatter.12.cloned.1.call-start = ((), (), s32[]{:S(2)}) async-start(), calls=%async_computation.11 | async-start | bytes 5898240 | tf_op jit(solution)/shard_map/reduce_scatter | solution.py:858
  457.6 408.6 %reduce-scatter.10.cloned.1.call-start = ((), (), s32[]{:S(2)}) async-start(), calls=%async_computation.10 | async-start | bytes 5898240 | tf_op jit(solution)/shard_map/reduce_scatter | solution.py:858
  465.1 61.7 %collective-permute-start.38 = (bf16[128,1536]{1,0:T(8,128)(2,1)S(1)}, bf16[128,1536]{1,0:T(8,128)(2,1)S(1)}, u32[]{:S(2)}, u32[]{:S(2)}) collective-permute-start(bf16[128,1536]{1,0:T(8,128)(2,1)S(1)} %get-tuple-element.112), channel_id=1, source_target_pairs={{0,4},{4,0},{1,5},{5,1},{2,6},{6,2},{3,7},{7,3},{8,12},{12,8},{9,1... | collective-permute-start | bytes 1179656 | tf_op jit(solution)/shard_map/ppermute | solution.py:469
  473.6 30.7 %collective-permute-start.41 = (bf16[128,1536]{1,0:T(8,128)(2,1)S(1)}, bf16[128,1536]{1,0:T(8,128)(2,1)S(1)}, u32[]{:S(2)}, u32[]{:S(2)}) collective-permute-start(bf16[128,1536]{1,0:T(8,128)(2,1)S(1)} %get-tuple-element.105), channel_id=1, source_target_pairs={{0,2},{2,0},{1,3},{3,1},{4,6},{6,4},{5,7},{7,5},{8,10},{10,8},{9,1... | collective-permute-start | bytes 1179656 | tf_op jit(solution)/shard_map/ppermute | solution.py:465
  492.6 34.4 %collective-permute-start.46 = (bf16[128,1536]{1,0:T(8,128)(2,1)S(1)}, bf16[128,1536]{1,0:T(8,128)(2,1)S(1)}, u32[]{:S(2)}, u32[]{:S(2)}) collective-permute-start(bf16[128,1536]{1,0:T(8,128)(2,1)S(1)} %get-tuple-element.106), channel_id=1, source_target_pairs={{0,4},{4,0},{1,5},{5,1},{2,6},{6,2},{3,7},{7,3},{8,12},{12,8},{9,1... | collective-permute-start | bytes 1179656 | tf_op jit(solution)/shard_map/ppermute | solution.py:469
  583.9 305.0 %reduce-scatter.8.cloned.1.call-start = ((), (), s32[]{:S(2)}) async-start(), calls=%async_computation.9 | async-start | bytes 1474560 | tf_op jit(solution)/shard_map/reduce_scatter | solution.py:858
  655.1 43.4 %collective-permute-start.53 = (bf16[1184,384]{1,0:T(8,128)(2,1)S(1)}, bf16[1184,384]{1,0:T(8,128)(2,1)S(1)}, u32[]{:S(2)}, u32[]{:S(2)}) collective-permute-start(bf16[1184,384]{1,0:T(8,128)(2,1)S(1)} %pad_maximum_fusion.27), channel_id=1, source_target_pairs={{0,8},{8,16},{16,24},{1,9},{9,17},{17,25},{2,10},{10,18},{18,26},{... | collective-permute-start | bytes 2727944 | tf_op jit(solution)/shard_map/ppermute | solution.py:461
  659.2 39.3 %collective-permute-start.52 = (bf16[1184,384]{1,0:T(8,128)(2,1)S(1)}, bf16[1184,384]{1,0:T(8,128)(2,1)S(1)}, u32[]{:S(2)}, u32[]{:S(2)}) collective-permute-start(bf16[1184,384]{1,0:T(8,128)(2,1)S(1)} %pad_maximum_fusion.26), channel_id=1, source_target_pairs={{8,0},{16,8},{24,16},{9,1},{17,9},{25,17},{10,2},{18,10},{26,18},{... | collective-permute-start | bytes 2727944 | tf_op jit(solution)/shard_map/ppermute | solution.py:461
  660.7 32.6 %collective-permute-start.55 = (bf16[160,384]{1,0:T(8,128)(2,1)S(1)}, bf16[160,384]{1,0:T(8,128)(2,1)S(1)}, u32[]{:S(2)}, u32[]{:S(2)}) collective-permute-start(bf16[160,384]{1,0:T(8,128)(2,1)S(1)} %pad_maximum_fusion.32), channel_id=1, source_target_pairs={{0,16},{8,24},{1,17},{9,25},{2,18},{10,26},{3,19},{11,27},{4,20},{... | collective-permute-start | bytes 368648 | tf_op jit(solution)/shard_map/ppermute | solution.py:461
  669.1 29.4 %collective-permute-start.54 = (bf16[160,384]{1,0:T(8,128)(2,1)S(1)}, bf16[160,384]{1,0:T(8,128)(2,1)S(1)}, u32[]{:S(2)}, u32[]{:S(2)}) collective-permute-start(bf16[160,384]{1,0:T(8,128)(2,1)S(1)} %pad_maximum_fusion.31), channel_id=1, source_target_pairs={{16,0},{24,8},{17,1},{25,9},{18,2},{26,10},{19,3},{27,11},{20,4},{... | collective-permute-start | bytes 368648 | tf_op jit(solution)/shard_map/ppermute | solution.py:461
  777.3 145.6 %all-reduce.3.cloned.1.call-start = ((), (), s32[]{:S(2)}) async-start(), calls=%async_computation.12 | async-start | bytes 983040
  806.7 184.2 %reduce-scatter.6.cloned.1.call-start = ((), (), s32[]{:S(2)}) async-start(), calls=%async_computation.8 | async-start | bytes 4423680 | tf_op jit(solution)/shard_map/reduce_scatter | solution.py:858
  812.5 50.8 %collective-permute-start.39 = (bf16[256,1536]{1,0:T(8,128)(2,1)S(1)}, bf16[256,1536]{1,0:T(8,128)(2,1)}, u32[]{:S(2)}, u32[]{:S(2)}) collective-permute-start(bf16[256,1536]{1,0:T(8,128)(2,1)S(1)} %copy-done.33), channel_id=1, source_target_pairs={{0,1},{1,0},{2,3},{3,2},{4,5},{5,4},{6,7},{7,6},{8,9},{9,8},{10,11... | collective-permute-start | bytes 2359304 | tf_op jit(solution)/shard_map/ppermute | solution.py:473
  887.2 111.3 %collective-permute-start.63 = (f32[256,1536]{1,0:T(8,128)S(1)}, f32[256,1536]{1,0:T(8,128)}, u32[]{:S(2)}, u32[]{:S(2)}) collective-permute-start(f32[256,1536]{1,0:T(8,128)S(1)} %fusion.18), channel_id=1, source_target_pairs={{0,1},{1,0},{2,3},{3,2},{4,5},{5,4},{6,7},{7,6},{8,9},{9,8},{10,11... | collective-permute-start | bytes 4718600 | tf_op jit(solution)/shard_map/ppermute | solution.py:473
  (178 other events, 2175.0 us)
Sparse Core Ops, SparseCore 0:
  34.2 71.8 all-gather.4
  108.2 29.0 all-gather.6
  139.4 111.6 all-gather.10
  307.4 86.7 all-gather.8
  457.7 89.4 reduce-scatter.11
  584.0 100.0 reduce-scatter.9
  777.4 29.1 reduce-scatter.7
  812.3 110.5 all-reduce.2
  925.3 65.5 reduce-scatter.5

commit v2 on v1

v2 whole, which is shorter than its diff:
```python
import functools

import jax
import jax.numpy as jnp
from jax import lax
from jax.experimental import pallas as pl
from jax.experimental.pallas import tpu as pltpu
from jax.sharding import Mesh, PartitionSpec as P

HEAD = 64
IMG = 1024
TXT = 154
EPSILON = 1e-06
NEGATIVE = -1e30
BLOCKS = 4
SUB = 128
TAIL = 1184
TAIL_PAD = 1536
EDGE = 160
CHUNK = 256
KEYS = 512
SLAB = 64
ALIGN = 16
TEXT_ROWS = 176
BF = jnp.bfloat16
F32 = jnp.float32
SWAP = [(0, 1), (1, 0)]
VMEM_LIMIT = 60 * 1024 * 1024

VMEM = pl.BlockSpec(memory_space=pltpu.VMEM)
SMEM = pl.BlockSpec(memory_space=pltpu.SMEM)
ANY = pl.BlockSpec(memory_space=pl.ANY)

COUNT, OFFSET, TEXT_FROM, TEXT_TO = 0, 4, 8, 12
CORE, TAIL_FROM, EDGE_FROM, OWN_FROM, OWN_SEQ, NEXT_FROM, INFO = 16, 17, 18, 19, 20, 21, 22


def dot(a, b):
    return jnp.dot(a, b, preferred_element_type=F32)


def dot_back(a, b):
    return lax.dot_general(a, b, (((1,), (1,)), ((), ())), preferred_element_type=F32)


def dot_rows(a, b):
    return lax.dot_general(a, b, (((0,), (0,)), ((), ())), preferred_element_type=F32)


def took_us(time):
    return pl.CostEstimate(flops=int(time * 1.15e9), bytes_accessed=int(time * 1e6), transcendentals=0)


def after(body, n_in, n_deps):
    return lambda *refs: body(*refs[:n_in], *refs[n_in + n_deps :])


def whole(shape):
    return pl.BlockSpec(shape, lambda j: (0,) * len(shape), pipeline_mode=pl.Buffered(1))


def kept(shape):
    return pl.BlockSpec(shape, lambda j: (0,) * len(shape))


def block(shape):
    return pl.BlockSpec((1,) + shape, lambda j: (j,) + (0,) * len(shape))


def columns_from(rows, n, at):
    return pl.BlockSpec((rows, n), lambda j: (0, at), pipeline_mode=pl.Buffered(1))


def stepped(body, steps, in_specs, out_specs, out_shape, scratch, time, deps=()):
    run = pl.pallas_call(
        after(body, len(in_specs), len(deps)),
        grid=(steps,),
        out_shape=out_shape,
        in_specs=list(in_specs) + [ANY] * len(deps),
        out_specs=out_specs,
        scratch_shapes=list(scratch),
        compiler_params=pltpu.CompilerParams(vmem_limit_bytes=VMEM_LIMIT),
        cost_estimate=took_us(time),
    )
    return lambda *args: run(*args, *deps)


def sum_after(parts, kind, deps, time=1):
    n = len(parts)

    def body(*refs):
        total = refs[0][...].astype(F32)
        for part in refs[1:n]:
            total = total + part[...].astype(F32)
        refs[n][...] = total.astype(kind)

    return pl.pallas_call(
        after(body, n, len(deps)),
        out_shape=jax.ShapeDtypeStruct(parts[0].shape, kind),
        in_specs=[VMEM] * n + [ANY] * len(deps),
        out_specs=VMEM,
        compiler_params=pltpu.CompilerParams(vmem_limit_bytes=VMEM_LIMIT),
        cost_estimate=took_us(time),
    )(*parts, *deps)


def window(start, rows, total):
    base = jnp.minimum(lax.shift_right_logical(start, 4) * ALIGN, total - rows - ALIGN)
    return pl.ds(pl.multiple_of(base, ALIGN), rows + ALIGN), start - base


def moved(part, skip):
    rows = part.shape[0]
    shape = (rows + ALIGN, rows)
    there = lax.broadcasted_iota(jnp.int32, shape, 0) - skip
    return dot((there == lax.broadcasted_iota(jnp.int32, shape, 1)).astype(F32).astype(BF), part)


def read_rows(ref, start, rows):
    place, skip = window(start, rows, ref.shape[0])
    shape = (rows, rows + ALIGN)
    here = lax.broadcasted_iota(jnp.int32, shape, 1) - skip
    pick = (here == lax.broadcasted_iota(jnp.int32, shape, 0)).astype(F32).astype(BF)
    return dot(pick, ref[place, :]).astype(BF)


def layout_kernel(group_rows, seq, blocks, place, info, chunks):
    g, q = place[0], place[1]
    n_groups, n_seq = (blocks.shape[0] - 1) // BLOCKS, seq.shape[0] - 1
    start, stop = blocks[g * BLOCKS], blocks[g * BLOCKS + BLOCKS]

    def seq_of(position, shift):
        found = jnp.int32(0)
        for s in range(n_seq):
            found = jnp.where(position >= seq[s], s + shift, found)
        return found

    for j in range(BLOCKS):
        b = g * BLOCKS + (q ^ j)
        low, high = blocks[b], blocks[b + 1]
        text_from, text_to = jnp.int32(0), jnp.int32(0)
        for s in range(n_seq):
            first, last = jnp.maximum(seq[s] + IMG, low), jnp.minimum(seq[s + 1], high)
            text_from = jnp.where(first < last, first - low, text_from)
            text_to = jnp.where(first < last, last - low, text_to)
        info[COUNT + j] = high - low
        info[OFFSET + j] = low - start
        info[TEXT_FROM + j] = text_from
        info[TEXT_TO + j] = text_to
    own = blocks[g * BLOCKS + q]
    info[CORE] = place[2]
    info[TAIL_FROM] = jnp.maximum(stop - start - TAIL, 0)
    info[EDGE_FROM] = jnp.maximum(stop - start - EDGE, 0)
    info[OWN_FROM] = own
    info[OWN_SEQ] = seq_of(own, 0)
    info[NEXT_FROM] = seq[seq_of(own, 0) + 1]

    def span(steps):
        there = (g + steps >= 0) & (g + steps < n_groups)
        at = jnp.clip(g + steps, 0, n_groups - 1) * BLOCKS
        return jnp.where(there, blocks[at], 0), jnp.where(there, blocks[at + BLOCKS], 0)

    before, behind, ahead, beyond = span(-2), span(-1), span(1), span(2)
    n_chunks = (2 * KEYS + 2 * TAIL_PAD + group_rows) // KEYS
    i = 0
    for base, low, high, rows in (
        (jnp.maximum(before[1] - EDGE, before[0]) - (KEYS - EDGE), jnp.maximum(before[1] - EDGE, before[0]), before[1], KEYS),
        (
            jnp.maximum(behind[1] - TAIL, behind[0]) - (TAIL_PAD - TAIL),
            jnp.maximum(behind[1] - TAIL, behind[0]),
            behind[1],
            TAIL_PAD,
        ),
        (start, start, stop, group_rows),
        (ahead[0], ahead[0], jnp.minimum(ahead[1], ahead[0] + TAIL), TAIL_PAD),
        (beyond[0], beyond[0], jnp.minimum(beyond[1], beyond[0] + EDGE), KEYS),
    ):
        for step in range(rows // KEYS):
            chunks[i] = base + step * KEYS
            chunks[n_chunks + i] = low
            chunks[2 * n_chunks + i] = high
            i += 1
    n_tiles = group_rows // CHUNK
    for t in range(n_tiles):
        first = start + t * CHUNK
        last = jnp.minimum(first + CHUNK, stop) - 1
        chunks[3 * n_chunks + 2 * t] = jnp.where(first < stop, seq[seq_of(first, 0)], 0)
        chunks[3 * n_chunks + 2 * t + 1] = jnp.where(first < stop, seq[seq_of(last, 1)], 0)
        one = (first + CHUNK <= stop) & (seq_of(first, 0) == seq_of(last, 0))
        chunks[3 * n_chunks + 2 * n_tiles + 2 + t] = jnp.where(one, 1, 0)
    chunks[3 * n_chunks + 3 * n_tiles + 2] = seq[seq_of(start, 0)]
    chunks[3 * n_chunks + 3 * n_tiles + 3] = seq[seq_of(stop - 1, 1)]
    chunks[3 * n_chunks + 2 * n_tiles] = start
    chunks[3 * n_chunks + 2 * n_tiles + 1] = stop


def lane_spans(chunks, seq, n_chunks, n_tiles, t):
    start, stop = chunks[3 * n_chunks + 2 * n_tiles], chunks[3 * n_chunks + 2 * n_tiles + 1]
    position = start + t * CHUNK + lax.broadcasted_iota(jnp.int32, (1, CHUNK), 1)
    low, high = jnp.zeros_like(position), jnp.zeros_like(position)
    for s in range(seq.shape[0] - 1):
        hit = (position >= seq[s]) & (position < seq[s + 1]) & (position < stop)
        low, high = jnp.where(hit, seq[s], low), jnp.where(hit, seq[s + 1], high)
    return low, high


def enter_kernel(info, tokens, cotangent, image_mod, text_mod, modulated, grad_mlp):
    half = modulated.shape[0]
    n_seq = image_mod.shape[0]
    place = pl.ds(pl.multiple_of(info[CORE] * half, half), half)
    s = info[OWN_SEQ]
    after_s = jnp.minimum(s + 1, n_seq - 1)
    ids = row_ids(info[CORE] * half, half)
    live = ids < info[COUNT]
    is_text = live & (ids >= info[TEXT_FROM]) & (ids < info[TEXT_TO])
    is_next = live & (info[OWN_FROM] + ids >= info[NEXT_FROM])

    def pick(i):
        row = pl.ds(i, 1)
        own, text, following = image_mod[s][i : i + 1], text_mod[s][i : i + 1], image_mod[after_s][i : i + 1]
        return jnp.where(is_text, text, jnp.where(is_next, following, own))

    rows = tokens[place, :].astype(F32)
    centered = rows - jnp.mean(rows, axis=1, keepdims=True)
    normed = centered * lax.rsqrt(jnp.mean(centered * centered, axis=1, keepdims=True) + EPSILON)
    modulated[...] = (normed * (1.0 + pick(1)) + pick(0)).astype(BF)
    grad_mlp[...] = (pick(5) * jnp.where(live, cotangent[place, :].astype(F32), 0.0)).astype(BF)


def leave_kernel(
    info, grad_modulated, grad_first, branch, grad_mod_mlp, mlp_branch, tokens, cotangent, image_mod, text_mod,
    tokens_grad, sums,
):
    step = tokens_grad.shape[0]
    half = step * pl.num_programs(0)
    n_seq = image_mod.shape[0]
    s = info[OWN_SEQ]
    after_s = jnp.minimum(s + 1, n_seq - 1)
    ids = row_ids(info[CORE] * half + pl.program_id(0) * step, step)
    live = ids < info[COUNT]
    is_text = live & (ids >= info[TEXT_FROM]) & (ids < info[TEXT_TO])
    is_next = live & (info[OWN_FROM] + ids >= info[NEXT_FROM])
    is_own = live & jnp.logical_not(is_text | is_next)

    def pick(i):
        own, text, following = image_mod[s][i : i + 1], text_mod[s][i : i + 1], image_mod[after_s][i : i + 1]
        return jnp.where(is_text, text, jnp.where(is_next, following, own))

    def normal(rows):
        centered = rows - jnp.mean(rows, axis=1, keepdims=True)
        inverse = lax.rsqrt(jnp.mean(centered * centered, axis=1, keepdims=True) + EPSILON)
        return centered * inverse, inverse

    rows = tokens[...].astype(F32)
    normed, inverse = normal(rows)
    normed_mlp, _ = normal(rows + pick(2) * branch[...])

    @pl.when(pl.program_id(0) == 0)
    def _():
        sums[...] = jnp.zeros_like(sums)

    def add(i, term):
        for kept_rows, at in ((is_own, s), (is_next, after_s), (is_text, n_seq + s)):
            row = jnp.sum(jnp.where(kept_rows, term, 0.0), axis=0, keepdims=True)
            sums[at, i : i + 1, :] += row

    add(0, grad_modulated[...])
    add(1, grad_modulated[...] * normed)
    add(2, grad_first[...] * branch[...])
    add(3, grad_mod_mlp[...])
    add(4, grad_mod_mlp[...] * normed_mlp)
    add(5, cotangent[...].astype(F32) * mlp_branch[...])
    h = grad_modulated[...] * (1.0 + pick(1))
    back = h - jnp.mean(h, axis=1, keepdims=True) - normed * jnp.mean(h * normed, axis=1, keepdims=True)
    tokens_grad[...] = jnp.where(live, grad_first[...] + inverse * back, 0.0)


def row_ids(base, rows):
    return base + lax.broadcasted_iota(jnp.int32, (rows, 1), 0)


def for_rows(info, cap, body):
    count = info[COUNT + pl.program_id(0)]
    low = 0
    for rows in range(cap // 2, cap + 1, SUB):

        @pl.when((count > low) & (count <= rows))
        def _():
            body(rows)

        low = rows


def for_text(info, cap, body):
    j = pl.program_id(0)
    low, high = info[TEXT_FROM + j], info[TEXT_TO + j]

    @pl.when(high > low)
    def _():
        base = jnp.minimum(lax.shift_right_logical(low, 4) * ALIGN, cap - TEXT_ROWS)
        base = pl.multiple_of(base, ALIGN)
        ids = row_ids(base, TEXT_ROWS)
        body(pl.ds(base, TEXT_ROWS), (ids >= low) & (ids < high))


def half_places(info, half):
    mine = pl.multiple_of(info[CORE] * half, half)
    return pl.ds(mine, half), pl.ds(pl.multiple_of(half - mine, half), half)


def join(info, own, oth, out):
    half = own.shape[1]
    at_own, at_oth = half_places(info, half)
    out[at_own, :] = own[0]
    out[at_oth, :] = oth[0]


def part_ways(info, rows_ref, own, oth):
    half = own.shape[1]
    at_own, at_oth = half_places(info, half)
    own[0] = rows_ref[at_own, :]
    oth[0] = rows_ref[at_oth, :]


def split_columns(w, first, image, text):
    n = image.shape[1]
    image[...] = w[:, first : first + n]
    text[...] = w[:, first + n : first + 2 * n]


def to_group_rows(info, own, oth, w_image, w_text, out, joined, tile):
    cap = joined.shape[0]
    join(info, own, oth, joined)

    @pl.when(pl.program_id(0) == 0)
    def _():
        out[...] = jnp.zeros_like(out)

    def body(rows):
        tile[:rows, :] = dot(joined[:rows, :], w_image[...]).astype(BF)

        def text(place, is_text):
            tile[place, :] = jnp.where(is_text, dot(joined[place, :], w_text[...]).astype(BF), tile[place, :])

        for_text(info, cap, text)
        j = pl.program_id(0)
        place, skip = window(info[OFFSET + j], rows, out.shape[0])
        part = moved(tile[:rows, :], skip).astype(BF)
        ids = row_ids(-skip, rows + ALIGN)
        out[place, :] = jnp.where((ids >= 0) & (ids < info[COUNT + j]), part, out[place, :])

    for_rows(info, cap, body)


def project_kernel(info, own, oth, w, q, kv, tail, edge, head, head_edge, w_image, w_text, out, joined, tile):
    @pl.when(pl.program_id(0) == 0)
    def _():
        split_columns(w, 0, w_image, w_text)

    to_group_rows(info, own, oth, w_image, w_text, out, joined, tile)

    @pl.when(pl.program_id(0) == BLOCKS - 1)
    def _():
        n = q.shape[1]
        q[...] = out[:, :n]
        kv[...] = out[:, n:]
        tail[...] = read_rows(kv, info[TAIL_FROM], TAIL)
        edge[...] = read_rows(kv, info[EDGE_FROM], EDGE)
        head[...] = kv[:TAIL, :]
        head_edge[...] = kv[:EDGE, :]


def back_project_kernel(first, info, own, oth, w, out, w_image, w_text, joined, tile):
    @pl.when(pl.program_id(0) == 0)
    def _():
        split_columns(w, first, w_image, w_text)

    to_group_rows(info, own, oth, w_image, w_text, out, joined, tile)


def times_turned(info, x, w_image, w_text, result):
    cap = result.shape[0]

    def body(rows):
        result[:rows, :] = dot_back(x[:rows, :], w_image[...]).astype(BF)
        if rows < cap:
            result[rows:, :] = jnp.zeros((cap - rows, result.shape[1]), BF)

        def text(place, is_text):
            part = dot_back(x[place, :], w_text[...]).astype(BF)
            result[place, :] = jnp.where(is_text, part, result[place, :])

        for_text(info, cap, text)

    for_rows(info, cap, body)


def rows_to_slots_kernel(first, info, rows_ref, w, own, oth, w_image, w_text, x, result):
    j = pl.program_id(0)

    @pl.when(j == 0)
    def _():
        split_columns(w, first, w_image, w_text)

    def take(rows):
        x[:rows, :] = read_rows(rows_ref, info[OFFSET + j], rows)

    for_rows(info, x.shape[0], take)
    times_turned(info, x, w_image, w_text, result)
    part_ways(info, result, own, oth)


def slots_to_slots_kernel(info, x, w_image, w_text, own, oth, result):
    times_turned(info, x.at[0], w_image, w_text, result)
    part_ways(info, result, own, oth)


def gelu_parts(v):
    k = 0.7978845608028654
    square = v * v
    t = jnp.tanh(k * v * (1.0 + 0.044715 * square))
    half = 0.5 * (1.0 + t)
    return v * half, half + 0.5 * v * (1.0 - t * t) * (k + 3 * 0.044715 * k * square)


def mlp_up_kernel(info, x_own, x_oth, w_image, w_text, hid, slope, x, before):
    cap = x.shape[0]
    join(info, x_own, x_oth, x)

    def body(rows):
        before[:rows, :] = dot(x[:rows, :], w_image[...])

        def text(place, is_text):
            before[place, :] = jnp.where(is_text, dot(x[place, :], w_text[...]), before[place, :])

        for_text(info, cap, text)
        value, steep = gelu_parts(before[:rows, :])
        hid[0, :rows, :] = value.astype(BF)
        slope[0, :rows, :] = steep.astype(BF)
        if rows < cap:
            for ref in (hid, slope):
                ref[0, rows:, :] = jnp.zeros((cap - rows, ref.shape[2]), BF)

    for_rows(info, cap, body)


def mlp_back_kernel(
    info, g_own, g_oth, slope, upper_image, upper_text, lower_image, lower_text, gm_own, gm_oth, gb, g, back, result
):
    cap = g.shape[0]
    join(info, g_own, g_oth, g)

    def body(rows):
        back[:rows, :] = dot(g[:rows, :], lower_image[...]).astype(BF)

        def text(place, is_text):
            back[place, :] = jnp.where(is_text, dot(g[place, :], lower_text[...]).astype(BF), back[place, :])

        for_text(info, cap, text)
        gb[0, :rows, :] = (back[:rows, :].astype(F32) * slope[0, :rows, :].astype(F32)).astype(BF)
        if rows < cap:
            gb[0, rows:, :] = jnp.zeros((cap - rows, gb.shape[2]), BF)

    for_rows(info, cap, body)
    times_turned(info, gb.at[0], upper_image, upper_text, result)
    part_ways(info, result, gm_own, gm_oth)


def add_sums(info, left, right, acc_image, acc_text):
    cap = left.shape[0]
    j = pl.program_id(0)

    @pl.when(j == 0)
    def _():
        acc_image[...] = jnp.zeros_like(acc_image)
        acc_text[...] = jnp.zeros_like(acc_text)

    def body(rows):
        ids = row_ids(0, rows)
        is_text = (ids >= info[TEXT_FROM + j]) & (ids < info[TEXT_TO + j])
        is_image = (ids < info[COUNT + j]) & jnp.logical_not(is_text)
        acc_image[...] += dot_rows(left[:rows, :], jnp.where(is_image, right[:rows, :], jnp.zeros((), BF)))

    for_rows(info, cap, body)

    def text(place, is_text):
        acc_text[...] += dot_rows(left[place, :], jnp.where(is_text, right[place, :], jnp.zeros((), BF)))

    for_text(info, cap, text)


def give_sums(out, acc_image, acc_text):
    cut = acc_image.shape[1]

    @pl.when(pl.program_id(0) == BLOCKS - 1)
    def _():
        out[:, :cut] = acc_image[...].astype(BF)
        out[:, cut:] = acc_text[...].astype(BF)


def slot_sums_kernel(info, l_own, l_oth, right, out, acc_image, acc_text, left):
    join(info, l_own, l_oth, left)
    add_sums(info, left, right.at[0], acc_image, acc_text)
    give_sums(out, acc_image, acc_text)


def row_sums_kernel(info, l_own, l_oth, rows_ref, out, acc_image, acc_text, left, right):
    join(info, l_own, l_oth, left)

    def take(rows):
        right[:rows, :] = read_rows(rows_ref, info[OFFSET + pl.program_id(0)], rows)

    for_rows(info, left.shape[0], take)
    add_sums(info, left, right, acc_image, acc_text)
    give_sums(out, acc_image, acc_text)


def head_rows(turned, h):
    ids = lax.broadcasted_iota(jnp.int32, turned.shape, 0)
    return jnp.where((ids >= h * HEAD) & (ids < (h + 1) * HEAD), turned, 0)


def head_columns(plain, h):
    ids = lax.broadcasted_iota(jnp.int32, plain.shape, 1)
    return jnp.where((ids >= h * HEAD) & (ids < (h + 1) * HEAD), plain, 0)


def fold(combine, rows):
    parts = [rows[at : at + 8, :] for at in range(0, rows.shape[0], 8)]
    while len(parts) > 1:
        parts = [combine(a, b) for a, b in zip(parts[::2], parts[1::2])]
    return parts[0]


def slab_mask(chunks, i, n_chunks, low, q_from, q_to):
    position = chunks[i] + low + lax.broadcasted_iota(jnp.int32, (SLAB, 1), 0)
    valid = (position >= chunks[n_chunks + i]) & (position < chunks[2 * n_chunks + i])
    position = jnp.where(valid, position, -1)
    return (position >= q_from) & (position < q_to)


def for_chunks(chunks, n_chunks, t, body):
    low, high = chunks[3 * n_chunks + 2 * t], chunks[3 * n_chunks + 2 * t + 1]
    one = chunks[3 * n_chunks + 2 * pl.num_programs(0) + 2 + t] > 0

    def step(i, carry):
        base = chunks[i]
        start = jnp.maximum(base, chunks[n_chunks + i])
        stop = jnp.minimum(base + KEYS, chunks[2 * n_chunks + i])
        reached = (start < high) & (stop > low) & (start < stop)
        inside = one & (start == base) & (stop == base + KEYS) & (base >= low) & (stop <= high)

        @pl.when(reached & inside)
        def _():
            body(i, True)

        @pl.when(reached & jnp.logical_not(inside))
        def _():
            body(i, False)

        return carry

    lax.fori_loop(0, n_chunks, step, 0)


def sources_at(far_back, near_back, kv, near_on, far_on):
    chunk = 0
    for source, size, last in (
        (far_back, KEYS, True),
        (near_back, TAIL_PAD, True),
        (kv, kv.shape[0], False),
        (near_on, TAIL_PAD, False),
        (far_on, KEYS, False),
    ):
        rows = source.shape[0]
        skip = size - rows if last else 0
        for low in range(0, size, KEYS):
            first, stop = max(low, skip), min(low + KEYS, skip + rows)
            yield chunk, source, slice(first - skip, stop - skip), first - low, stop - low
            chunk += 1


def if_reached(chunks, n_chunks, i, body, otherwise=None):
    last = 3 * n_chunks + 3 * pl.num_programs(0) + 2
    start = jnp.maximum(chunks[i], chunks[n_chunks + i])
    stop = jnp.minimum(chunks[i] + KEYS, chunks[2 * n_chunks + i])
    reached = (start < chunks[last + 1]) & (stop > chunks[last]) & (start < stop)
    pl.when(reached)(body)
    if otherwise:
        pl.when(jnp.logical_not(reached))(otherwise)


def gather_keys(chunks, sources, k, v, plain, turned):
    n = k.shape[1]
    n_chunks = k.shape[0] // KEYS
    for i, source, rows, first, stop in sources_at(*sources):

        def take():
            at = i * KEYS
            for ref, columns in ((k, slice(0, n)), (v, slice(n, 2 * n))):
                ref[at + first : at + stop, :] = source[rows, columns]
                for low, high in ((0, first), (stop, KEYS)):
                    if low < high:
                        ref[at + low : at + high, :] = jnp.zeros((high - low, n), BF)
            part = slice(at, at + KEYS)
            turned[:, part] = plain[part, :].T

        if_reached(chunks, n_chunks, i, take)


def attend_kernel(
    chunks, seq, q, far_back, near_back, kv, near_on, far_on,
    out, exact, lse, top,
    k, v, v_turned, q_turn, logits, probs, total, high,
):
    t = pl.program_id(0)
    n_chunks = k.shape[0] // KEYS
    heads = q.shape[1] // HEAD
    wide = q.shape[0]

    @pl.when(t == 0)
    def _():
        gather_keys(chunks, (far_back, near_back, kv, near_on, far_on), k, v, v, v_turned)
        top[...] = jnp.full_like(top, NEGATIVE)

    live = chunks[3 * n_chunks + 2 * t + 1] > 0

    @pl.when(live)
    def _():
        turned = (q[...].astype(F32) * HEAD**-0.5).T
        for h in range(heads):
            q_turn[h] = head_rows(turned, h).astype(BF)
        lanes_from, lanes_to = lane_spans(chunks, seq, n_chunks, pl.num_programs(0), t)
        total[...] = jnp.zeros_like(total)
        high[...] = jnp.full_like(high, NEGATIVE)

        def first(i, whole_chunk):
            place = pl.ds(pl.multiple_of(i * KEYS, KEYS), KEYS)
            for h in range(heads):
                logits[h, i] = dot(k[place, :], q_turn[h])
            for low in range(0, KEYS, SLAB):
                part = slice(low, low + SLAB)
                if not whole_chunk:
                    mask = slab_mask(chunks, i, n_chunks, low, lanes_from, lanes_to)
                for h in range(heads):
                    values = logits[h, i, part, :]
                    if not whole_chunk:
                        values = jnp.where(mask, values, NEGATIVE)
                        logits[h, i, part, :] = values
                    rows = slice(8 * h, 8 * h + 8)
                    high[rows, :] = jnp.maximum(high[rows, :], fold(jnp.maximum, values))

        for_chunks(chunks, n_chunks, t, first)
        tops = [jnp.max(high[8 * h : 8 * h + 8, :], axis=0, keepdims=True) for h in range(heads)]
        high[...] = jnp.zeros_like(high)

        def second(i, whole_chunk):
            place = pl.ds(pl.multiple_of(i * KEYS, KEYS), KEYS)
            for low in range(0, KEYS, SLAB):
                part = slice(low, low + SLAB)
                for h in range(heads):
                    p = jnp.exp(logits[h, i, part, :] - tops[h])
                    rows = slice(8 * h, 8 * h + 8)
                    high[rows, :] += fold(jnp.add, p)
                    probs[part, h * wide : (h + 1) * wide] = p.astype(BF)
            for h in range(heads):
                rows = slice(h * HEAD, (h + 1) * HEAD)
                total[rows, :] += dot(v_turned[rows, place], probs[:, h * wide : (h + 1) * wide])

        for_chunks(chunks, n_chunks, t, second)
        for h in range(heads):
            rows = slice(h * HEAD, (h + 1) * HEAD)
            sums = jnp.sum(high[8 * h : 8 * h + 8, :], axis=0, keepdims=True)
            total[rows, :] = total[rows, :] / sums
            lse[0, h : h + 1, :] = tops[h] + jnp.log(sums)
            seen = jnp.where(lanes_to > lanes_from, tops[h], NEGATIVE)
            top[h : h + 1, :] = jnp.maximum(top[h : h + 1, :], seen)
        result = total[...].T
        exact[...] = result
        out[...] = result.astype(BF)

    @pl.when(jnp.logical_not(live))
    def _():
        exact[...] = jnp.zeros_like(exact)
        out[...] = jnp.zeros_like(out)
        lse[...] = jnp.zeros_like(lse)


def attend_back_kernel(
    chunks, seq, q, g, attended, far_back, near_back, kv, near_on, far_on, lse,
    dq, d_far_back, d_near_back, d_kv, d_near_on, d_far_on,
    k, v, k_turned, q_stack, g_stack, q_turn, g_turn, logits, grads_of, probs, grad_logits, total, dk, dv,
):
    t = pl.program_id(0)
    n_chunks = k.shape[0] // KEYS
    heads = q.shape[1] // HEAD
    wide = q.shape[0]

    @pl.when(t == 0)
    def _():
        gather_keys(chunks, (far_back, near_back, kv, near_on, far_on), k, v, k, k_turned)
        for i in range(n_chunks):

            def clear():
                dk[i * KEYS : (i + 1) * KEYS, :] = jnp.zeros((KEYS, dk.shape[1]), F32)
                dv[i * KEYS : (i + 1) * KEYS, :] = jnp.zeros((KEYS, dk.shape[1]), F32)

            if_reached(chunks, n_chunks, i, clear)

    live = chunks[3 * n_chunks + 2 * t + 1] > 0

    @pl.when(live)
    def _():
        scaled = q[...].astype(F32) * HEAD**-0.5
        grads = g[...].astype(F32)
        q_turned, g_turned = scaled.T, grads.T
        product = g_turned * attended[...].T
        delta, logs = [], []
        for h in range(heads):
            rows = slice(h * wide, (h + 1) * wide)
            q_stack[rows, :] = head_columns(scaled, h).astype(BF)
            g_stack[rows, :] = head_columns(grads, h).astype(BF)
            q_turn[h] = head_rows(q_turned, h).astype(BF)
            g_turn[h] = head_rows(g_turned, h).astype(BF)
            delta.append(jnp.sum(product[h * HEAD : (h + 1) * HEAD, :], axis=0, keepdims=True))
            logs.append(lse[0, h : h + 1, :])
        lanes_from, lanes_to = lane_spans(chunks, seq, n_chunks, pl.num_programs(0), t)
        total[...] = jnp.zeros_like(total)

        def body(i, whole_chunk):
            place = pl.ds(pl.multiple_of(i * KEYS, KEYS), KEYS)
            for h in range(heads):
                logits[h] = dot(k[place, :], q_turn[h])
                grads_of[h] = dot(v[place, :], g_turn[h])
            for low in range(0, KEYS, SLAB):
                part = slice(low, low + SLAB)
                if not whole_chunk:
                    mask = slab_mask(chunks, i, n_chunks, low, lanes_from, lanes_to)
                for h in range(heads):
                    lanes = slice(h * wide, (h + 1) * wide)
                    p = jnp.exp(logits[h, part, :] - logs[h])
                    if not whole_chunk:
                        p = jnp.where(mask, p, 0.0)
                    probs[part, lanes] = p.astype(BF)
                    grad_logits[part, lanes] = (p * (grads_of[h, part, :] - delta[h])).astype(BF)
            for h in range(heads):
                rows = slice(h * HEAD, (h + 1) * HEAD)
                total[rows, :] += dot(k_turned[rows, place], grad_logits[:, h * wide : (h + 1) * wide])
            dv[place, :] += dot(probs[...], g_stack[...])
            dk[place, :] += dot(grad_logits[...], q_stack[...])

        for_chunks(chunks, n_chunks, t, body)
        dq[...] = (total[...].T * HEAD**-0.5).astype(BF)

    @pl.when(jnp.logical_not(live))
    def _():
        dq[...] = jnp.zeros_like(dq)

    @pl.when(t == pl.num_programs(0) - 1)
    def _():
        n = dk.shape[1]
        for i, out, rows, first, stop in sources_at(d_far_back, d_near_back, d_kv, d_near_on, d_far_on):

            def give():
                place = slice(i * KEYS + first, i * KEYS + stop)
                out[rows, :n] = dk[place, :].astype(out.dtype)
                out[rows, n:] = dv[place, :].astype(out.dtype)

            def blank():
                out[rows, :] = jnp.zeros((stop - first, 2 * n), out.dtype)

            if_reached(chunks, n_chunks, i, give, blank)


def gather_grads_kernel(info, dq, d_kv, near_back, near_on, far_back, far_on, out, total):
    total[...] = d_kv[...]
    for start, part in ((info[TAIL_FROM], near_back), (info[EDGE_FROM], far_back)):
        place, skip = window(start, part.shape[0], total.shape[0])
        total[place, :] += moved(part[...], skip)
    for part in (near_on, far_on):
        total[: part.shape[0], :] += part[...].astype(F32)
    n = dq.shape[1]
    out[:, :n] = dq[...]
    out[:, n:] = total[...].astype(BF)


def copy_after(source, deps):
    return sum_after([source], source.dtype, deps)


def shift(value, steps):
    count = lax.axis_size("g")
    pairs = [(i, i + steps) for i in range(count) if 0 <= i + steps < count]
    if not pairs:
        return jnp.zeros_like(value)
    return lax.ppermute(value, "g", pairs)


def if_needed(predicate, run, *values):
    return lax.cond(predicate, run, lambda *v: tuple(jnp.zeros_like(a) for a in v), *values)


def max_over_groups(value):
    groups = lax.axis_size("g")
    top = value
    for step in range(1, groups):
        top = jnp.maximum(top, lax.ppermute(value, "g", [(i, (i + step) % groups) for i in range(groups)]))
    return top


def max_over_plane(value):
    return jnp.maximum(jnp.maximum(value, over_x(value)), jnp.maximum(over_y(value), over_xy(value)))


def over_x(value):
    return lax.ppermute(value, "x", SWAP)


def over_y(value):
    return lax.ppermute(value, "y", SWAP)


def over_core(value):
    return lax.ppermute(value, "c", SWAP)


def over_xy(value):
    return lax.ppermute(value, ("y", "x"), [(0, 3), (1, 2), (2, 1), (3, 0)])


def over_groups(sums):
    return lax.psum_scatter(sums, "g", scatter_dimension=0, tiled=True)


def spread_begin(value):
    return value, over_x(value), over_y(value)


def spread_next(begun, deps=()):
    value, from_x, from_y = begun
    cut = value.shape[0] // 2
    on_y, on_x = from_x[:cut], from_y[cut:]
    if deps:
        on_y, on_x = sum_after([on_y], BF, deps), sum_after([on_x], BF, deps)
    return value, from_x, from_y, on_y, on_x, over_y(on_y), over_x(on_x)


def spread_end(state):
    value, from_x, from_y, _, _, low, high = state
    own = jnp.stack([value, from_x, from_y, jnp.concatenate([low, high], axis=0)])
    return own, over_core(own)


def spread(value, deps=()):
    return spread_end(spread_next(spread_begin(value), deps))


def add16(*parts):
    total = parts[0].astype(F32)
    for part in parts[1:]:
        total = total + part.astype(F32)
    return total


def core_sum(own, oth, deps=()):
    other = over_core(oth)
    half, width = own.shape[1:]
    cut = half // 2
    cuts = ((0, 0, half), (3, 0, cut), (3, cut, half), (1, 0, cut), (1, cut, half), (2, 0, cut), (2, cut, half))

    def body(*refs):
        for out, (j, low, high) in zip(refs[2:], cuts):
            out[...] = (refs[0][j, low:high, :].astype(F32) + refs[1][j, low:high, :].astype(F32)).astype(BF)

    return pl.pallas_call(
        after(body, 2, len(deps)),
        out_shape=tuple(jax.ShapeDtypeStruct((high - low, width), BF) for _, low, high in cuts),
        in_specs=[VMEM] * 2 + [ANY] * len(deps),
        out_specs=(VMEM,) * len(cuts),
        compiler_params=pltpu.CompilerParams(vmem_limit_bytes=VMEM_LIMIT),
        cost_estimate=took_us(3),
    )(own, other, *deps)


def collect_begin(pieces):
    mine, far_x, far_y, x_low, x_high, y_low, y_high = pieces
    from_x, from_y = over_x(far_x), over_y(far_y)
    return mine, x_high, y_low, from_x, from_y, over_x(x_low), over_y(y_high)


def collect_next(begun, deps=()):
    mine, x_high, y_low, from_x, from_y, first_x, first_y = begun
    on_x, on_y = sum_after((x_high, from_y), BF, deps), sum_after((y_low, from_x), BF, deps)
    return mine, first_x, first_y, on_x, on_y, over_x(on_x), over_y(on_y)


def collect_end(state, deps=()):
    own, first_x, first_y, _, _, last_x, last_y = state
    cut = own.shape[0] // 2
    n = 5

    def body(mine, first_x, first_y, last_x, last_y, out):
        out[:cut, :] = mine[:cut, :].astype(F32) + first_x[...].astype(F32) + last_y[...].astype(F32)
        out[cut:, :] = mine[cut:, :].astype(F32) + last_x[...].astype(F32) + first_y[...].astype(F32)

    return pl.pallas_call(
        after(body, n, len(deps)),
        out_shape=jax.ShapeDtypeStruct(own.shape, F32),
        in_specs=[VMEM] * n + [ANY] * len(deps),
        out_specs=VMEM,
        compiler_params=pltpu.CompilerParams(vmem_limit_bytes=VMEM_LIMIT),
        cost_estimate=took_us(2),
    )(own, first_x, first_y, last_x, last_y, *deps)


def sums_of_shares(shares, g, q, deps):
    groups = lax.axis_size("g")
    pick = lambda values, at: lax.dynamic_index_in_dim(values, at, 0, keepdims=False)
    shares = jnp.moveaxis(shares.reshape((groups, BLOCKS) + shares.shape[1:]), 1, 0)
    shares = (
        pick(shares, q)
        + over_x(pick(shares, q ^ 1))
        + over_y(pick(shares, q ^ 2))
        + over_xy(pick(shares, q ^ 3))
    )
    shares = sum_after([shares], F32, deps)
    total = pick(shares, g)
    for step in range(1, groups):
        pairs = [(i, (i + step) % groups) for i in range(groups)]
        total = total + lax.ppermute(pick(shares, lax.rem(g + step, groups)), "g", pairs)
    return total


def layer_norm(inputs):
    centered = inputs - jnp.mean(inputs, axis=1, keepdims=True)
    inverse_std = lax.rsqrt(jnp.mean(centered * centered, axis=1, keepdims=True) + EPSILON)
    return (centered * inverse_std, inverse_std)


def norm_back(grad_normed, normed, inverse_std):
    return inverse_std * (
        grad_normed
        - jnp.mean(grad_normed, axis=1, keepdims=True)
        - normed * jnp.mean(grad_normed * normed, axis=1, keepdims=True)
    )


def pick_pieces(pieces, place, deps=()):
    shape = pieces.shape[1:]

    def body(place_ref, source, *outs):
        for j, out in enumerate(outs):
            out[...] = source[place_ref[1] ^ j]

    return pl.pallas_call(
        after(body, 2, len(deps)),
        out_shape=(jax.ShapeDtypeStruct(shape, pieces.dtype),) * BLOCKS,
        in_specs=[SMEM, VMEM] + [ANY] * len(deps),
        out_specs=(VMEM,) * BLOCKS,
        compiler_params=pltpu.CompilerParams(vmem_limit_bytes=VMEM_LIMIT),
        cost_estimate=took_us(2),
    )(place, pieces, *deps)


def swap_pieces(picked):
    own, to_x, to_y, to_xy = picked
    return own, over_x(to_x), over_y(to_y), over_xy(to_xy)


def exchange(pieces, place):
    return swap_pieces(pick_pieces(pieces, place))


def arrange(got, place, body, out_shape, deps=()):
    n = len(got)

    def kernel(place_ref, *refs):
        for j in range(n):
            body(place_ref[1] ^ j, refs[j], refs[n:])

    return pl.pallas_call(
        after(kernel, 1 + n, len(deps)),
        out_shape=out_shape,
        in_specs=[SMEM] + [VMEM] * n + [ANY] * len(deps),
        out_specs=(VMEM,) * len(out_shape),
        compiler_params=pltpu.CompilerParams(vmem_limit_bytes=VMEM_LIMIT),
        cost_estimate=took_us(2),
    )(place, *got, *deps)


def stack_rows(b, piece, outs):
    rows = piece.shape[0]
    outs[0][pl.ds(pl.multiple_of(b * rows, ALIGN), rows), :] = piece[...]


def give_wide(b, piece, outs):
    n = piece.shape[1] // 2
    for k, out in enumerate(outs):
        out[:, pl.ds(pl.multiple_of(b * n, SUB), n)] = piece[:, k * n : (k + 1) * n].astype(F32)


def give_turned(b, piece, outs):
    n = piece.shape[1] // 2
    for k, out in enumerate(outs):
        out[pl.ds(pl.multiple_of(b * n, ALIGN), n), :] = piece[:, k * n : (k + 1) * n].astype(F32).T


def give_qkv(b, piece, outs):
    n = piece.shape[1] // 6
    for at in range(BLOCKS):

        @pl.when(b == at)
        def _():
            for k, out in enumerate(outs):
                for p in range(3):
                    part = piece[:, (3 * k + p) * n : (3 * k + p + 1) * n].astype(F32)
                    out[:, p, at * n : (at + 1) * n] = part


def local(
    tokens,
    cotangent,
    seq_offsets,
    block_offsets,
    image_mod,
    text_mod,
    image_qkv,
    text_qkv,
    image_out,
    text_out,
    image_fc1,
    text_fc1,
    image_fc2,
    text_fc2,
    clip_limits,
):
    rows_cap, width = tokens.shape
    half = rows_cap // 2
    share = image_qkv.shape[0]
    columns = image_qkv.shape[2]
    group_rows = BLOCKS * rows_cap
    mine = columns // BLOCKS
    fc = image_fc1.shape[1] // BLOCKS
    heads = mine // HEAD
    seq_count = seq_offsets.shape[0] - 1
    n_groups = lax.axis_size("g")
    g, c = lax.axis_index("g"), lax.axis_index("c")
    q = 2 * lax.axis_index("y") + lax.axis_index("x")

    def both_halves(rows):
        other = over_core(rows)
        return jnp.where(c == 0, jnp.concatenate([rows, other], axis=0), jnp.concatenate([other, rows], axis=0))

    def quarter(inputs):
        return jnp.moveaxis(inputs.reshape(share, -1, BLOCKS, mine), 2, 0).reshape(BLOCKS, share, -1)

    def quarter_turned(inputs):
        return jnp.swapaxes(inputs.reshape(BLOCKS, -1, share), 1, 2)

    def quarter_wide(inputs):
        return jnp.swapaxes(inputs.reshape(share, BLOCKS, -1), 0, 1)

    pack_qkv = jnp.concatenate([quarter(image_qkv), quarter(text_qkv)], axis=2)
    place = jnp.stack([g, q, c]).astype(jnp.int32)
    plane_of = lambda n: (jax.ShapeDtypeStruct((BLOCKS * share, n), BF),)
    (plane_qkv,) = arrange(exchange(pack_qkv, place), place, stack_rows, plane_of(6 * mine))

    n_tiles = group_rows // CHUNK
    reach = 2 * KEYS + 2 * TAIL_PAD + group_rows
    n_chunks = reach // KEYS
    info, chunks = pl.pallas_call(
        functools.partial(layout_kernel, group_rows),
        out_shape=(
            jax.ShapeDtypeStruct((INFO,), jnp.int32),
            jax.ShapeDtypeStruct((3 * n_chunks + 3 * n_tiles + 4,), jnp.int32),
        ),
        in_specs=[SMEM] * 3,
        out_specs=(SMEM, SMEM),
        cost_estimate=took_us(1),
    )(seq_offsets, block_offsets, place)

    my_rows = lambda inputs: lax.dynamic_slice_in_dim(inputs, c * half, half, 0)
    ids = c * half + jnp.arange(half, dtype=jnp.int32)
    my_seq = info[OWN_SEQ]
    next_seq = jnp.minimum(my_seq + 1, seq_count - 1)
    is_live = (ids < info[COUNT])[:, None]
    is_text = is_live & ((ids >= info[TEXT_FROM]) & (ids < info[TEXT_TO]))[:, None]
    is_next = is_live & (info[OWN_FROM] + ids >= info[NEXT_FROM])[:, None]
    vectors = (image_mod[my_seq], text_mod[my_seq], image_mod[next_seq])

    def modulation(which):
        return jnp.where(
            is_text, vectors[1][which][None], jnp.where(is_next, vectors[2][which][None], vectors[0][which][None])
        )

    shift_rows, scale_rows, gate_rows, shift_mlp, scale_mlp, gate_mlp = (modulation(i) for i in range(6))
    stream = my_rows(tokens).astype(F32)
    grad_stream = jnp.where(is_live, my_rows(cotangent).astype(F32), 0.0)
    normed, inverse_std = layer_norm(stream)
    modulated, grad_mlp = pl.pallas_call(
        enter_kernel,
        out_shape=(jax.ShapeDtypeStruct((half, width), BF),) * 2,
        in_specs=[SMEM] + [VMEM] * 4,
        out_specs=(VMEM, VMEM),
        compiler_params=pltpu.CompilerParams(vmem_limit_bytes=VMEM_LIMIT),
        cost_estimate=took_us(4),
    )(info, tokens, cotangent, image_mod, text_mod)

    slot = lambda n: jax.ShapeDtypeStruct((BLOCKS, half, n), BF)
    full = lambda n: jax.ShapeDtypeStruct((BLOCKS, rows_cap, n), BF)
    rows_of = lambda n, kind: jax.ShapeDtypeStruct((group_rows, n), kind)
    slot_block = block((half, width))
    scratch = lambda rows, n, kind=BF: pltpu.VMEM((rows, n), kind)
    weight_pair = lambda n: [scratch(width, n), scratch(width, n)]

    whole_qkv = lax.all_gather(plane_qkv, "g", axis=0, tiled=True)
    mod_begun = spread_begin(modulated)
    pack_rest = jnp.concatenate(
        [
            quarter_wide(image_fc1),
            quarter_wide(text_fc1),
            quarter_turned(image_fc2),
            quarter_turned(text_fc2),
            quarter_turned(image_out),
            quarter_turned(text_out),
        ],
        axis=2,
    )
    rest_picked = pick_pieces(pack_rest, place)
    mod_own, mod_oth = spread_end(spread_next(mod_begun, rest_picked[:1]))
    (plane_rest,) = arrange(swap_pieces(rest_picked), place, stack_rows, plane_of(4 * fc + 2 * mine))
    whole_out = lax.all_gather(plane_rest[:, 4 * fc :], "g", axis=0, tiled=True)
    whole_fc2 = lax.all_gather(plane_rest[:, 2 * fc : 4 * fc], "g", axis=0, tiled=True)

    pair = lambda rows: jax.ShapeDtypeStruct((rows, 2 * mine), BF)
    queries, pairs, tail, edge, head, head_edge = stepped(
        project_kernel,
        BLOCKS,
        [SMEM, slot_block, slot_block, whole(whole_qkv.shape)],
        [kept(s) for s in ((group_rows, mine), (group_rows, 2 * mine), (TAIL, 2 * mine), (EDGE, 2 * mine), (TAIL, 2 * mine), (EDGE, 2 * mine))],
        (rows_of(mine, BF), pair(group_rows), pair(TAIL), pair(EDGE), pair(TAIL), pair(EDGE)),
        weight_pair(3 * mine) + [scratch(group_rows, 3 * mine), scratch(rows_cap, width), scratch(rows_cap, 3 * mine)],
        1,
    )(info, mod_own, mod_oth, whole_qkv)

    near_back, near_on = shift(tail, 1), shift(head, -1)
    gmlp_begun = spread_begin(copy_after(grad_mlp, (queries,)))
    fc1_piece = copy_after(plane_rest[:, : 2 * fc], (near_back, near_on, *gmlp_begun[1:]))
    whole_fc1 = lax.all_gather(fc1_piece, "g", axis=0, tiled=True)
    gmlp_state = spread_next(gmlp_begun, (near_back, near_on, whole_out))
    gmlp_own, gmlp_oth = spread_end(gmlp_state)
    need_far = jnp.min(block_offsets[BLOCKS::BLOCKS] - block_offsets[:-1:BLOCKS]) < IMG + TXT
    far_back, far_on = if_needed(need_far, lambda a, b: (shift(a, 2), shift(b, -2)), edge, head_edge)
    sources = (far_back, near_back, pairs, near_on, far_on)
    source_specs = [whole(s.shape) for s in sources]

    tile_spec = pl.BlockSpec((CHUNK, mine), lambda t: (t, 0))
    log_spec = block((8, CHUNK))
    attended, attended_exact, logs, tops = stepped(
        attend_kernel,
        n_tiles,
        [SMEM, SMEM, tile_spec, *source_specs],
        (tile_spec, tile_spec, log_spec, kept((8, CHUNK))),
        (
            rows_of(mine, BF),
            rows_of(mine, F32),
            jax.ShapeDtypeStruct((n_tiles, 8, CHUNK), F32),
            jax.ShapeDtypeStruct((8, CHUNK), F32),
        ),
        [
            scratch(reach, mine),
            scratch(reach, mine),
            scratch(mine, reach),
            pltpu.VMEM((heads, mine, CHUNK), BF),
            pltpu.VMEM((heads, n_chunks, KEYS, CHUNK), F32),
            scratch(KEYS, heads * CHUNK),
            scratch(mine, CHUNK, F32),
            scratch(8 * heads, CHUNK, F32),
        ],
        1,
        (*gmlp_state[3:5], fc1_piece),
    )(chunks, seq_offsets, queries, *sources)

    def to_slots(n, first, rows, w, deps=(), time=10):
        return stepped(
            functools.partial(rows_to_slots_kernel, first),
            BLOCKS,
            [SMEM, whole(rows.shape), whole(w.shape)],
            (slot_block, slot_block),
            (slot(width), slot(width)),
            weight_pair(n) + [scratch(rows_cap, n), scratch(rows_cap, width)],
            time,
            deps,
        )(info, rows, w)

    branch_state = collect_next(collect_begin(core_sum(*to_slots(mine, 0, attended, whole_out, (), 1))), (whole_fc1,))
    branch = collect_end(branch_state)
    first = stream + gate_rows * branch
    normed_mlp, inverse_mlp = layer_norm(first)
    modulated_mlp = (normed_mlp * (1.0 + scale_mlp) + shift_mlp).astype(BF)

    mm_own, mm_oth = spread(copy_after(modulated_mlp, (gmlp_oth,)))
    fc_block = block((rows_cap, fc))
    hid, slope = stepped(
        mlp_up_kernel,
        BLOCKS,
        [SMEM, slot_block, slot_block, columns_from(width, fc, 0), columns_from(width, fc, 1)],
        (fc_block, fc_block),
        (full(fc), full(fc)),
        [scratch(rows_cap, width), scratch(rows_cap, fc, F32)],
        1,
    )(info, mm_own, mm_oth, whole_fc1, whole_fc1)

    def slot_sums(left, right, deps, time):
        return stepped(
            slot_sums_kernel,
            BLOCKS,
            [SMEM, slot_block, slot_block, fc_block],
            kept((width, 2 * fc)),
            jax.ShapeDtypeStruct((width, 2 * fc), BF),
            [scratch(width, fc, F32), scratch(width, fc, F32), scratch(rows_cap, width)],
            time,
            deps,
        )(info, *left, right)

    def row_sums(left, rows, deps=()):
        n = rows.shape[1]
        return stepped(
            row_sums_kernel,
            BLOCKS,
            [SMEM, slot_block, slot_block, whole(rows.shape)],
            kept((width, 2 * n)),
            jax.ShapeDtypeStruct((width, 2 * n), BF),
            [scratch(width, n, F32), scratch(width, n, F32), scratch(rows_cap, width), scratch(rows_cap, n)],
            n / 42,
            deps,
        )(info, *left, rows)

    fc2_sums = slot_sums((gmlp_own, gmlp_oth), hid, (), 1)
    fc2_part = over_groups(fc2_sums)
    head_top = jnp.max(tops[:heads], axis=1)
    spot = jnp.arange(BLOCKS)[:, None] == q
    head_max = jnp.where(spot, head_top[None, :], NEGATIVE).reshape(1, -1)
    gm_own, gm_oth, gb = stepped(
        mlp_back_kernel,
        BLOCKS,
        [SMEM, slot_block, slot_block, fc_block] + [columns_from(width, fc, at) for at in (0, 1, 0, 1)],
        (slot_block, slot_block, fc_block),
        (slot(width), slot(width), full(fc)),
        [scratch(rows_cap, width), scratch(rows_cap, fc), scratch(rows_cap, width)],
        1,
        (fc2_sums,),
    )(info, gmlp_own, gmlp_oth, slope, whole_fc1, whole_fc1, whole_fc2, whole_fc2)

    gm_part = core_sum(gm_own, gm_oth)
    gm_state = collect_begin(gm_part)
    fc1_sums = slot_sums((mm_own, mm_oth), gb, gm_part, 12)
    fc1_part = over_groups(fc1_sums)
    gm_state = collect_next(gm_state, (fc1_sums,))
    head_max = max_over_groups(copy_after(head_max, gm_state[3:5]))
    mlp_own, mlp_oth = stepped(
        slots_to_slots_kernel,
        BLOCKS,
        [SMEM, fc_block, columns_from(width, fc, 0), columns_from(width, fc, 1)],
        (slot_block, slot_block),
        (slot(width), slot(width)),
        [scratch(rows_cap, width)],
        10,
        gm_state[3:5],
    )(info, hid, whole_fc2, whole_fc2)
    grad_mod_mlp = collect_end(gm_state, (mlp_own, head_max))

    grad_first = jnp.where(
        is_live,
        grad_stream + norm_back(grad_mod_mlp * (1.0 + scale_mlp), normed_mlp, inverse_mlp),
        0.0,
    )
    grad_branch = (gate_rows * grad_first).astype(BF)
    gbr_begun = spread_begin(grad_branch)
    gbr_own, gbr_oth = spread_end(spread_next(gbr_begun, (fc2_part,)))
    mlp_part = core_sum(mlp_own, mlp_oth, (gbr_oth,))
    grad_attended = stepped(
        functools.partial(back_project_kernel, 0),
        BLOCKS,
        [SMEM, slot_block, slot_block, whole(whole_out.shape)],
        kept((group_rows, mine)),
        rows_of(mine, BF),
        weight_pair(mine) + [scratch(rows_cap, width), scratch(rows_cap, mine)],
        1,
    )(info, gbr_own, gbr_oth, whole_out)

    mlp_state = collect_begin(mlp_part)
    head_max = max_over_plane(copy_after(head_max, mlp_part[:1]))
    dq, give_far_back, give_back, d_pairs, give_on, give_far_on = stepped(
        attend_back_kernel,
        n_tiles,
        [SMEM, SMEM, tile_spec, tile_spec, tile_spec, *source_specs, log_spec],
        (tile_spec, *(kept(s.shape) for s in sources)),
        (rows_of(mine, BF), pair(EDGE), pair(TAIL), rows_of(2 * mine, F32), pair(TAIL), pair(EDGE)),
        [
            scratch(reach, mine),
            scratch(reach, mine),
            scratch(mine, reach),
            scratch(heads * CHUNK, mine),
            scratch(heads * CHUNK, mine),
            pltpu.VMEM((heads, mine, CHUNK), BF),
            pltpu.VMEM((heads, mine, CHUNK), BF),
            pltpu.VMEM((heads, KEYS, CHUNK), F32),
            pltpu.VMEM((heads, KEYS, CHUNK), F32),
            scratch(KEYS, heads * CHUNK),
            scratch(KEYS, heads * CHUNK),
            scratch(mine, CHUNK, F32),
            scratch(reach, mine, F32),
            scratch(reach, mine, F32),
        ],
        1,
        (mlp_part[0],),
    )(chunks, seq_offsets, queries, grad_attended, attended_exact, *sources, logs)
    gave_back, gave_on = shift(give_back, -1), shift(give_on, 1)
    gave_far_back, gave_far_on = if_needed(
        need_far, lambda a, b: (shift(a, -2), shift(b, 2)), give_far_back, give_far_on
    )

    out_sums = row_sums((gbr_own, gbr_oth), attended, (dq,))
    out_part = over_groups(copy_after(out_sums, (gave_back, gave_on)))
    mlp_state = collect_next(mlp_state, (out_sums,))
    pieces_of = lambda part, deps: pick_pieces(part.reshape(BLOCKS, share, -1), place, deps)
    mlp_branch = collect_end(mlp_state, (gave_back, gave_on))
    grad_qkv = pl.pallas_call(
        after(gather_grads_kernel, 7, 4),
        out_shape=rows_of(3 * mine, BF),
        in_specs=[SMEM] + [VMEM] * 6 + [ANY] * 4,
        out_specs=VMEM,
        scratch_shapes=[scratch(group_rows, 2 * mine, F32)],
        compiler_params=pltpu.CompilerParams(vmem_limit_bytes=VMEM_LIMIT),
        cost_estimate=took_us(8),
    )(info, dq, d_pairs, gave_back, gave_on, gave_far_back, gave_far_on, mlp_branch, out_sums, fc1_part, head_max)

    qkv_sums = row_sums((mod_own, mod_oth), grad_qkv)
    qkv_part = over_groups(qkv_sums)
    mod_part = core_sum(*to_slots(3 * mine, 0, grad_qkv, whole_qkv, (qkv_sums,)))
    mod_state = collect_next(collect_begin(mod_part))
    pair_f32 = lambda *shape: (jax.ShapeDtypeStruct(shape, F32),) * 2
    mixed_rows = jnp.where(is_live, first + gate_mlp * mlp_branch, 0.0).astype(BF)
    mixed = both_halves(copy_after(mixed_rows, mod_part[:1]))
    late_max = copy_after(head_max, mod_part[:1])[0]
    root_factor = jnp.sqrt(clip_limits / jnp.maximum(late_max, clip_limits))
    column_scale = jnp.repeat(root_factor, HEAD)[None, None, :]
    clipped = tuple((w[:, :2, :].astype(F32) * column_scale).astype(BF) for w in (image_qkv, text_qkv))
    grad_modulated = collect_end(mod_state, (mixed, *clipped))
    fc2_picked, fc1_picked = pieces_of(fc2_part, mod_state[3:5]), pieces_of(fc1_part, mod_state[3:5])
    fc2_got, fc1_got = swap_pieces(fc2_picked), swap_pieces(fc1_picked)
    fc2_outs = arrange(fc2_got, place, give_turned, pair_f32(BLOCKS * fc, share))
    fc1_outs = arrange(fc1_got, place, give_wide, pair_f32(share, BLOCKS * fc))
    qkv_picked, out_picked = pieces_of(qkv_part, ()), pieces_of(out_part, (grad_modulated,))
    qkv_got, out_got = swap_pieces(qkv_picked), swap_pieces(out_picked)
    out_outs = arrange(out_got, place, give_turned, pair_f32(columns, share))
    qkv_outs = arrange(qkv_got, place, give_qkv, pair_f32(share, 3, columns))

    row_block = pl.BlockSpec((half // 4, width), lambda t: (t, 0))
    vectors_spec = whole(image_mod.shape)
    tokens_grad_rows, mod_sum = stepped(
        leave_kernel,
        4,
        [SMEM] + [row_block] * 7 + [vectors_spec] * 2,
        (row_block, kept((2 * seq_count, 6, width))),
        (
            jax.ShapeDtypeStruct((half, width), F32),
            jax.ShapeDtypeStruct((2 * seq_count, 6, width), F32),
        ),
        (),
        8,
        (qkv_picked[0], fc2_picked[0], fc1_picked[0], out_picked[0]),
    )(
        info,
        grad_modulated,
        grad_first,
        branch,
        grad_mod_mlp,
        mlp_branch,
        my_rows(tokens),
        my_rows(cotangent),
        image_mod,
        text_mod,
    )
    mod_sum = mod_sum.reshape(2 * seq_count * 6, -1, share)
    mod_sum = jnp.swapaxes(mod_sum, 0, 1)
    mod_sum = mod_sum + over_core(mod_sum)
    mod_sum = sums_of_shares(mod_sum, g, q, qkv_got)
    mod_sum = mod_sum.reshape(2, seq_count, 6, share)

    return (
        mixed,
        both_halves(tokens_grad_rows),
        mod_sum[0],
        mod_sum[1],
        *qkv_outs,
        *out_outs,
        *fc1_outs,
        *fc2_outs,
        head_max[0],
        *clipped,
    )


def solution(mesh):
    devices = mesh.devices
    split = Mesh(devices.reshape(devices.shape[0] // BLOCKS, 2, 2, devices.shape[1]), ("g", "y", "x", "c"))
    dp = ("g", "y", "x")
    placed = (
        P(dp, None),
        P(dp, None),
        P(),
        P(),
        P(),
        P(),
        P(dp, None, "c"),
        P(dp, None, "c"),
        P("c", dp),
        P("c", dp),
        P(dp, "c"),
        P(dp, "c"),
        P("c", dp),
        P("c", dp),
        P("c"),
    )
    return jax.shard_map(
        local,
        mesh=split,
        in_specs=placed,
        out_specs=(
            P(dp, None),
            P(dp, None),
            P(None, None, dp),
            P(None, None, dp),
            P(dp, None, "c"),
            P(dp, None, "c"),
            P("c", dp),
            P("c", dp),
            P(dp, "c"),
            P(dp, "c"),
            P("c", dp),
            P("c", dp),
            P("c"),
            P(dp, None, "c"),
            P(dp, None, "c"),
        ),
        check_vma=False,
    )
```

time: 1030 us -> 777 us (0.75)
  waiting for transfers between devices: 408 us -> 222 us
  Pallas kernels: 249 us -> 333 us
  other arithmetic: 91.3 us -> 33.6 us
  blocking collectives: 42.2 us -> 0 us
  local copies, waits for them, and re-layouts: 93.4 us -> 56.4 us
    ppermute x8 -> x4, waiting for transfers between devices: 94.1 us -> 6.85 us  [shift(): return lax.ppermute(value, 'g', pairs)]
    pallas_call x13 -> x60, Pallas kernels: 249 us -> 333 us  [the longest x14 214 us: stepped(): return lambda *args: run(*args, *deps)]
    reduce_scatter x4, waiting for transfers between devices: 65.1 us -> 10 us  [over_groups(): return lax.psum_scatter(sums, 'g', scatter_dimension=0, tiled=True)]
    pmax x1 -> x0, blocking collectives: 42.2 us -> none  [local(): lax.pmax(jnp.where(spot, head_top[None, :], NEGATIVE).reshape(-1), ('g',...]
    unnamed x10 -> x8, waiting for transfers between devices: 21.5 us -> 0.13 us
    slice x33 -> x15, local copies, waits for them, and re-layouts: 27.6 us -> 6.54 us  [the longest x8 5.72 us: spread_next(): on_y, on_x = (from_x[:cut], from_y[cut:])]
    ppermute x26 -> x28, waiting for transfers between devices: 107 us -> 89 us  [over_x(): return lax.ppermute(value, 'x', SWAP)]
    ppermute x0 -> x6, starting transfers between devices: none -> 16.2 us  [the longest x3 10.5 us: max_over_groups(): lax.ppermute(value, 'g', [(i, (i + step) % groups) for i in range(groups)])]
  transfers between devices with their start and end apart: 86 -> 93, of which waited for: 44 -> 40; matrix products, arithmetic and copies ran while one was open for 16% -> 8% of each run, Pallas kernels for 20% -> 43%
where the time goes in v2:
time: 777 us; the launch traced here: 772 us
  Pallas kernels  333 us (43%)
  waiting for transfers between devices  222 us (29%)
  starting transfers between devices  108 us (14%)
  local copies, waits for them, and re-layouts  56.4 us (7%)
  other arithmetic  33.6 us (4%)
  between operations  18.8 us (2%)
    pallas_call x14, Pallas kernels, stepped(): return lambda *args: run(*args, *deps)  214 us
    ppermute x28, waiting for transfers between devices, over_x(): return lax.ppermute(value, 'x', SWAP)  89 us
    ppermute x28, waiting for transfers between devices, over_y(): return lax.ppermute(value, 'y', SWAP)  65.9 us
    pallas_call x23, Pallas kernels, sum_after(): pl.pallas_call(after(body, n, len(deps)), out_shape=jax.ShapeDtypeStruct(...  42.6 us
    ppermute x28, starting transfers between devices, over_y(): return lax.ppermute(value, 'y', SWAP)  29.3 us
    ppermute x28, starting transfers between devices, over_x(): return lax.ppermute(value, 'x', SWAP)  28 us
    unnamed x172, local copies, waits for them, and re-layouts  27.4 us
    ppermute x11, waiting for transfers between devices, over_core(): return lax.ppermute(value, 'c', SWAP)  24.8 us
  transfers between devices with their start and end apart: 93, of which 40 were waited for; matrix products, arithmetic and copies ran while one was open for 8% of the time, Pallas kernels for 43%

profile of v2, /device:TPU:0, one launch (start us, length us, event | category | flops | bytes accessed | tf_op | source)
XLA Modules:
  0.0 771.9 jit_solution(6930945885406200968)
XLA Ops:
  20.1 8.9 %collective-permute-done.10.refs_3_ = bf16[96,1152]{1,0:T(8,128)(2,1)S(1)} collective-permute-done((bf16[96,1152]{1,0:T(8,128)(2,1)}, bf16[96,1152]{1,0:T(8,128)(2,1)S(1)}, u32[]{:S(2)}, u32[]{:S(2)}) %collective-permute-start.10) | collective-permute-done | bytes 221216 | tf_op jit(solution)/shard_map/ppermute | solution.py:820
  79.9 14.2 %collective-permute-done.15.refs_2_ = bf16[96,3456]{1,0:T(8,128)(2,1)S(1)} collective-permute-done((bf16[96,3456]{1,0:T(8,128)(2,1)S(1)}, bf16[96,3456]{1,0:T(8,128)(2,1)S(1)}, u32[]{:S(2)}, u32[]{:S(2)}) %collective-permute-start.15) | collective-permute-done | bytes 663584 | tf_op jit(solution)/shard_map/ppermute | solution.py:816
  94.2 15.0 %collective-permute-done.16.refs_3_ = bf16[96,3456]{1,0:T(8,128)(2,1)S(1)} collective-permute-done((bf16[96,3456]{1,0:T(8,128)(2,1)S(1)}, bf16[96,3456]{1,0:T(8,128)(2,1)S(1)}, u32[]{:S(2)}, u32[]{:S(2)}) %collective-permute-start.16) | collective-permute-done | bytes 663584 | tf_op jit(solution)/shard_map/ppermute | solution.py:820
  115.4 16.1 %shard_map.269 = (bf16[2048,192]{1,0:T(8,128)(2,1)}, bf16[2048,384]{1,0:T(8,128)(2,1)}, bf16[1184,384]{1,0:T(8,128)(2,1)}, bf16[160,384]{1,0:T(8,128)(2,1)S(1)},...) custom-call(s32[22]{0:T(128)} %get-tuple-element.124.info.refs_0_, bf16[4,256,1536]{2,1,0:T(8,128)(2,1)} %copy-done, ...), custom_call_target="tpu_custom_call" | custom-call | flops 1150000000 | bytes 1000000 | tf_op jit(solution)/shard_map/pallas_call | solution.py:85
  142.0 14.5 %collective-permute-done.18.refs_4_ = bf16[256,1536]{1,0:T(8,128)(2,1)S(1)} collective-permute-done((bf16[256,1536]{1,0:T(8,128)(2,1)}, bf16[256,1536]{1,0:T(8,128)(2,1)S(1)}, u32[]{:S(2)}, u32[]{:S(2)}) %collective-permute-start.18) | collective-permute-done | bytes 786464 | tf_op jit(solution)/shard_map/ppermute | solution.py:820
  175.1 26.8 %shard_map.275 = (bf16[2048,192]{1,0:T(8,128)(2,1)}, f32[2048,192]{1,0:T(8,128)}, f32[8,8,256]{2,1,0:T(8,128)}, f32[8,256]{1,0:T(8,128)}) custom-call(s32[64]{0:T(128)} %get-tuple-element.125.refs_0_, s32[6]{0:T(128)} %refs_1_.3, bf16[2048,192]{1,0:T(8,128)(2,1)} %get-tuple-element.132.refs_1_.refs_2_, bf16[160,384]{1,0:T(8,128)(2,1)} %get-tuple-element.135.refs_3_.refs_5_, ...), custom_call_target="tpu_custom_call" | custom-call | flops 1150000000 | bytes 1000000 | tf_op jit(solution)/shard_map/pallas_call | solution.py:85
  212.9 8.4 %collective-permute-done.27 = bf16[128,1536]{1,0:T(8,128)(2,1)S(1)} collective-permute-done((bf16[128,1536]{1,0:T(8,128)(2,1)S(1)}, bf16[128,1536]{1,0:T(8,128)(2,1)S(1)}, u32[]{:S(2)}, u32[]{:S(2)}) %collective-permute-start.27) | collective-permute-done | bytes 393248 | tf_op jit(solution)/shard_map/ppermute | solution.py:816
  233.2 8.1 %collective-permute-done.24.refs_1_ = bf16[128,1536]{1,0:T(8,128)(2,1)S(1)} collective-permute-done((bf16[128,1536]{1,0:T(8,128)(2,1)}, bf16[128,1536]{1,0:T(8,128)(2,1)S(1)}, u32[]{:S(2)}, u32[]{:S(2)}) %collective-permute-start.24) | collective-permute-done | bytes 393248 | tf_op jit(solution)/shard_map/ppermute | solution.py:816
  241.3 15.3 %all-gather.9.cloned.1.call-done.refs_2_.refs_3_.refs_4_.refs_5_ = bf16[1536,1536]{1,0:T(8,128)(2,1)} async-done(((bf16[384,1536]{1,0:T(8,128)(2,1)}), bf16[1536,1536]{1,0:T(8,128)(2,1)}) %all-gather.9.cloned.1.call-update) | async-done | bytes 4718608 | tf_op jit(solution)/shard_map/all_gather | solution.py:1149
  287.9 16.4 %collective-permute-done.29 = bf16[256,1536]{1,0:T(8,128)(2,1)S(1)} collective-permute-done((bf16[256,1536]{1,0:T(8,128)(2,1)}, bf16[256,1536]{1,0:T(8,128)(2,1)S(1)}, u32[]{:S(2)}, u32[]{:S(2)}) %collective-permute-start.29) | collective-permute-done | bytes 786464 | tf_op jit(solution)/shard_map/ppermute | solution.py:816
  322.6 13.0 %shard_map.282 = (bf16[4,512,768]{2,1,0:T(8,128)(2,1)}, bf16[4,512,768]{2,1,0:T(8,128)(2,1)}) custom-call(s32[22]{0:T(128)} %get-tuple-element.124.info.refs_0_, bf16[4,256,1536]{2,1,0:T(8,128)(2,1)} %copy-done.2, bf16[4,256,1536]{2,1,0:T(8,128)(2,1)} %collective-permute-done.33.refs_2_, ...), custom_call_target="tpu_custom_call" | custom-call | flops 1150000000 | bytes 1000000 | tf_op jit(solution)/shard_map/pallas_call | solution.py:85
  335.6 12.8 %shard_map.283.refs_8_ = bf16[1536,1536]{1,0:T(8,128)(2,1)} custom-call(s32[22]{0:T(128)} %get-tuple-element.124.info.refs_0_, bf16[4,256,1536]{2,1,0:T(8,128)(2,1)} %pad_maximum_fusion.1.refs_1_, bf16[4,256,1536]{2,1,0:T(8,128)(2,1)} %collective-permute-done.28.refs_1_.refs_2_, bf16[4,512,768]{2,1,0:T(8,128)(2,1)} %get-tuple-element.154.refs_3_.refs_1_), custom_call_target="tpu_custom_call" | custom-call | flops 1150000000 | bytes 1000000 | tf_op jit(solution)/shard_map/pallas_call | solution.py:85
  355.1 20.0 %shard_map.284 = (bf16[4,256,1536]{2,1,0:T(8,128)(2,1)}, bf16[4,256,1536]{2,1,0:T(8,128)(2,1)}, bf16[4,512,768]{2,1,0:T(8,128)(2,1)}) custom-call(s32[22]{0:T(128)} %get-tuple-element.124.info.refs_0_, bf16[4,256,1536]{2,1,0:T(8,128)(2,1)} %pad_maximum_fusion.1.refs_1_, bf16[4,256,1536]{2,1,0:T(8,128)(2,1)} %collective-permute-done.28.refs_1_.refs_2_, ...), custom_call_target="tpu_custom_call" | custom-call | flops 1150000000 | bytes 1000000 | tf_op jit(solution)/shard_map/pallas_call | solution.py:85
  389.8 13.1 %shard_map.286.refs_2_ = bf16[1536,1536]{1,0:T(8,128)(2,1)} custom-call(s32[22]{0:T(128)} %get-tuple-element.124.info.refs_0_, bf16[4,256,1536]{2,1,0:T(8,128)(2,1)} %copy-done.2, bf16[4,256,1536]{2,1,0:T(8,128)(2,1)} %collective-permute-done.33.refs_2_, bf16[4,512,768]{2,1,0:T(8,128)(2,1)} %get-tuple-element.160.refs_3_, ...), custom_call_target="tpu_custom_call" | custom-call | flops 13799999488 | bytes 12000000 | tf_op jit(solution)/shard_map/pallas_call | solution.py:85
  412.5 11.2 %shard_map.289 = (bf16[4,256,1536]{2,1,0:T(8,128)(2,1)}, bf16[4,256,1536]{2,1,0:T(8,128)(2,1)}) custom-call(s32[22]{0:T(128)} %get-tuple-element.124.info.refs_0_, bf16[4,512,768]{2,1,0:T(8,128)(2,1)} %get-tuple-element.154.refs_3_.refs_1_, bf16[1536,1536]{1,0:T(8,128)(2,1)} %all-gather.11.cloned.1.call-done.refs_6_.refs_7_.refs_2_.refs_3_, ...), custom_call_target="tpu_custom_call" | custom-call | flops 11500000256 | bytes 10000000 | tf_op jit(solution)/shard_map/pallas_call | solution.py:85
  447.6 11.9 %collective-permute-done.45 = bf16[256,1536]{1,0:T(8,128)(2,1)S(1)} collective-permute-done((bf16[256,1536]{1,0:T(8,128)(2,1)S(1)}, bf16[256,1536]{1,0:T(8,128)(2,1)S(1)}, u32[]{:S(2)}, u32[]{:S(2)}) %collective-permute-start.45) | collective-permute-done | bytes 786464 | tf_op jit(solution)/shard_map/ppermute | solution.py:816
  477.1 9.7 %collective-permute-done.49.refs_2_ = bf16[4,256,1536]{2,1,0:T(8,128)(2,1)} collective-permute-done((bf16[4,256,1536]{2,1,0:T(8,128)(2,1)S(1)}, bf16[4,256,1536]{2,1,0:T(8,128)(2,1)}, u32[]{:S(2)}, u32[]{:S(2)}) %collective-permute-start.49) | collective-permute-done | bytes 3145760 | tf_op jit(solution)/shard_map/ppermute | solution.py:824
  499.1 38.7 %shard_map.296 = (bf16[2048,192]{1,0:T(8,128)(2,1)}, bf16[160,384]{1,0:T(8,128)(2,1)S(1)}, bf16[1184,384]{1,0:T(8,128)(2,1)}, f32[2048,384]{1,0:T(8,128)}, bf16[...) custom-call(s32[64]{0:T(128)} %get-tuple-element.125.refs_0_, s32[6]{0:T(128)} %refs_1_.3, ...), custom_call_target="tpu_custom_call" | custom-call | flops 1150000000 | bytes 1000000 | tf_op jit(solution)/shard_map/pallas_call | solution.py:85
  544.3 12.2 %collective-permute-start.57 = (bf16[1184,384]{1,0:T(8,128)(2,1)}, bf16[1184,384]{1,0:T(8,128)(2,1)}, u32[]{:S(2)}, u32[]{:S(2)}) collective-permute-start(bf16[1184,384]{1,0:T(8,128)(2,1)} %get-tuple-element.180), channel_id=1, source_target_pairs={{0,8},{8,16},{16,24},{1,9},{9,17},{17,25},{2,10},{10,18},{18,26},{... | collective-permute-start | bytes 2727944 | tf_op jit(solution)/shard_map/ppermute | solution.py:796
  556.5 8.6 %shard_map.297.refs_2_.refs_8_.refs_0_ = bf16[1536,384]{1,0:T(8,128)(2,1)} custom-call(s32[22]{0:T(128)} %get-tuple-element.124.info.refs_0_, bf16[4,256,1536]{2,1,0:T(8,128)(2,1)} %copy-done.1, bf16[4,256,1536]{2,1,0:T(8,128)(2,1)} %collective-permute-done.49.refs_2_, bf16[2048,192]{1,0:T(8,128)(2,1)} %get-tuple-element.144.refs_1_.refs_3_, ...), custom_call_target="tpu_custom_call" | custom-call | flops 5257142784 | bytes 4571428 | tf_op jit(solution)/shard_map/pallas_call | solution.py:85
  600.3 15.0 %shard_map.303.refs_3_ = bf16[1536,1152]{1,0:T(8,128)(2,1)} custom-call(s32[22]{0:T(128)} %get-tuple-element.124.info.refs_0_, bf16[4,256,1536]{2,1,0:T(8,128)(2,1)} %copy-done, bf16[4,256,1536]{2,1,0:T(8,128)(2,1)} %collective-permute-done.8.refs_2_, bf16[2048,576]{1,0:T(8,128)(2,1)} %shard_map.302.refs_3_.refs_1_), custom_call_target="tpu_custom_call" | custom-call | flops 15771428864 | bytes 13714285 | tf_op jit(solution)/shard_map/pallas_call | solution.py:85
  615.3 13.6 %shard_map.304 = (bf16[4,256,1536]{2,1,0:T(8,128)(2,1)}, bf16[4,256,1536]{2,1,0:T(8,128)(2,1)}) custom-call(s32[22]{0:T(128)} %get-tuple-element.124.info.refs_0_, bf16[2048,576]{1,0:T(8,128)(2,1)} %shard_map.302.refs_3_.refs_1_, bf16[1536,1152]{1,0:T(8,128)(2,1)} %all-gather.5.cloned.1.call-done.refs_3_.refs_2_, bf16[1536,1152]{1,0:T(8,128)(2,1)} %shard_map.303.refs_3_), custom_call_target="tpu_custom_call" | custom-call | flops 11500000256 | bytes 10000000 | tf_op jit(solution)/shard_map/pallas_call | solution.py:85
  676.8 10.0 %reduce-scatter.9.cloned.1.call-done = bf16[384,1152]{1,0:T(8,128)(2,1)} async-done(((bf16[1536,1152]{1,0:T(8,128)(2,1)}), bf16[384,1152]{1,0:T(8,128)(2,1)}) %reduce-scatter.9.cloned.1.call-update) | async-done | bytes 884752 | tf_op jit(solution)/shard_map/reduce_scatter | solution.py:832
  691.6 9.3 %shard_map.316 = (f32[256,1536]{1,0:T(8,128)}, f32[10,6,1536]{2,1,0:T(8,128)}) custom-call(s32[22]{0:T(128)} %get-tuple-element.124.info.refs_0_, f32[256,1536]{1,0:T(8,128)} %shard_map.310.refs_2_.refs_1_, f32[256,1536]{1,0:T(8,128)} %get-tuple-element.266.refs_2_, f32[256,1536]{1,0:T(8,128)} %shard_map.280.refs_3_, f32[256,1536]{1,0:T(8,128)} %shard_map.291.refs_4_, ...), custom_call_target="tpu_custom_call" | custom-call | flops 9200000000 | bytes 8000000 | tf_op jit(solution)/shard_map/pallas_call | solution.py:85
  (485 shorter events, 412.8 us)
Async XLA Ops:
  7.2 108.2 %all-gather.5.cloned.1.call-start = ((), (), s32[]{:S(2)}) async-start(), calls=%async_computation.4 | async-start | bytes 4423680 | tf_op jit(solution)/shard_map/all_gather | solution.py:1116
  33.2 138.4 %all-gather.7.cloned.1.call-start = ((), (), s32[]{:S(2)}) async-start(), calls=%async_computation.5 | async-start | bytes 1474560 | tf_op jit(solution)/shard_map/all_gather | solution.py:1132
  76.3 39.1 %collective-permute-start.8 = (bf16[4,256,1536]{2,1,0:T(8,128)(2,1)S(1)}, bf16[4,256,1536]{2,1,0:T(8,128)(2,1)}, u32[]{:S(2)}, u32[]{:S(2)}) collective-permute-start(bf16[4,256,1536]{2,1,0:T(8,128)(2,1)S(1)} %pad_maximum_fusion.refs_1_), channel_id=1, source_target_pairs={{0,1},{1,0},{2,3},{3,2},{4,5},{5,4},{6,7},{7,6},{8,9},{9,8},{10,11... | collective-permute-start | bytes 9437192 | tf_op jit(solution)/shard_map/ppermute | solution.py:824
  78.4 31.5 %collective-permute-start.17 = (bf16[96,3456]{1,0:T(8,128)(2,1)S(1)}, bf16[96,3456]{1,0:T(8,128)(2,1)}, u32[]{:S(2)}, u32[]{:S(2)}) collective-permute-start(bf16[96,3456]{1,0:T(8,128)(2,1)S(1)} %copy-done.40), channel_id=1, source_target_pairs={{0,6},{2,4},{4,2},{6,0},{1,7},{3,5},{5,3},{7,1},{8,14},{10,12},{12... | collective-permute-start | bytes 1990664 | tf_op jit(solution)/shard_map/ppermute | solution.py:828
  115.1 141.5 %all-gather.9.cloned.1.call-start = ((), (), s32[]{:S(2)}) async-start(), calls=%async_computation.6 | async-start | bytes 5898240 | tf_op jit(solution)/shard_map/all_gather | solution.py:1149
  166.7 188.4 %all-gather.11.cloned.1.call-start = ((), (), s32[]{:S(2)}) async-start(), calls=%async_computation.7 | async-start | bytes 5898240 | tf_op jit(solution)/shard_map/all_gather | solution.py:1133
  224.5 59.2 %collective-permute-start.28 = (bf16[4,256,1536]{2,1,0:T(8,128)(2,1)}, bf16[4,256,1536]{2,1,0:T(8,128)(2,1)}, u32[]{:S(2)}, u32[]{:S(2)}) collective-permute-start(bf16[4,256,1536]{2,1,0:T(8,128)(2,1)} %pad_maximum_fusion.1.refs_1_), channel_id=1, source_target_pairs={{0,1},{1,0},{2,3},{3,2},{4,5},{5,4},{6,7},{7,6},{8,9},{9,8},{10,11... | collective-permute-start | bytes 9437192 | tf_op jit(solution)/shard_map/ppermute | solution.py:824
  231.2 40.9 %collective-permute-start.20 = (bf16[128,1536]{1,0:T(8,128)(2,1)}, bf16[128,1536]{1,0:T(8,128)(2,1)S(1)}, u32[]{:S(2)}, u32[]{:S(2)}) collective-permute-start(bf16[128,1536]{1,0:T(8,128)(2,1)} %get-tuple-element.148), channel_id=1, source_target_pairs={{0,2},{2,0},{1,3},{3,1},{4,6},{6,4},{5,7},{7,5},{8,10},{10,8},{9,1... | collective-permute-start | bytes 1179656 | tf_op jit(solution)/shard_map/ppermute | solution.py:816
  232.7 39.5 %collective-permute-start.21 = (bf16[128,1536]{1,0:T(8,128)(2,1)}, bf16[128,1536]{1,0:T(8,128)(2,1)S(1)}, u32[]{:S(2)}, u32[]{:S(2)}) collective-permute-start(bf16[128,1536]{1,0:T(8,128)(2,1)} %get-tuple-element.149), channel_id=1, source_target_pairs={{0,4},{4,0},{1,5},{5,1},{2,6},{6,2},{3,7},{7,3},{8,12},{12,8},{9,1... | collective-permute-start | bytes 1179656 | tf_op jit(solution)/shard_map/ppermute | solution.py:820
  268.9 192.5 %reduce-scatter.5.cloned.1.call-start = ((), (), s32[]{:S(2)}) async-start(), calls=%async_computation.8 | async-start | bytes 5898240 | tf_op jit(solution)/shard_map/reduce_scatter | solution.py:832
  348.5 244.8 %reduce-scatter.7.cloned.1.call-start = ((), (), s32[]{:S(2)}) async-start(), calls=%async_computation.9 | async-start | bytes 5898240 | tf_op jit(solution)/shard_map/reduce_scatter | solution.py:832
  388.7 49.2 %collective-permute-start.38 = (bf16[128,1536]{1,0:T(8,128)(2,1)}, bf16[128,1536]{1,0:T(8,128)(2,1)S(1)}, u32[]{:S(2)}, u32[]{:S(2)}) collective-permute-start(bf16[128,1536]{1,0:T(8,128)(2,1)} %get-tuple-element.163.refs_7_), channel_id=1, source_target_pairs={{0,2},{2,0},{1,3},{3,1},{4,6},{6,4},{5,7},{7,5},{8,10},{10,8},{9,1... | collective-permute-start | bytes 1179656 | tf_op jit(solution)/shard_map/ppermute | solution.py:816
  389.3 48.7 %collective-permute-start.39 = (bf16[128,1536]{1,0:T(8,128)(2,1)}, bf16[128,1536]{1,0:T(8,128)(2,1)}, u32[]{:S(2)}, u32[]{:S(2)}) collective-permute-start(bf16[128,1536]{1,0:T(8,128)(2,1)} %get-tuple-element.165.refs_10_), channel_id=1, source_target_pairs={{0,4},{4,0},{1,5},{5,1},{2,6},{6,2},{3,7},{7,3},{8,12},{12,8},{9,1... | collective-permute-start | bytes 1179656 | tf_op jit(solution)/shard_map/ppermute | solution.py:820
  402.9 272.2 %reduce-scatter.11.cloned.1.call-start = ((), (), s32[]{:S(2)}) async-start(), calls=%async_computation.11 | async-start | bytes 1474560 | tf_op jit(solution)/shard_map/reduce_scatter | solution.py:832
  405.7 32.2 %collective-permute-start.41 = (bf16[128,1536]{1,0:T(8,128)(2,1)}, bf16[128,1536]{1,0:T(8,128)(2,1)S(1)}, u32[]{:S(2)}, u32[]{:S(2)}) collective-permute-start(bf16[128,1536]{1,0:T(8,128)(2,1)} %shard_map.288.refs_5_.refs_2_), channel_id=1, source_target_pairs={{0,4},{4,0},{1,5},{5,1},{2,6},{6,2},{3,7},{7,3},{8,12},{12,8},{9,1... | collective-permute-start | bytes 1179656 | tf_op jit(solution)/shard_map/ppermute | solution.py:820
  537.8 36.8 %collective-permute-start.56 = (bf16[1184,384]{1,0:T(8,128)(2,1)}, bf16[1184,384]{1,0:T(8,128)(2,1)S(1)}, u32[]{:S(2)}, u32[]{:S(2)}) collective-permute-start(bf16[1184,384]{1,0:T(8,128)(2,1)} %get-tuple-element.179), channel_id=1, source_target_pairs={{8,0},{16,8},{24,16},{9,1},{17,9},{25,17},{10,2},{18,10},{26,18},{... | collective-permute-start | bytes 2727944 | tf_op jit(solution)/shard_map/ppermute | solution.py:796
  540.4 31.5 %collective-permute-start.58 = (f32[1,12]{1,0:T(1,128)}, f32[1,12]{1,0:T(1,128)S(1)}, u32[]{:S(2)}, u32[]{:S(2)}) collective-permute-start(f32[1,12]{1,0:T(1,128)} %shard_map.301), channel_id=1, source_target_pairs={{0,2},{2,0},{1,3},{3,1},{4,6},{6,4},{5,7},{7,5},{8,10},{10,8},{9,1... | collective-permute-start | bytes 152 | tf_op jit(solution)/shard_map/ppermute | solution.py:816
  544.3 32.2 %collective-permute-start.57 = (bf16[1184,384]{1,0:T(8,128)(2,1)}, bf16[1184,384]{1,0:T(8,128)(2,1)}, u32[]{:S(2)}, u32[]{:S(2)}) collective-permute-start(bf16[1184,384]{1,0:T(8,128)(2,1)} %get-tuple-element.180), channel_id=1, source_target_pairs={{0,8},{8,16},{16,24},{1,9},{9,17},{17,25},{2,10},{10,18},{18,26},{... | collective-permute-start | bytes 2727944 | tf_op jit(solution)/shard_map/ppermute | solution.py:796
  578.9 108.0 %reduce-scatter.9.cloned.1.call-start = ((), (), s32[]{:S(2)}) async-start(), calls=%async_computation.10 | async-start | bytes 4423680 | tf_op jit(solution)/shard_map/reduce_scatter | solution.py:832
  666.4 35.7 %collective-permute-start.87 = (bf16[96,1536]{1,0:T(8,128)(2,1)}, bf16[96,1536]{1,0:T(8,128)(2,1)S(1)}, u32[]{:S(2)}, u32[]{:S(2)}) collective-permute-start(bf16[96,1536]{1,0:T(8,128)(2,1)} %get-tuple-element.217), channel_id=1, source_target_pairs={{0,4},{4,0},{1,5},{5,1},{2,6},{6,2},{3,7},{7,3},{8,12},{12,8},{9,1... | collective-permute-start | bytes 884744 | tf_op jit(solution)/shard_map/ppermute | solution.py:820
  667.0 35.2 %collective-permute-start.88 = (bf16[96,1536]{1,0:T(8,128)(2,1)S(1)}, bf16[96,1536]{1,0:T(8,128)(2,1)S(1)}, u32[]{:S(2)}, u32[]{:S(2)}) collective-permute-start(bf16[96,1536]{1,0:T(8,128)(2,1)S(1)} %copy-done.62), channel_id=1, source_target_pairs={{0,6},{2,4},{4,2},{6,0},{1,7},{3,5},{5,3},{7,1},{8,14},{10,12},{12... | collective-permute-start | bytes 884744 | tf_op jit(solution)/shard_map/ppermute | solution.py:828
  670.0 41.5 %collective-permute-start.83 = (bf16[96,1536]{1,0:T(8,128)(2,1)}, bf16[96,1536]{1,0:T(8,128)(2,1)}, u32[]{:S(2)}, u32[]{:S(2)}) collective-permute-start(bf16[96,1536]{1,0:T(8,128)(2,1)} %get-tuple-element.211), channel_id=1, source_target_pairs={{0,2},{2,0},{1,3},{3,1},{4,6},{6,4},{5,7},{7,5},{8,10},{10,8},{9,1... | collective-permute-start | bytes 884744 | tf_op jit(solution)/shard_map/ppermute | solution.py:816
  670.6 40.8 %collective-permute-start.84 = (bf16[96,1536]{1,0:T(8,128)(2,1)}, bf16[96,1536]{1,0:T(8,128)(2,1)}, u32[]{:S(2)}, u32[]{:S(2)}) collective-permute-start(bf16[96,1536]{1,0:T(8,128)(2,1)} %get-tuple-element.212), channel_id=1, source_target_pairs={{0,4},{4,0},{1,5},{5,1},{2,6},{6,2},{3,7},{7,3},{8,12},{12,8},{9,1... | collective-permute-start | bytes 884744 | tf_op jit(solution)/shard_map/ppermute | solution.py:820
  718.5 42.1 %collective-permute-start.69 = (f32[256,1536]{1,0:T(8,128)S(1)}, f32[256,1536]{1,0:T(8,128)}, u32[]{:S(2)}, u32[]{:S(2)}) collective-permute-start(f32[256,1536]{1,0:T(8,128)S(1)} %copy-done.16), channel_id=1, source_target_pairs={{0,1},{1,0},{2,3},{3,2},{4,5},{5,4},{6,7},{7,6},{8,9},{9,8},{10,11... | collective-permute-start | bytes 4718600 | tf_op jit(solution)/shard_map/ppermute | solution.py:824
  (154 other events, 1401.9 us)
Sparse Core Ops, SparseCore 0:
  33.3 71.4 all-gather.4
  115.2 33.8 all-gather.6
  166.8 89.7 all-gather.8
  269.0 86.0 all-gather.10
  357.3 83.7 reduce-scatter.4
  443.2 85.6 reduce-scatter.6
  579.0 34.5 reduce-scatter.10
  615.9 70.9 reduce-scatter.8

commit v3 on v2

--- a/solution.py
+++ b/solution.py
@@ -32,7 +32,7 @@
 ANY = pl.BlockSpec(memory_space=pl.ANY)
 
 COUNT, OFFSET, TEXT_FROM, TEXT_TO = 0, 4, 8, 12
-CORE, TAIL_FROM, EDGE_FROM, OWN_FROM, OWN_SEQ, NEXT_FROM, INFO = 16, 17, 18, 19, 20, 21, 22
+CORE, TAIL_FROM, EDGE_FROM, OWN_FROM, OWN_SEQ, NEXT_FROM, HALF, INFO = 16, 17, 18, 19, 20, 21, 22, 23
 
 
 def dot(a, b):
@@ -152,6 +152,7 @@
     info[TAIL_FROM] = jnp.maximum(stop - start - TAIL, 0)
     info[EDGE_FROM] = jnp.maximum(stop - start - EDGE, 0)
     info[OWN_FROM] = own
+    info[HALF] = group_rows // (2 * BLOCKS)
     info[OWN_SEQ] = seq_of(own, 0)
     info[NEXT_FROM] = seq[seq_of(own, 0) + 1]
 
@@ -204,75 +205,114 @@
     return low, high
 
 
-def enter_kernel(info, tokens, cotangent, image_mod, text_mod, modulated, grad_mlp):
-    half = modulated.shape[0]
-    n_seq = image_mod.shape[0]
-    place = pl.ds(pl.multiple_of(info[CORE] * half, half), half)
-    s = info[OWN_SEQ]
-    after_s = jnp.minimum(s + 1, n_seq - 1)
-    ids = row_ids(info[CORE] * half, half)
+def own_kinds(info, first, rows):
+    ids = row_ids(info[CORE] * info[HALF] + first, rows)
     live = ids < info[COUNT]
     is_text = live & (ids >= info[TEXT_FROM]) & (ids < info[TEXT_TO])
     is_next = live & (info[OWN_FROM] + ids >= info[NEXT_FROM])
+    return live, live & jnp.logical_not(is_text | is_next), is_next, is_text
+
+
+def vector_of(info, image_mod, text_mod, is_next, is_text):
+    s = info[OWN_SEQ]
+    after_s = jnp.minimum(s + 1, image_mod.shape[0] - 1)
 
     def pick(i):
-        row = pl.ds(i, 1)
         own, text, following = image_mod[s][i : i + 1], text_mod[s][i : i + 1], image_mod[after_s][i : i + 1]
         return jnp.where(is_text, text, jnp.where(is_next, following, own))
 
-    rows = tokens[place, :].astype(F32)
+    return pick
+
+
+def normal(rows):
     centered = rows - jnp.mean(rows, axis=1, keepdims=True)
-    normed = centered * lax.rsqrt(jnp.mean(centered * centered, axis=1, keepdims=True) + EPSILON)
+    inverse = lax.rsqrt(jnp.mean(centered * centered, axis=1, keepdims=True) + EPSILON)
+    return centered * inverse, inverse
+
+
+def normal_back(grad, normed, inverse):
+    return inverse * (
+        grad - jnp.mean(grad, axis=1, keepdims=True) - normed * jnp.mean(grad * normed, axis=1, keepdims=True)
+    )
+
+
+def enter_kernel(info, tokens, cotangent, image_mod, text_mod, modulated, grad_mlp):
+    half = modulated.shape[0]
+    place = pl.ds(pl.multiple_of(info[CORE] * half, half), half)
+    live, _, is_next, is_text = own_kinds(info, 0, half)
+    pick = vector_of(info, image_mod, text_mod, is_next, is_text)
+    normed, _ = normal(tokens[place, :].astype(F32))
     modulated[...] = (normed * (1.0 + pick(1)) + pick(0)).astype(BF)
     grad_mlp[...] = (pick(5) * jnp.where(live, cotangent[place, :].astype(F32), 0.0)).astype(BF)
 
 
+def collected(mine, first_x, first_y, last_x, last_y, out):
+    cut = out.shape[0] // 2
+    out[:cut, :] = mine[:cut, :].astype(F32) + first_x[...].astype(F32) + last_y[...].astype(F32)
+    out[cut:, :] = mine[cut:, :].astype(F32) + last_x[...].astype(F32) + first_y[...].astype(F32)
+
+
+def middle_kernel(
+    info, mine, first_x, first_y, last_x, last_y, tokens, image_mod, text_mod, branch, modulated_mlp
+):
+    collected(mine, first_x, first_y, last_x, last_y, branch)
+    _, _, is_next, is_text = own_kinds(info, 0, branch.shape[0])
+    pick = vector_of(info, image_mod, text_mod, is_next, is_text)
+    normed, _ = normal(tokens[...].astype(F32) + pick(2) * branch[...])
+    modulated_mlp[...] = (normed * (1.0 + pick(4)) + pick(3)).astype(BF)
+
+
+def turn_kernel(
+    info, mine, first_x, first_y, last_x, last_y, branch, tokens, cotangent, image_mod, text_mod,
+    grad_mod_mlp, grad_first, grad_branch,
+):
+    collected(mine, first_x, first_y, last_x, last_y, grad_mod_mlp)
+    live, _, is_next, is_text = own_kinds(info, 0, branch.shape[0])
+    pick = vector_of(info, image_mod, text_mod, is_next, is_text)
+    normed, inverse = normal(tokens[...].astype(F32) + pick(2) * branch[...])
+    back = normal_back(grad_mod_mlp[...] * (1.0 + pick(4)), normed, inverse)
+    result = jnp.where(live, cotangent[...].astype(F32) + back, 0.0)
+    grad_first[...] = result
+    grad_branch[...] = (pick(2) * result).astype(BF)
+
+
 def leave_kernel(
-    info, grad_modulated, grad_first, branch, grad_mod_mlp, mlp_branch, tokens, cotangent, image_mod, text_mod,
-    tokens_grad, sums,
+    info, mine, first_x, first_y, last_x, last_y,
+    mlp_mine, mlp_first_x, mlp_first_y, mlp_last_x, mlp_last_y,
+    grad_first, branch, grad_mod_mlp, tokens, cotangent, image_mod, text_mod,
+    tokens_grad, mixed, sums, grad_modulated, mlp_branch,
 ):
-    step = tokens_grad.shape[0]
-    half = step * pl.num_programs(0)
+    collected(mine, first_x, first_y, last_x, last_y, grad_modulated)
+    collected(mlp_mine, mlp_first_x, mlp_first_y, mlp_last_x, mlp_last_y, mlp_branch)
+    sums[...] = jnp.zeros_like(sums)
     n_seq = image_mod.shape[0]
     s = info[OWN_SEQ]
     after_s = jnp.minimum(s + 1, n_seq - 1)
-    ids = row_ids(info[CORE] * half + pl.program_id(0) * step, step)
-    live = ids < info[COUNT]
-    is_text = live & (ids >= info[TEXT_FROM]) & (ids < info[TEXT_TO])
-    is_next = live & (info[OWN_FROM] + ids >= info[NEXT_FROM])
-    is_own = live & jnp.logical_not(is_text | is_next)
-
-    def pick(i):
-        own, text, following = image_mod[s][i : i + 1], text_mod[s][i : i + 1], image_mod[after_s][i : i + 1]
-        return jnp.where(is_text, text, jnp.where(is_next, following, own))
-
-    def normal(rows):
-        centered = rows - jnp.mean(rows, axis=1, keepdims=True)
-        inverse = lax.rsqrt(jnp.mean(centered * centered, axis=1, keepdims=True) + EPSILON)
-        return centered * inverse, inverse
-
-    rows = tokens[...].astype(F32)
-    normed, inverse = normal(rows)
-    normed_mlp, _ = normal(rows + pick(2) * branch[...])
-
-    @pl.when(pl.program_id(0) == 0)
-    def _():
-        sums[...] = jnp.zeros_like(sums)
-
-    def add(i, term):
-        for kept_rows, at in ((is_own, s), (is_next, after_s), (is_text, n_seq + s)):
-            row = jnp.sum(jnp.where(kept_rows, term, 0.0), axis=0, keepdims=True)
-            sums[at, i : i + 1, :] += row
-
-    add(0, grad_modulated[...])
-    add(1, grad_modulated[...] * normed)
-    add(2, grad_first[...] * branch[...])
-    add(3, grad_mod_mlp[...])
-    add(4, grad_mod_mlp[...] * normed_mlp)
-    add(5, cotangent[...].astype(F32) * mlp_branch[...])
-    h = grad_modulated[...] * (1.0 + pick(1))
-    back = h - jnp.mean(h, axis=1, keepdims=True) - normed * jnp.mean(h * normed, axis=1, keepdims=True)
-    tokens_grad[...] = jnp.where(live, grad_first[...] + inverse * back, 0.0)
+    step = 64
+    for low in range(0, tokens_grad.shape[0], step):
+        part = slice(low, low + step)
+        live, is_own, is_next, is_text = own_kinds(info, low, step)
+        pick = vector_of(info, image_mod, text_mod, is_next, is_text)
+        rows = tokens[part, :].astype(F32)
+        normed, inverse = normal(rows)
+        first = rows + pick(2) * branch[part, :]
+        normed_mlp, _ = normal(first)
+
+        def add(i, term):
+            for kept_rows, at in ((is_own, s), (is_next, after_s), (is_text, n_seq + s)):
+                row = jnp.sum(jnp.where(kept_rows, term, 0.0), axis=0, keepdims=True)
+                sums[at, i : i + 1, :] += row
+
+        grads = grad_modulated[part, :]
+        add(0, grads)
+        add(1, grads * normed)
+        add(2, grad_first[part, :] * branch[part, :])
+        add(3, grad_mod_mlp[part, :])
+        add(4, grad_mod_mlp[part, :] * normed_mlp)
+        add(5, cotangent[part, :].astype(F32) * mlp_branch[part, :])
+        back = normal_back(grads * (1.0 + pick(1)), normed, inverse)
+        tokens_grad[part, :] = jnp.where(live, grad_first[part, :] + back, 0.0)
+        mixed[part, :] = jnp.where(live, first + pick(5) * mlp_branch[part, :], 0.0).astype(BF)
 
 
 def row_ids(base, rows):
@@ -800,18 +840,6 @@
     return lax.cond(predicate, run, lambda *v: tuple(jnp.zeros_like(a) for a in v), *values)
 
 
-def max_over_groups(value):
-    groups = lax.axis_size("g")
-    top = value
-    for step in range(1, groups):
-        top = jnp.maximum(top, lax.ppermute(value, "g", [(i, (i + step) % groups) for i in range(groups)]))
-    return top
-
-
-def max_over_plane(value):
-    return jnp.maximum(jnp.maximum(value, over_x(value)), jnp.maximum(over_y(value), over_xy(value)))
-
-
 def over_x(value):
     return lax.ppermute(value, "x", SWAP)
 
@@ -845,8 +873,10 @@
     return value, from_x, from_y, on_y, on_x, over_y(on_y), over_x(on_x)
 
 
-def spread_end(state):
+def spread_end(state, deps=()):
     value, from_x, from_y, _, _, low, high = state
+    if deps:
+        low, high = sum_after([low], BF, deps), sum_after([high], BF, deps)
     own = jnp.stack([value, from_x, from_y, jnp.concatenate([low, high], axis=0)])
     return own, over_core(own)
 
@@ -862,7 +892,7 @@
     return total
 
 
-def core_sum(own, oth, deps=()):
+def core_sum(own, oth, deps=(), time=3):
     other = over_core(oth)
     half, width = own.shape[1:]
     cut = half // 2
@@ -878,7 +908,7 @@
         in_specs=[VMEM] * 2 + [ANY] * len(deps),
         out_specs=(VMEM,) * len(cuts),
         compiler_params=pltpu.CompilerParams(vmem_limit_bytes=VMEM_LIMIT),
-        cost_estimate=took_us(3),
+        cost_estimate=took_us(time),
     )(own, other, *deps)
 
 
@@ -888,61 +918,26 @@
     return mine, x_high, y_low, from_x, from_y, over_x(x_low), over_y(y_high)
 
 
-def collect_next(begun, deps=()):
+def collect_next(begun, deps=(), time=1):
     mine, x_high, y_low, from_x, from_y, first_x, first_y = begun
-    on_x, on_y = sum_after((x_high, from_y), BF, deps), sum_after((y_low, from_x), BF, deps)
+    on_x, on_y = sum_after((x_high, from_y), BF, deps, time), sum_after((y_low, from_x), BF, deps, time)
     return mine, first_x, first_y, on_x, on_y, over_x(on_x), over_y(on_y)
 
 
-def collect_end(state, deps=()):
-    own, first_x, first_y, _, _, last_x, last_y = state
-    cut = own.shape[0] // 2
-    n = 5
-
-    def body(mine, first_x, first_y, last_x, last_y, out):
-        out[:cut, :] = mine[:cut, :].astype(F32) + first_x[...].astype(F32) + last_y[...].astype(F32)
-        out[cut:, :] = mine[cut:, :].astype(F32) + last_x[...].astype(F32) + first_y[...].astype(F32)
-
-    return pl.pallas_call(
-        after(body, n, len(deps)),
-        out_shape=jax.ShapeDtypeStruct(own.shape, F32),
-        in_specs=[VMEM] * n + [ANY] * len(deps),
-        out_specs=VMEM,
-        compiler_params=pltpu.CompilerParams(vmem_limit_bytes=VMEM_LIMIT),
-        cost_estimate=took_us(2),
-    )(own, first_x, first_y, last_x, last_y, *deps)
-
-
-def sums_of_shares(shares, g, q, deps):
+def sums_of_shares(shares, top_rows, g, q, deps):
     groups = lax.axis_size("g")
     pick = lambda values, at: lax.dynamic_index_in_dim(values, at, 0, keepdims=False)
+    is_top = (jnp.arange(shares.shape[1]) >= shares.shape[1] - top_rows)[:, None]
+    join = lambda a, b: jnp.where(is_top, jnp.maximum(a, b), a + b)
     shares = jnp.moveaxis(shares.reshape((groups, BLOCKS) + shares.shape[1:]), 1, 0)
-    shares = (
-        pick(shares, q)
-        + over_x(pick(shares, q ^ 1))
-        + over_y(pick(shares, q ^ 2))
-        + over_xy(pick(shares, q ^ 3))
-    )
+    got = [over_x(pick(shares, q ^ 1)), over_y(pick(shares, q ^ 2)), over_xy(pick(shares, q ^ 3))]
+    shares = join(join(pick(shares, q), got[0]), join(got[1], got[2]))
     shares = sum_after([shares], F32, deps)
     total = pick(shares, g)
     for step in range(1, groups):
         pairs = [(i, (i + step) % groups) for i in range(groups)]
-        total = total + lax.ppermute(pick(shares, lax.rem(g + step, groups)), "g", pairs)
+        total = join(total, lax.ppermute(pick(shares, lax.rem(g + step, groups)), "g", pairs))
     return total
-
-
-def layer_norm(inputs):
-    centered = inputs - jnp.mean(inputs, axis=1, keepdims=True)
-    inverse_std = lax.rsqrt(jnp.mean(centered * centered, axis=1, keepdims=True) + EPSILON)
-    return (centered * inverse_std, inverse_std)
-
-
-def norm_back(grad_normed, normed, inverse_std):
-    return inverse_std * (
-        grad_normed
-        - jnp.mean(grad_normed, axis=1, keepdims=True)
-        - normed * jnp.mean(grad_normed * normed, axis=1, keepdims=True)
-    )
 
 
 def pick_pieces(pieces, place, deps=()):
@@ -971,7 +966,7 @@
     return swap_pieces(pick_pieces(pieces, place))
 
 
-def arrange(got, place, body, out_shape, deps=()):
+def arrange(got, place, body, out_shape, deps=(), time=2):
     n = len(got)
 
     def kernel(place_ref, *refs):
@@ -984,13 +979,16 @@
         in_specs=[SMEM] + [VMEM] * n + [ANY] * len(deps),
         out_specs=(VMEM,) * len(out_shape),
         compiler_params=pltpu.CompilerParams(vmem_limit_bytes=VMEM_LIMIT),
-        cost_estimate=took_us(2),
+        cost_estimate=took_us(time),
     )(place, *got, *deps)
 
 
 def stack_rows(b, piece, outs):
-    rows = piece.shape[0]
-    outs[0][pl.ds(pl.multiple_of(b * rows, ALIGN), rows), :] = piece[...]
+    rows, at = piece.shape[0], 0
+    for out in outs:
+        n = out.shape[1]
+        out[pl.ds(pl.multiple_of(b * rows, ALIGN), rows), :] = piece[:, at : at + n]
+        at += n
 
 
 def give_wide(b, piece, outs):
@@ -999,12 +997,6 @@
         out[:, pl.ds(pl.multiple_of(b * n, SUB), n)] = piece[:, k * n : (k + 1) * n].astype(F32)
 
 
-def give_turned(b, piece, outs):
-    n = piece.shape[1] // 2
-    for k, out in enumerate(outs):
-        out[pl.ds(pl.multiple_of(b * n, ALIGN), n), :] = piece[:, k * n : (k + 1) * n].astype(F32).T
-
-
 def give_qkv(b, piece, outs):
     n = piece.shape[1] // 6
     for at in range(BLOCKS):
@@ -1013,8 +1005,17 @@
         def _():
             for k, out in enumerate(outs):
                 for p in range(3):
-                    part = piece[:, (3 * k + p) * n : (3 * k + p + 1) * n].astype(F32)
-                    out[:, p, at * n : (at + 1) * n] = part
+                    out[p, :, at * n : (at + 1) * n] = piece[:, (3 * k + p) * n : (3 * k + p + 1) * n].astype(F32)
+
+
+def give_narrow(b, piece, outs):
+    n = piece.shape[1] // 2
+    for at in range(BLOCKS):
+
+        @pl.when(b == at)
+        def _():
+            for k, out in enumerate(outs):
+                out[:, at * n : (at + 1) * n] = piece[:, k * n : (k + 1) * n].astype(F32)
 
 
 def local(
@@ -1062,7 +1063,7 @@
 
     pack_qkv = jnp.concatenate([quarter(image_qkv), quarter(text_qkv)], axis=2)
     place = jnp.stack([g, q, c]).astype(jnp.int32)
-    plane_of = lambda n: (jax.ShapeDtypeStruct((BLOCKS * share, n), BF),)
+    plane_of = lambda *cuts: tuple(jax.ShapeDtypeStruct((BLOCKS * share, n), BF) for n in cuts)
     (plane_qkv,) = arrange(exchange(pack_qkv, place), place, stack_rows, plane_of(6 * mine))
 
     n_tiles = group_rows // CHUNK
@@ -1080,31 +1081,21 @@
     )(seq_offsets, block_offsets, place)
 
     my_rows = lambda inputs: lax.dynamic_slice_in_dim(inputs, c * half, half, 0)
-    ids = c * half + jnp.arange(half, dtype=jnp.int32)
-    my_seq = info[OWN_SEQ]
-    next_seq = jnp.minimum(my_seq + 1, seq_count - 1)
-    is_live = (ids < info[COUNT])[:, None]
-    is_text = is_live & ((ids >= info[TEXT_FROM]) & (ids < info[TEXT_TO]))[:, None]
-    is_next = is_live & (info[OWN_FROM] + ids >= info[NEXT_FROM])[:, None]
-    vectors = (image_mod[my_seq], text_mod[my_seq], image_mod[next_seq])
-
-    def modulation(which):
-        return jnp.where(
-            is_text, vectors[1][which][None], jnp.where(is_next, vectors[2][which][None], vectors[0][which][None])
-        )
-
-    shift_rows, scale_rows, gate_rows, shift_mlp, scale_mlp, gate_mlp = (modulation(i) for i in range(6))
-    stream = my_rows(tokens).astype(F32)
-    grad_stream = jnp.where(is_live, my_rows(cotangent).astype(F32), 0.0)
-    normed, inverse_std = layer_norm(stream)
-    modulated, grad_mlp = pl.pallas_call(
-        enter_kernel,
-        out_shape=(jax.ShapeDtypeStruct((half, width), BF),) * 2,
-        in_specs=[SMEM] + [VMEM] * 4,
-        out_specs=(VMEM, VMEM),
-        compiler_params=pltpu.CompilerParams(vmem_limit_bytes=VMEM_LIMIT),
-        cost_estimate=took_us(4),
-    )(info, tokens, cotangent, image_mod, text_mod)
+    my_tokens, my_cotangent = my_rows(tokens), my_rows(cotangent)
+
+    def rows_kernel(body, kinds, args, time, deps=(), extra=(), scratches=()):
+        return pl.pallas_call(
+            after(body, 1 + len(args), len(deps)),
+            out_shape=tuple(jax.ShapeDtypeStruct((half, width), kind) for kind in kinds) + tuple(extra),
+            in_specs=[SMEM] + [VMEM] * len(args) + [ANY] * len(deps),
+            out_specs=(VMEM,) * (len(kinds) + len(extra)),
+            scratch_shapes=list(scratches),
+            compiler_params=pltpu.CompilerParams(vmem_limit_bytes=VMEM_LIMIT),
+            cost_estimate=took_us(time),
+        )(info, *args, *deps)
+
+    parts_of = lambda state: (*state[:3], *state[5:])
+    modulated, grad_mlp = rows_kernel(enter_kernel, (BF, BF), (tokens, cotangent, image_mod, text_mod), 4)
 
     slot = lambda n: jax.ShapeDtypeStruct((BLOCKS, half, n), BF)
     full = lambda n: jax.ShapeDtypeStruct((BLOCKS, rows_cap, n), BF)
@@ -1127,10 +1118,11 @@
         axis=2,
     )
     rest_picked = pick_pieces(pack_rest, place)
-    mod_own, mod_oth = spread_end(spread_next(mod_begun, rest_picked[:1]))
-    (plane_rest,) = arrange(swap_pieces(rest_picked), place, stack_rows, plane_of(4 * fc + 2 * mine))
-    whole_out = lax.all_gather(plane_rest[:, 4 * fc :], "g", axis=0, tiled=True)
-    whole_fc2 = lax.all_gather(plane_rest[:, 2 * fc : 4 * fc], "g", axis=0, tiled=True)
+    rest_got = swap_pieces(rest_picked)
+    mod_own, mod_oth = spread_end(spread_next(mod_begun, rest_picked[:1]), rest_got[1:])
+    plane_fc1, plane_fc2, plane_out = arrange(rest_got, place, stack_rows, plane_of(2 * fc, 2 * fc, 2 * mine))
+    whole_out = lax.all_gather(plane_out, "g", axis=0, tiled=True)
+    whole_fc2 = lax.all_gather(plane_fc2, "g", axis=0, tiled=True)
 
     pair = lambda rows: jax.ShapeDtypeStruct((rows, 2 * mine), BF)
     queries, pairs, tail, edge, head, head_edge = stepped(
@@ -1140,12 +1132,12 @@
         [kept(s) for s in ((group_rows, mine), (group_rows, 2 * mine), (TAIL, 2 * mine), (EDGE, 2 * mine), (TAIL, 2 * mine), (EDGE, 2 * mine))],
         (rows_of(mine, BF), pair(group_rows), pair(TAIL), pair(EDGE), pair(TAIL), pair(EDGE)),
         weight_pair(3 * mine) + [scratch(group_rows, 3 * mine), scratch(rows_cap, width), scratch(rows_cap, 3 * mine)],
-        1,
+        6,
     )(info, mod_own, mod_oth, whole_qkv)
 
     near_back, near_on = shift(tail, 1), shift(head, -1)
     gmlp_begun = spread_begin(copy_after(grad_mlp, (queries,)))
-    fc1_piece = copy_after(plane_rest[:, : 2 * fc], (near_back, near_on, *gmlp_begun[1:]))
+    fc1_piece = copy_after(plane_fc1, (near_back, near_on, *gmlp_begun[1:]))
     whole_fc1 = lax.all_gather(fc1_piece, "g", axis=0, tiled=True)
     gmlp_state = spread_next(gmlp_begun, (near_back, near_on, whole_out))
     gmlp_own, gmlp_oth = spread_end(gmlp_state)
@@ -1194,12 +1186,10 @@
         )(info, rows, w)
 
     branch_state = collect_next(collect_begin(core_sum(*to_slots(mine, 0, attended, whole_out, (), 1))), (whole_fc1,))
-    branch = collect_end(branch_state)
-    first = stream + gate_rows * branch
-    normed_mlp, inverse_mlp = layer_norm(first)
-    modulated_mlp = (normed_mlp * (1.0 + scale_mlp) + shift_mlp).astype(BF)
-
-    mm_own, mm_oth = spread(copy_after(modulated_mlp, (gmlp_oth,)))
+    branch, modulated_mlp = rows_kernel(
+        middle_kernel, (F32, BF), (*parts_of(branch_state), my_tokens, image_mod, text_mod), 4, (gmlp_oth,)
+    )
+    mm_own, mm_oth = spread(modulated_mlp)
     fc_block = block((rows_cap, fc))
     hid, slope = stepped(
         mlp_up_kernel,
@@ -1223,7 +1213,7 @@
             deps,
         )(info, *left, right)
 
-    def row_sums(left, rows, deps=()):
+    def row_sums(left, rows, deps=(), time=0.1):
         n = rows.shape[1]
         return stepped(
             row_sums_kernel,
@@ -1232,15 +1222,12 @@
             kept((width, 2 * n)),
             jax.ShapeDtypeStruct((width, 2 * n), BF),
             [scratch(width, n, F32), scratch(width, n, F32), scratch(rows_cap, width), scratch(rows_cap, n)],
-            n / 42,
+            time,
             deps,
         )(info, *left, rows)
 
     fc2_sums = slot_sums((gmlp_own, gmlp_oth), hid, (), 1)
     fc2_part = over_groups(fc2_sums)
-    head_top = jnp.max(tops[:heads], axis=1)
-    spot = jnp.arange(BLOCKS)[:, None] == q
-    head_max = jnp.where(spot, head_top[None, :], NEGATIVE).reshape(1, -1)
     gm_own, gm_oth, gb = stepped(
         mlp_back_kernel,
         BLOCKS,
@@ -1256,8 +1243,7 @@
     gm_state = collect_begin(gm_part)
     fc1_sums = slot_sums((mm_own, mm_oth), gb, gm_part, 12)
     fc1_part = over_groups(fc1_sums)
-    gm_state = collect_next(gm_state, (fc1_sums,))
-    head_max = max_over_groups(copy_after(head_max, gm_state[3:5]))
+    gm_state = collect_next(gm_state, (fc1_sums,), 1)
     mlp_own, mlp_oth = stepped(
         slots_to_slots_kernel,
         BLOCKS,
@@ -1265,20 +1251,18 @@
         (slot_block, slot_block),
         (slot(width), slot(width)),
         [scratch(rows_cap, width)],
-        10,
+        25,
         gm_state[3:5],
     )(info, hid, whole_fc2, whole_fc2)
-    grad_mod_mlp = collect_end(gm_state, (mlp_own, head_max))
-
-    grad_first = jnp.where(
-        is_live,
-        grad_stream + norm_back(grad_mod_mlp * (1.0 + scale_mlp), normed_mlp, inverse_mlp),
-        0.0,
+    grad_mod_mlp, grad_first, grad_branch = rows_kernel(
+        turn_kernel,
+        (F32, F32, BF),
+        (*parts_of(gm_state), branch, my_tokens, my_cotangent, image_mod, text_mod),
+        5,
+        (mlp_own,),
     )
-    grad_branch = (gate_rows * grad_first).astype(BF)
     gbr_begun = spread_begin(grad_branch)
     gbr_own, gbr_oth = spread_end(spread_next(gbr_begun, (fc2_part,)))
-    mlp_part = core_sum(mlp_own, mlp_oth, (gbr_oth,))
     grad_attended = stepped(
         functools.partial(back_project_kernel, 0),
         BLOCKS,
@@ -1289,8 +1273,8 @@
         1,
     )(info, gbr_own, gbr_oth, whole_out)
 
+    mlp_part = core_sum(mlp_own, mlp_oth, (gbr_oth,), 3)
     mlp_state = collect_begin(mlp_part)
-    head_max = max_over_plane(copy_after(head_max, mlp_part[:1]))
     dq, give_far_back, give_back, d_pairs, give_on, give_far_on = stepped(
         attend_back_kernel,
         n_tiles,
@@ -1323,82 +1307,79 @@
 
     out_sums = row_sums((gbr_own, gbr_oth), attended, (dq,))
     out_part = over_groups(copy_after(out_sums, (gave_back, gave_on)))
-    mlp_state = collect_next(mlp_state, (out_sums,))
+    mlp_state = collect_next(mlp_state, (out_sums,), 1)
     pieces_of = lambda part, deps: pick_pieces(part.reshape(BLOCKS, share, -1), place, deps)
-    mlp_branch = collect_end(mlp_state, (gave_back, gave_on))
     grad_qkv = pl.pallas_call(
-        after(gather_grads_kernel, 7, 4),
+        after(gather_grads_kernel, 7, 2),
         out_shape=rows_of(3 * mine, BF),
-        in_specs=[SMEM] + [VMEM] * 6 + [ANY] * 4,
+        in_specs=[SMEM] + [VMEM] * 6 + [ANY] * 2,
         out_specs=VMEM,
         scratch_shapes=[scratch(group_rows, 2 * mine, F32)],
         compiler_params=pltpu.CompilerParams(vmem_limit_bytes=VMEM_LIMIT),
         cost_estimate=took_us(8),
-    )(info, dq, d_pairs, gave_back, gave_on, gave_far_back, gave_far_on, mlp_branch, out_sums, fc1_part, head_max)
-
-    qkv_sums = row_sums((mod_own, mod_oth), grad_qkv)
+    )(info, dq, d_pairs, gave_back, gave_on, gave_far_back, gave_far_on, out_sums, fc1_part)
+
+    mod_sent = to_slots(3 * mine, 0, grad_qkv, whole_qkv, mlp_state[3:5], 0.1)
+    qkv_sums = row_sums((mod_own, mod_oth), grad_qkv, (*mod_sent, *mlp_state[5:]), 14)
     qkv_part = over_groups(qkv_sums)
-    mod_part = core_sum(*to_slots(3 * mine, 0, grad_qkv, whole_qkv, (qkv_sums,)))
-    mod_state = collect_next(collect_begin(mod_part))
+    mod_part = core_sum(*mod_sent, (qkv_sums,), 3)
+    mod_state = collect_next(collect_begin(mod_part), mod_part[:1], 1)
     pair_f32 = lambda *shape: (jax.ShapeDtypeStruct(shape, F32),) * 2
-    mixed_rows = jnp.where(is_live, first + gate_mlp * mlp_branch, 0.0).astype(BF)
-    mixed = both_halves(copy_after(mixed_rows, mod_part[:1]))
-    late_max = copy_after(head_max, mod_part[:1])[0]
-    root_factor = jnp.sqrt(clip_limits / jnp.maximum(late_max, clip_limits))
-    column_scale = jnp.repeat(root_factor, HEAD)[None, None, :]
-    clipped = tuple((w[:, :2, :].astype(F32) * column_scale).astype(BF) for w in (image_qkv, text_qkv))
-    grad_modulated = collect_end(mod_state, (mixed, *clipped))
     fc2_picked, fc1_picked = pieces_of(fc2_part, mod_state[3:5]), pieces_of(fc1_part, mod_state[3:5])
-    fc2_got, fc1_got = swap_pieces(fc2_picked), swap_pieces(fc1_picked)
-    fc2_outs = arrange(fc2_got, place, give_turned, pair_f32(BLOCKS * fc, share))
+    out_picked = pieces_of(out_part, mod_state[3:5])
+    fc2_got, fc1_got, out_got = swap_pieces(fc2_picked), swap_pieces(fc1_picked), swap_pieces(out_picked)
+    tokens_grad_rows, mixed_rows, mod_sum = rows_kernel(
+        leave_kernel,
+        (F32, BF),
+        (
+            *parts_of(mod_state),
+            *parts_of(mlp_state),
+            grad_first,
+            branch,
+            grad_mod_mlp,
+            my_tokens,
+            my_cotangent,
+            image_mod,
+            text_mod,
+        ),
+        12,
+        (fc2_picked[0], fc1_picked[0], out_picked[0]),
+        (jax.ShapeDtypeStruct((2 * seq_count, 6, width), F32),),
+        (scratch(half, width, F32), scratch(half, width, F32)),
+    )
+    mixed = both_halves(mixed_rows)
+    qkv_got = swap_pieces(pieces_of(qkv_part, (mod_sum,)))
+    fc2_outs = arrange(fc2_got, place, give_wide, pair_f32(share, BLOCKS * fc))
     fc1_outs = arrange(fc1_got, place, give_wide, pair_f32(share, BLOCKS * fc))
-    qkv_picked, out_picked = pieces_of(qkv_part, ()), pieces_of(out_part, (grad_modulated,))
-    qkv_got, out_got = swap_pieces(qkv_picked), swap_pieces(out_picked)
-    out_outs = arrange(out_got, place, give_turned, pair_f32(columns, share))
-    qkv_outs = arrange(qkv_got, place, give_qkv, pair_f32(share, 3, columns))
-
-    row_block = pl.BlockSpec((half // 4, width), lambda t: (t, 0))
-    vectors_spec = whole(image_mod.shape)
-    tokens_grad_rows, mod_sum = stepped(
-        leave_kernel,
-        4,
-        [SMEM] + [row_block] * 7 + [vectors_spec] * 2,
-        (row_block, kept((2 * seq_count, 6, width))),
-        (
-            jax.ShapeDtypeStruct((half, width), F32),
-            jax.ShapeDtypeStruct((2 * seq_count, 6, width), F32),
-        ),
-        (),
-        8,
-        (qkv_picked[0], fc2_picked[0], fc1_picked[0], out_picked[0]),
-    )(
-        info,
-        grad_modulated,
-        grad_first,
-        branch,
-        grad_mod_mlp,
-        mlp_branch,
-        my_rows(tokens),
-        my_rows(cotangent),
-        image_mod,
-        text_mod,
-    )
+    out_outs = arrange(out_got, place, give_narrow, pair_f32(share, columns))
+    qkv_outs = arrange(qkv_got, place, give_qkv, pair_f32(3, share, columns))
     mod_sum = mod_sum.reshape(2 * seq_count * 6, -1, share)
     mod_sum = jnp.swapaxes(mod_sum, 0, 1)
     mod_sum = mod_sum + over_core(mod_sum)
-    mod_sum = sums_of_shares(mod_sum, g, q, qkv_got)
-    mod_sum = mod_sum.reshape(2, seq_count, 6, share)
+    head_top = jnp.max(tops[:heads], axis=1)
+    spot = jnp.arange(BLOCKS)[:, None] == q
+    head_top = jnp.where(spot, head_top[None, :], NEGATIVE).reshape(-1)
+    n_heads = head_top.shape[0]
+    head_top = jnp.pad(head_top, (0, -n_heads % share))[None, :]
+    top_rows = -(-n_heads // share)
+    head_top = jnp.broadcast_to(head_top.reshape(1, top_rows, share), (mod_sum.shape[0], top_rows, share))
+    mod_sum = sums_of_shares(jnp.concatenate([mod_sum, head_top], axis=1), top_rows, g, q, qkv_got)
+    head_max = mod_sum[-top_rows:].reshape(-1)[:n_heads]
+    mod_sum = mod_sum[:-top_rows].reshape(2, seq_count, 6, share)
+    root_factor = jnp.sqrt(clip_limits / jnp.maximum(head_max, clip_limits))
+    column_scale = jnp.repeat(root_factor, HEAD)[None, None, :]
+    clipped = tuple((w[:, :2, :].astype(F32) * column_scale).astype(BF) for w in (image_qkv, text_qkv))
 
     return (
         mixed,
         both_halves(tokens_grad_rows),
         mod_sum[0],
         mod_sum[1],
-        *qkv_outs,
-        *out_outs,
+        *(jnp.swapaxes(part, 0, 1) for part in qkv_outs),
+        *(part.T for part in out_outs),
         *fc1_outs,
-        *fc2_outs,
-        head_max[0],
+        *(part.T for part in fc2_outs),
+        head_max,
         *clipped,
     )
 

time: 777 us -> 719 us (0.925)
  waiting for transfers between devices: 222 us -> 206 us
  local copies, waits for them, and re-layouts: 56.4 us -> 41.4 us
  other arithmetic: 33.6 us -> 20.3 us
  starting transfers between devices: 108 us -> 96.8 us
    unnamed x172 -> x138, local copies, waits for them, and re-layouts: 27.4 us -> 14.8 us
    pallas_call x6 -> x5, Pallas kernels: 24.2 us -> 35.3 us  [the longest x4 28.2 us: rows_kernel(): pl.pallas_call(after(body, 1 + len(args), len(deps)), out_shape=tuple((ja...]
    ppermute x3 -> x0, starting transfers between devices: 10.5 us -> none  [max_over_groups(): lax.ppermute(value, 'g', [(i, (i + step) % groups) for i in range(groups)])]
    reduce_scatter x4, waiting for transfers between devices: 10 us -> 0.02 us  [over_groups(): return lax.psum_scatter(sums, 'g', scatter_dimension=0, tiled=True)]
    pallas_call x14 -> x13, Pallas kernels: 214 us -> 204 us  [stepped(): return lambda *args: run(*args, *deps)]
    ppermute x3, starting transfers between devices: 5.66 us -> 15.3 us  [sums_of_shares(): lax.ppermute(pick(shares, lax.rem(g + step, groups)), 'g', pairs)]
    ppermute x4, starting transfers between devices: 17.7 us -> 8.52 us  [shift(): return lax.ppermute(value, 'g', pairs)]
    pallas_call x23 -> x20, Pallas kernels: 42.6 us -> 38.4 us  [sum_after(): pl.pallas_call(after(body, n, len(deps)), out_shape=jax.ShapeDtypeStruct(...]
  transfers between devices with their start and end apart: 93 -> 87, of which waited for: 40 -> 37; matrix products, arithmetic and copies ran while one was open for 8% -> 5% of each run, Pallas kernels for 43% -> 46%
where the time goes in v3:
time: 719 us; the launch traced here: 712 us
  Pallas kernels  331 us (46%)
  waiting for transfers between devices  206 us (29%)
  starting transfers between devices  96.8 us (13%)
  local copies, waits for them, and re-layouts  41.4 us (6%)
  other arithmetic  20.3 us (3%)
  between operations  16.1 us (2%)
    pallas_call x13, Pallas kernels, stepped(): return lambda *args: run(*args, *deps)  204 us
    ppermute x27, waiting for transfers between devices, over_x(): return lax.ppermute(value, 'x', SWAP)  88.5 us
    ppermute x27, waiting for transfers between devices, over_y(): return lax.ppermute(value, 'y', SWAP)  62.4 us
    pallas_call x20, Pallas kernels, sum_after(): pl.pallas_call(after(body, n, len(deps)), out_shape=jax.ShapeDtypeStruct(...  38.4 us
    ppermute x27, starting transfers between devices, over_x(): return lax.ppermute(value, 'x', SWAP)  31 us
    ppermute x27, starting transfers between devices, over_y(): return lax.ppermute(value, 'y', SWAP)  28.9 us
    pallas_call x4, Pallas kernels, rows_kernel(): pl.pallas_call(after(body, 1 + len(args), len(deps)), out_shape=tuple((ja...  28.2 us
    ppermute x11, waiting for transfers between devices, over_core(): return lax.ppermute(value, 'c', SWAP)  20.9 us
  transfers between devices with their start and end apart: 87, of which 37 were waited for; matrix products, arithmetic and copies ran while one was open for 5% of the time, Pallas kernels for 46%

profile of v3, /device:TPU:0, one launch (start us, length us, event | category | flops | bytes accessed | tf_op | source)
XLA Modules:
  0.0 712.0 jit_solution(6401434043743212312)
XLA Ops:
  61.2 16.2 %collective-permute-done.8.refs_2_.refs_3_ = bf16[96,3456]{1,0:T(8,128)(2,1)S(1)} collective-permute-done((bf16[96,3456]{1,0:T(8,128)(2,1)}, bf16[96,3456]{1,0:T(8,128)(2,1)S(1)}, u32[]{:S(2)}, u32[]{:S(2)}) %collective-permute-start.8) | collective-permute-done | bytes 663584 | tf_op jit(solution)/shard_map/ppermute | solution.py:848
  104.5 16.1 %shard_map.271 = (bf16[2048,192]{1,0:T(8,128)(2,1)}, bf16[2048,384]{1,0:T(8,128)(2,1)}, bf16[1184,384]{1,0:T(8,128)(2,1)}, bf16[160,384]{1,0:T(8,128)(2,1)S(1)},...) custom-call(s32[23]{0:T(128)} %get-tuple-element.133.refs_0_, bf16[4,256,1536]{2,1,0:T(8,128)(2,1)} %copy-done.7, ...), custom_call_target="tpu_custom_call" | custom-call | flops 6899999744 | bytes 6000000 | tf_op jit(solution)/shard_map/pallas_call | solution.py:85
  128.2 16.5 %collective-permute-done.15.refs_3_ = bf16[256,1536]{1,0:T(8,128)(2,1)S(1)} collective-permute-done((bf16[256,1536]{1,0:T(8,128)(2,1)}, bf16[256,1536]{1,0:T(8,128)(2,1)S(1)}, u32[]{:S(2)}, u32[]{:S(2)}) %collective-permute-start.15) | collective-permute-done | bytes 786464 | tf_op jit(solution)/shard_map/ppermute | solution.py:844
  167.7 26.7 %shard_map.277 = (bf16[2048,192]{1,0:T(8,128)(2,1)}, f32[2048,192]{1,0:T(8,128)}, f32[8,8,256]{2,1,0:T(8,128)}, f32[8,256]{1,0:T(8,128)}) custom-call(s32[64]{0:T(128)} %get-tuple-element.134.refs_0_, s32[6]{0:T(128)} %refs_1_.5, bf16[2048,192]{1,0:T(8,128)(2,1)} %get-tuple-element.144.refs_1_.refs_2_, bf16[160,384]{1,0:T(8,128)(2,1)} %get-tuple-element.151.refs_3_.refs_5_, ...), custom_call_target="tpu_custom_call" | custom-call | flops 1150000000 | bytes 1000000 | tf_op jit(solution)/shard_map/pallas_call | solution.py:85
  194.4 7.9 %shard_map.278 = (bf16[4,256,1536]{2,1,0:T(8,128)(2,1)}, bf16[4,256,1536]{2,1,0:T(8,128)(2,1)}) custom-call(s32[23]{0:T(128)} %get-tuple-element.133.refs_0_, bf16[2048,192]{1,0:T(8,128)(2,1)} %get-tuple-element.155.refs_1_.refs_3_, bf16[1536,384]{1,0:T(8,128)(2,1)} %all-gather.7.cloned.1.call-done.refs_3_.refs_2_), custom_call_target="tpu_custom_call" | custom-call | flops 1150000000 | bytes 1000000 | tf_op jit(solution)/shard_map/pallas_call | solution.py:85
  205.3 8.5 %collective-permute-done.19 = bf16[128,1536]{1,0:T(8,128)(2,1)S(1)} collective-permute-done((bf16[128,1536]{1,0:T(8,128)(2,1)S(1)}, bf16[128,1536]{1,0:T(8,128)(2,1)S(1)}, u32[]{:S(2)}, u32[]{:S(2)}) %collective-permute-start.19) | collective-permute-done | bytes 393248 | tf_op jit(solution)/shard_map/ppermute | solution.py:848
  226.7 8.3 %collective-permute-done.27.refs_1_ = bf16[128,1536]{1,0:T(8,128)(2,1)} collective-permute-done((bf16[128,1536]{1,0:T(8,128)(2,1)}, bf16[128,1536]{1,0:T(8,128)(2,1)}, u32[]{:S(2)}, u32[]{:S(2)}) %collective-permute-start.27) | collective-permute-done | bytes 393248 | tf_op jit(solution)/shard_map/ppermute | solution.py:844
  235.0 12.1 %all-gather.9.cloned.1.call-done.refs_2_.refs_3_.refs_4_.refs_5_ = bf16[1536,1536]{1,0:T(8,128)(2,1)} async-done(((bf16[384,1536]{1,0:T(8,128)(2,1)}), bf16[1536,1536]{1,0:T(8,128)(2,1)}) %all-gather.9.cloned.1.call-update) | async-done | bytes 4718608 | tf_op jit(solution)/shard_map/all_gather | solution.py:1141
  271.9 16.4 %collective-permute-done.29 = bf16[256,1536]{1,0:T(8,128)(2,1)S(1)} collective-permute-done((bf16[256,1536]{1,0:T(8,128)(2,1)}, bf16[256,1536]{1,0:T(8,128)(2,1)S(1)}, u32[]{:S(2)}, u32[]{:S(2)}) %collective-permute-start.29) | collective-permute-done | bytes 786464 | tf_op jit(solution)/shard_map/ppermute | solution.py:844
  304.9 13.1 %shard_map.283 = (bf16[4,512,768]{2,1,0:T(8,128)(2,1)}, bf16[4,512,768]{2,1,0:T(8,128)(2,1)}) custom-call(s32[23]{0:T(128)} %get-tuple-element.133.refs_0_, bf16[4,256,1536]{2,1,0:T(8,128)(2,1)} %copy-done.2, bf16[4,256,1536]{2,1,0:T(8,128)(2,1)} %collective-permute-done.33.refs_2_, ...), custom_call_target="tpu_custom_call" | custom-call | flops 1150000000 | bytes 1000000 | tf_op jit(solution)/shard_map/pallas_call | solution.py:85
  318.0 12.8 %shard_map.284.refs_8_ = bf16[1536,1536]{1,0:T(8,128)(2,1)} custom-call(s32[23]{0:T(128)} %get-tuple-element.133.refs_0_, bf16[4,256,1536]{2,1,0:T(8,128)(2,1)} %copy-done, bf16[4,256,1536]{2,1,0:T(8,128)(2,1)} %collective-permute-done.21.refs_9_.refs_2_, bf16[4,512,768]{2,1,0:T(8,128)(2,1)} %get-tuple-element.168.refs_3_.refs_1_), custom_call_target="tpu_custom_call" | custom-call | flops 1150000000 | bytes 1000000 | tf_op jit(solution)/shard_map/pallas_call | solution.py:85
  337.0 20.0 %shard_map.285 = (bf16[4,256,1536]{2,1,0:T(8,128)(2,1)}, bf16[4,256,1536]{2,1,0:T(8,128)(2,1)}, bf16[4,512,768]{2,1,0:T(8,128)(2,1)}) custom-call(s32[23]{0:T(128)} %get-tuple-element.133.refs_0_, bf16[4,256,1536]{2,1,0:T(8,128)(2,1)} %copy-done, bf16[4,256,1536]{2,1,0:T(8,128)(2,1)} %collective-permute-done.21.refs_9_.refs_2_, ...), custom_call_target="tpu_custom_call" | custom-call | flops 1150000000 | bytes 1000000 | tf_op jit(solution)/shard_map/pallas_call | solution.py:85
  371.6 12.9 %shard_map.287.refs_2_ = bf16[1536,1536]{1,0:T(8,128)(2,1)} custom-call(s32[23]{0:T(128)} %get-tuple-element.133.refs_0_, bf16[4,256,1536]{2,1,0:T(8,128)(2,1)} %copy-done.2, bf16[4,256,1536]{2,1,0:T(8,128)(2,1)} %collective-permute-done.33.refs_2_, bf16[4,512,768]{2,1,0:T(8,128)(2,1)} %get-tuple-element.176.refs_3_, ...), custom_call_target="tpu_custom_call" | custom-call | flops 13799999488 | bytes 12000000 | tf_op jit(solution)/shard_map/pallas_call | solution.py:85
  393.0 11.3 %shard_map.290 = (bf16[4,256,1536]{2,1,0:T(8,128)(2,1)}, bf16[4,256,1536]{2,1,0:T(8,128)(2,1)}) custom-call(s32[23]{0:T(128)} %get-tuple-element.133.refs_0_, bf16[4,512,768]{2,1,0:T(8,128)(2,1)} %get-tuple-element.168.refs_3_.refs_1_, bf16[1536,1536]{1,0:T(8,128)(2,1)} %all-gather.11.cloned.1.call-done.refs_6_.refs_7_.refs_2_.refs_3_, ...), custom_call_target="tpu_custom_call" | custom-call | flops 28750000128 | bytes 25000000 | tf_op jit(solution)/shard_map/pallas_call | solution.py:85
  412.8 16.9 %collective-permute-done.41 = bf16[256,1536]{1,0:T(8,128)(2,1)S(1)} collective-permute-done((bf16[256,1536]{1,0:T(8,128)(2,1)}, bf16[256,1536]{1,0:T(8,128)(2,1)S(1)}, u32[]{:S(2)}, u32[]{:S(2)}) %collective-permute-start.41) | collective-permute-done | bytes 786464 | tf_op jit(solution)/shard_map/ppermute | solution.py:844
  446.3 9.0 %collective-permute-done.45.refs_2_ = bf16[4,256,1536]{2,1,0:T(8,128)(2,1)} collective-permute-done((bf16[4,256,1536]{2,1,0:T(8,128)(2,1)S(1)}, bf16[4,256,1536]{2,1,0:T(8,128)(2,1)}, u32[]{:S(2)}, u32[]{:S(2)}) %collective-permute-start.45) | collective-permute-done | bytes 3145760 | tf_op jit(solution)/shard_map/ppermute | solution.py:852
  455.3 7.7 %shard_map.294.refs_3_ = bf16[2048,192]{1,0:T(8,128)(2,1)} custom-call(s32[23]{0:T(128)} %get-tuple-element.133.refs_0_, bf16[4,256,1536]{2,1,0:T(8,128)(2,1)} %copy-done.1, bf16[4,256,1536]{2,1,0:T(8,128)(2,1)} %collective-permute-done.45.refs_2_, bf16[1536,384]{1,0:T(8,128)(2,1)} %all-gather.7.cloned.1.call-done.refs_3_.refs_2_), custom_call_target="tpu_custom_call" | custom-call | flops 1150000000 | bytes 1000000 | tf_op jit(solution)/shard_map/pallas_call | solution.py:85
  467.7 38.6 %shard_map.296 = (bf16[2048,192]{1,0:T(8,128)(2,1)}, bf16[160,384]{1,0:T(8,128)(2,1)S(1)}, bf16[1184,384]{1,0:T(8,128)(2,1)}, f32[2048,384]{1,0:T(8,128)}, bf16[...) custom-call(s32[64]{0:T(128)} %get-tuple-element.134.refs_0_, s32[6]{0:T(128)} %refs_1_.5, ...), custom_call_target="tpu_custom_call" | custom-call | flops 1150000000 | bytes 1000000 | tf_op jit(solution)/shard_map/pallas_call | solution.py:85
  515.7 8.5 %shard_map.297.refs_7_.refs_2_.refs_0_ = bf16[1536,384]{1,0:T(8,128)(2,1)} custom-call(s32[23]{0:T(128)} %get-tuple-element.133.refs_0_, bf16[4,256,1536]{2,1,0:T(8,128)(2,1)} %copy-done.1, bf16[4,256,1536]{2,1,0:T(8,128)(2,1)} %collective-permute-done.45.refs_2_, bf16[2048,192]{1,0:T(8,128)(2,1)} %get-tuple-element.155.refs_1_.refs_3_, ...), custom_call_target="tpu_custom_call" | custom-call | flops 115000000 | bytes 100000 | tf_op jit(solution)/shard_map/pallas_call | solution.py:85
  543.2 13.3 %shard_map.301 = (bf16[4,256,1536]{2,1,0:T(8,128)(2,1)}, bf16[4,256,1536]{2,1,0:T(8,128)(2,1)}) custom-call(s32[23]{0:T(128)} %get-tuple-element.133.refs_0_, bf16[2048,576]{1,0:T(8,128)(2,1)} %shard_map.298.refs_1_.refs_3_, bf16[1536,1152]{1,0:T(8,128)(2,1)} %all-gather.5.cloned.1.call-done.refs_3_.refs_2_, bf16[128,1536]{1,0:T(8,128)(2,1)} %shard_map.299.refs_3_, ...), custom_call_target="tpu_custom_call" | custom-call | flops 115000000 | bytes 100000 | tf_op jit(solution)/shard_map/pallas_call | solution.py:85
  557.2 15.1 %shard_map.302.refs_2_ = bf16[1536,1152]{1,0:T(8,128)(2,1)} custom-call(s32[23]{0:T(128)} %get-tuple-element.133.refs_0_, bf16[4,256,1536]{2,1,0:T(8,128)(2,1)} %copy-done.7, bf16[4,256,1536]{2,1,0:T(8,128)(2,1)} %collective-permute-done.11.refs_2_, bf16[2048,576]{1,0:T(8,128)(2,1)} %shard_map.298.refs_1_.refs_3_, ...), custom_call_target="tpu_custom_call" | custom-call | flops 16099999744 | bytes 14000000 | tf_op jit(solution)/shard_map/pallas_call | solution.py:85
  609.8 7.9 %collective-permute-done.74.refs_2_ = bf16[96,384]{1,0:T(8,128)(2,1)S(1)} collective-permute-done((bf16[96,384]{1,0:T(8,128)(2,1)}, bf16[96,384]{1,0:T(8,128)(2,1)S(1)}, u32[]{:S(2)}, u32[]{:S(2)}) %collective-permute-start.74) | collective-permute-done | bytes 73760 | tf_op jit(solution)/shard_map/ppermute | solution.py:844
  622.1 12.3 %shard_map.310 = (f32[256,1536]{1,0:T(8,128)}, bf16[256,1536]{1,0:T(8,128)(2,1)}, f32[10,6,1536]{2,1,0:T(8,128)}) custom-call(s32[23]{0:T(128)} %get-tuple-element.133.refs_0_, bf16[256,1536]{1,0:T(8,128)(2,1)} %get-tuple-element.200.refs_2_.refs_1_, bf16[128,1536]{1,0:T(8,128)(2,1)} %copy-done.37, bf16[128,1536]{1,0:T(8,128)(2,1)} %copy-done.38, ...), custom_call_target="tpu_custom_call" | custom-call | flops 13799999488 | bytes 12000000 | tf_op jit(solution)/shard_map/pallas_call | solution.py:1087
  681.8 9.7 %collective-permute-start.71 = (f32[61,96]{1,0:T(8,128)S(1)}, f32[61,96]{1,0:T(8,128)S(1)}, u32[]{:S(2)}, u32[]{:S(2)}) collective-permute-start(f32[61,96]{1,0:T(8,128)S(1)} %get-tuple-element.245), channel_id=1, source_target_pairs={{0,8},{8,16},{16,24},{24,0},{1,9},{9,17},{17,25},{25,1},{2,10},{10... | collective-permute-start | bytes 70280 | tf_op jit(solution)/shard_map/ppermute | solution.py:939
  (422 shorter events, 360.7 us)
Async XLA Ops:
  7.2 97.3 %all-gather.5.cloned.1.call-start = ((), (), s32[]{:S(2)}) async-start(), calls=%async_computation.4 | async-start | bytes 4423680 | tf_op jit(solution)/shard_map/all_gather | solution.py:1107
  33.8 130.3 %all-gather.7.cloned.1.call-start = ((), (), s32[]{:S(2)}) async-start(), calls=%async_computation.5 | async-start | bytes 1474560 | tf_op jit(solution)/shard_map/all_gather | solution.py:1124
  44.1 33.2 %collective-permute-start.8 = (bf16[96,3456]{1,0:T(8,128)(2,1)}, bf16[96,3456]{1,0:T(8,128)(2,1)S(1)}, u32[]{:S(2)}, u32[]{:S(2)}) collective-permute-start(bf16[96,3456]{1,0:T(8,128)(2,1)} %get-tuple-element.138), channel_id=1, source_target_pairs={{0,4},{4,0},{1,5},{5,1},{2,6},{6,2},{3,7},{7,3},{8,12},{12,8},{9,1... | collective-permute-start | bytes 1990664 | tf_op jit(solution)/shard_map/ppermute | solution.py:848
  44.7 32.6 %collective-permute-start.9 = (bf16[96,3456]{1,0:T(8,128)(2,1)}, bf16[96,3456]{1,0:T(8,128)(2,1)S(1)}, u32[]{:S(2)}, u32[]{:S(2)}) collective-permute-start(bf16[96,3456]{1,0:T(8,128)(2,1)} %get-tuple-element.139), channel_id=1, source_target_pairs={{0,6},{2,4},{4,2},{6,0},{1,7},{3,5},{5,3},{7,1},{8,14},{10,12},{12... | collective-permute-start | bytes 1990664 | tf_op jit(solution)/shard_map/ppermute | solution.py:856
  49.6 34.5 %collective-permute-start.6 = (bf16[128,1536]{1,0:T(8,128)(2,1)}, bf16[128,1536]{1,0:T(8,128)(2,1)S(1)}, u32[]{:S(2)}, u32[]{:S(2)}) collective-permute-start(bf16[128,1536]{1,0:T(8,128)(2,1)} %shard_map.265), channel_id=1, source_target_pairs={{0,4},{4,0},{1,5},{5,1},{2,6},{6,2},{3,7},{7,3},{8,12},{12,8},{9,1... | collective-permute-start | bytes 1179656 | tf_op jit(solution)/shard_map/ppermute | solution.py:848
  55.1 31.5 %collective-permute-start.10 = (bf16[128,1536]{1,0:T(8,128)(2,1)}, bf16[128,1536]{1,0:T(8,128)(2,1)S(1)}, u32[]{:S(2)}, u32[]{:S(2)}) collective-permute-start(bf16[128,1536]{1,0:T(8,128)(2,1)} %shard_map.267), channel_id=1, source_target_pairs={{0,2},{2,0},{1,3},{3,1},{4,6},{6,4},{5,7},{7,5},{8,10},{10,8},{9,1... | collective-permute-start | bytes 1179656 | tf_op jit(solution)/shard_map/ppermute | solution.py:844
  96.5 150.6 %all-gather.9.cloned.1.call-start = ((), (), s32[]{:S(2)}) async-start(), calls=%async_computation.6 | async-start | bytes 5898240 | tf_op jit(solution)/shard_map/all_gather | solution.py:1141
  120.6 31.3 %collective-permute-start.17 = (bf16[1184,384]{1,0:T(8,128)(2,1)}, bf16[1184,384]{1,0:T(8,128)(2,1)S(1)}, u32[]{:S(2)}, u32[]{:S(2)}) collective-permute-start(bf16[1184,384]{1,0:T(8,128)(2,1)} %get-tuple-element.146), channel_id=1, source_target_pairs={{0,8},{8,16},{16,24},{1,9},{9,17},{17,25},{2,10},{10,18},{18,26},{... | collective-permute-start | bytes 2727944 | tf_op jit(solution)/shard_map/ppermute | solution.py:836
  121.9 32.0 %collective-permute-start.18 = (bf16[1184,384]{1,0:T(8,128)(2,1)}, bf16[1184,384]{1,0:T(8,128)(2,1)S(1)}, u32[]{:S(2)}, u32[]{:S(2)}) collective-permute-start(bf16[1184,384]{1,0:T(8,128)(2,1)} %get-tuple-element.147), channel_id=1, source_target_pairs={{8,0},{16,8},{24,16},{9,1},{17,9},{25,17},{10,2},{18,10},{26,18},{... | collective-permute-start | bytes 2727944 | tf_op jit(solution)/shard_map/ppermute | solution.py:836
  157.2 179.8 %all-gather.11.cloned.1.call-start = ((), (), s32[]{:S(2)}) async-start(), calls=%async_computation.7 | async-start | bytes 5898240 | tf_op jit(solution)/shard_map/all_gather | solution.py:1125
  216.9 40.0 %collective-permute-start.21 = (bf16[4,256,1536]{2,1,0:T(8,128)(2,1)S(1)}, bf16[4,256,1536]{2,1,0:T(8,128)(2,1)}, u32[]{:S(2)}, u32[]{:S(2)}) collective-permute-start(bf16[4,256,1536]{2,1,0:T(8,128)(2,1)S(1)} %pad_maximum_fusion.1.refs_1_), channel_id=1, source_target_pairs={{0,1},{1,0},{2,3},{3,2},{4,5},{5,4},{6,7},{7,6},{8,9},{9,8},{10,11... | collective-permute-start | bytes 9437192 | tf_op jit(solution)/shard_map/ppermute | solution.py:852
  217.0 214.3 %reduce-scatter.5.cloned.1.call-start = ((), (), s32[]{:S(2)}) async-start(), calls=%async_computation.8 | async-start | bytes 5898240 | tf_op jit(solution)/shard_map/reduce_scatter | solution.py:860
  224.1 26.5 %collective-permute-start.25 = (bf16[128,1536]{1,0:T(8,128)(2,1)}, bf16[128,1536]{1,0:T(8,128)(2,1)S(1)}, u32[]{:S(2)}, u32[]{:S(2)}) collective-permute-start(bf16[128,1536]{1,0:T(8,128)(2,1)} %get-tuple-element.162), channel_id=1, source_target_pairs={{0,4},{4,0},{1,5},{5,1},{2,6},{6,2},{3,7},{7,3},{8,12},{12,8},{9,1... | collective-permute-start | bytes 1179656 | tf_op jit(solution)/shard_map/ppermute | solution.py:848
  224.7 32.2 %collective-permute-start.23 = (bf16[128,1536]{1,0:T(8,128)(2,1)}, bf16[128,1536]{1,0:T(8,128)(2,1)}, u32[]{:S(2)}, u32[]{:S(2)}) collective-permute-start(bf16[128,1536]{1,0:T(8,128)(2,1)} %get-tuple-element.159), channel_id=1, source_target_pairs={{0,2},{2,0},{1,3},{3,1},{4,6},{6,4},{5,7},{7,5},{8,10},{10,8},{9,1... | collective-permute-start | bytes 1179656 | tf_op jit(solution)/shard_map/ppermute | solution.py:844
  225.2 31.7 %collective-permute-start.24 = (bf16[128,1536]{1,0:T(8,128)(2,1)}, bf16[128,1536]{1,0:T(8,128)(2,1)}, u32[]{:S(2)}, u32[]{:S(2)}) collective-permute-start(bf16[128,1536]{1,0:T(8,128)(2,1)} %get-tuple-element.160), channel_id=1, source_target_pairs={{0,4},{4,0},{1,5},{5,1},{2,6},{6,2},{3,7},{7,3},{8,12},{12,8},{9,1... | collective-permute-start | bytes 1179656 | tf_op jit(solution)/shard_map/ppermute | solution.py:848
  330.8 205.3 %reduce-scatter.7.cloned.1.call-start = ((), (), s32[]{:S(2)}) async-start(), calls=%async_computation.9 | async-start | bytes 5898240 | tf_op jit(solution)/shard_map/reduce_scatter | solution.py:860
  370.6 33.7 %collective-permute-start.35 = (bf16[128,1536]{1,0:T(8,128)(2,1)}, bf16[128,1536]{1,0:T(8,128)(2,1)S(1)}, u32[]{:S(2)}, u32[]{:S(2)}) collective-permute-start(bf16[128,1536]{1,0:T(8,128)(2,1)} %get-tuple-element.172.refs_7_), channel_id=1, source_target_pairs={{0,2},{2,0},{1,3},{3,1},{4,6},{6,4},{5,7},{7,5},{8,10},{10,8},{9,1... | collective-permute-start | bytes 1179656 | tf_op jit(solution)/shard_map/ppermute | solution.py:844
  371.1 33.2 %collective-permute-start.36 = (bf16[128,1536]{1,0:T(8,128)(2,1)}, bf16[128,1536]{1,0:T(8,128)(2,1)S(1)}, u32[]{:S(2)}, u32[]{:S(2)}) collective-permute-start(bf16[128,1536]{1,0:T(8,128)(2,1)} %get-tuple-element.173.refs_10_), channel_id=1, source_target_pairs={{0,4},{4,0},{1,5},{5,1},{2,6},{6,2},{3,7},{7,3},{8,12},{12,8},{9,1... | collective-permute-start | bytes 1179656 | tf_op jit(solution)/shard_map/ppermute | solution.py:848
  384.6 215.5 %reduce-scatter.9.cloned.1.call-start = ((), (), s32[]{:S(2)}) async-start(), calls=%async_computation.10 | async-start | bytes 1474560 | tf_op jit(solution)/shard_map/reduce_scatter | solution.py:860
  527.0 29.5 %collective-permute-start.53 = (bf16[128,1536]{1,0:T(8,128)(2,1)}, bf16[128,1536]{1,0:T(8,128)(2,1)S(1)}, u32[]{:S(2)}, u32[]{:S(2)}) collective-permute-start(bf16[128,1536]{1,0:T(8,128)(2,1)} %shard_map.300.refs_4_), channel_id=1, source_target_pairs={{0,4},{4,0},{1,5},{5,1},{2,6},{6,2},{3,7},{7,3},{8,12},{12,8},{9,1... | collective-permute-start | bytes 1179656 | tf_op jit(solution)/shard_map/ppermute | solution.py:848
  535.9 130.1 %reduce-scatter.11.cloned.1.call-start = ((), (), s32[]{:S(2)}) async-start(), calls=%async_computation.11 | async-start | bytes 4423680 | tf_op jit(solution)/shard_map/reduce_scatter | solution.py:860
  607.7 31.8 %collective-permute-start.80 = (bf16[96,1536]{1,0:T(8,128)(2,1)}, bf16[96,1536]{1,0:T(8,128)(2,1)}, u32[]{:S(2)}, u32[]{:S(2)}) collective-permute-start(bf16[96,1536]{1,0:T(8,128)(2,1)} %get-tuple-element.234), channel_id=1, source_target_pairs={{0,2},{2,0},{1,3},{3,1},{4,6},{6,4},{5,7},{7,5},{8,10},{10,8},{9,1... | collective-permute-start | bytes 884744 | tf_op jit(solution)/shard_map/ppermute | solution.py:844
  608.3 31.8 %collective-permute-start.81 = (bf16[96,1536]{1,0:T(8,128)(2,1)}, bf16[96,1536]{1,0:T(8,128)(2,1)}, u32[]{:S(2)}, u32[]{:S(2)}) collective-permute-start(bf16[96,1536]{1,0:T(8,128)(2,1)} %get-tuple-element.235), channel_id=1, source_target_pairs={{0,4},{4,0},{1,5},{5,1},{2,6},{6,2},{3,7},{7,3},{8,12},{12,8},{9,1... | collective-permute-start | bytes 884744 | tf_op jit(solution)/shard_map/ppermute | solution.py:848
  642.3 29.2 %collective-permute-start.63 = (f32[256,1536]{1,0:T(8,128)S(1)}, f32[256,1536]{1,0:T(8,128)}, u32[]{:S(2)}, u32[]{:S(2)}) collective-permute-start(f32[256,1536]{1,0:T(8,128)S(1)} %copy-done.10), channel_id=1, source_target_pairs={{0,1},{1,0},{2,3},{3,2},{4,5},{5,4},{6,7},{7,6},{8,9},{9,8},{10,11... | collective-permute-start | bytes 4718600 | tf_op jit(solution)/shard_map/ppermute | solution.py:852
  (134 other events, 1366.9 us)
Sparse Core Ops, SparseCore 0:
  33.9 70.5 all-gather.4
  106.6 35.5 all-gather.6
  157.4 89.7 all-gather.8
  249.1 87.8 all-gather.10
  339.2 83.6 reduce-scatter.4
  425.1 85.7 reduce-scatter.6
  536.0 40.3 reduce-scatter.8
  578.7 71.4 reduce-scatter.10

commit v4 on v3

--- a/solution.py
+++ b/solution.py
@@ -962,8 +962,29 @@
     return own, over_x(to_x), over_y(to_y), over_xy(to_xy)
 
 
-def exchange(pieces, place):
-    return swap_pieces(pick_pieces(pieces, place))
+def pick_heads(image, text, place):
+    share, parts, columns = image.shape
+    n = columns // BLOCKS
+
+    def body(place_ref, image_ref, text_ref, *outs):
+        for j, out in enumerate(outs):
+            for b in range(BLOCKS):
+
+                @pl.when((place_ref[1] ^ j) == b)
+                def _():
+                    for k, source in enumerate((image_ref, text_ref)):
+                        for p in range(parts):
+                            at = (parts * k + p) * n
+                            out[:, at : at + n] = source[p, :, b * n : (b + 1) * n]
+
+    return pl.pallas_call(
+        body,
+        out_shape=(jax.ShapeDtypeStruct((share, 2 * parts * n), image.dtype),) * BLOCKS,
+        in_specs=[SMEM, VMEM, VMEM],
+        out_specs=(VMEM,) * BLOCKS,
+        compiler_params=pltpu.CompilerParams(vmem_limit_bytes=VMEM_LIMIT),
+        cost_estimate=took_us(2),
+    )(place, jnp.swapaxes(image, 0, 1), jnp.swapaxes(text, 0, 1))
 
 
 def arrange(got, place, body, out_shape, deps=(), time=2):
@@ -1052,19 +1073,15 @@
         other = over_core(rows)
         return jnp.where(c == 0, jnp.concatenate([rows, other], axis=0), jnp.concatenate([other, rows], axis=0))
 
-    def quarter(inputs):
-        return jnp.moveaxis(inputs.reshape(share, -1, BLOCKS, mine), 2, 0).reshape(BLOCKS, share, -1)
-
     def quarter_turned(inputs):
         return jnp.swapaxes(inputs.reshape(BLOCKS, -1, share), 1, 2)
 
     def quarter_wide(inputs):
         return jnp.swapaxes(inputs.reshape(share, BLOCKS, -1), 0, 1)
 
-    pack_qkv = jnp.concatenate([quarter(image_qkv), quarter(text_qkv)], axis=2)
     place = jnp.stack([g, q, c]).astype(jnp.int32)
     plane_of = lambda *cuts: tuple(jax.ShapeDtypeStruct((BLOCKS * share, n), BF) for n in cuts)
-    (plane_qkv,) = arrange(exchange(pack_qkv, place), place, stack_rows, plane_of(6 * mine))
+    (plane_qkv,) = arrange(swap_pieces(pick_heads(image_qkv, text_qkv, place)), place, stack_rows, plane_of(6 * mine))
 
     n_tiles = group_rows // CHUNK
     reach = 2 * KEYS + 2 * TAIL_PAD + group_rows

time: 719 us -> 714 us (level)
    unnamed x138 -> x136, local copies, waits for them, and re-layouts: 14.8 us -> 15.1 us
  transfers between devices with their start and end apart: 87 -> 87, of which waited for: 37 -> 38; matrix products, arithmetic and copies ran while one was open for 5% -> 5% of each run, Pallas kernels for 46% -> 46%
where the time goes in v4:
time: 714 us; the launch traced here: 708 us
  Pallas kernels  331 us (46%)
  waiting for transfers between devices  208 us (29%)
  starting transfers between devices  96.1 us (13%)
  local copies, waits for them, and re-layouts  37.5 us (5%)
  other arithmetic  19 us (3%)
  between operations  16.1 us (2%)
    pallas_call x13, Pallas kernels, stepped(): return lambda *args: run(*args, *deps)  204 us
    ppermute x27, waiting for transfers between devices, over_x(): return lax.ppermute(value, 'x', SWAP)  88.6 us
    ppermute x27, waiting for transfers between devices, over_y(): return lax.ppermute(value, 'y', SWAP)  63.1 us
    pallas_call x20, Pallas kernels, sum_after(): pl.pallas_call(after(body, n, len(deps)), out_shape=jax.ShapeDtypeStruct(...  38.3 us
    ppermute x27, starting transfers between devices, over_x(): return lax.ppermute(value, 'x', SWAP)  31.3 us
    pallas_call x4, Pallas kernels, rows_kernel(): pl.pallas_call(after(body, 1 + len(args), len(deps)), out_shape=tuple((ja...  28.2 us
    ppermute x27, starting transfers between devices, over_y(): return lax.ppermute(value, 'y', SWAP)  28.2 us
    ppermute x11, waiting for transfers between devices, over_core(): return lax.ppermute(value, 'c', SWAP)  20.9 us
  transfers between devices with their start and end apart: 87, of which 38 were waited for; matrix products, arithmetic and copies ran while one was open for 5% of the time, Pallas kernels for 46%

profile of v4, /device:TPU:0, one launch (start us, length us, event | category | flops | bytes accessed | tf_op | source)
XLA Modules:
  0.0 707.9 jit_solution(8261772868823800300)
XLA Ops:
  56.0 16.2 %collective-permute-done.8.refs_2_.refs_3_ = bf16[96,3456]{1,0:T(8,128)(2,1)S(1)} collective-permute-done((bf16[96,3456]{1,0:T(8,128)(2,1)}, bf16[96,3456]{1,0:T(8,128)(2,1)S(1)}, u32[]{:S(2)}, u32[]{:S(2)}) %collective-permute-start.8) | collective-permute-done | bytes 663584 | tf_op jit(solution)/shard_map/ppermute | solution.py:848
  99.3 16.1 %shard_map.271 = (bf16[2048,192]{1,0:T(8,128)(2,1)}, bf16[2048,384]{1,0:T(8,128)(2,1)}, bf16[1184,384]{1,0:T(8,128)(2,1)}, bf16[160,384]{1,0:T(8,128)(2,1)S(1)},...) custom-call(s32[23]{0:T(128)} %get-tuple-element.133.refs_0_, bf16[4,256,1536]{2,1,0:T(8,128)(2,1)} %copy-done.7, ...), custom_call_target="tpu_custom_call" | custom-call | flops 6899999744 | bytes 6000000 | tf_op jit(solution)/shard_map/pallas_call | solution.py:85
  123.0 16.5 %collective-permute-done.15.refs_3_ = bf16[256,1536]{1,0:T(8,128)(2,1)S(1)} collective-permute-done((bf16[256,1536]{1,0:T(8,128)(2,1)}, bf16[256,1536]{1,0:T(8,128)(2,1)S(1)}, u32[]{:S(2)}, u32[]{:S(2)}) %collective-permute-start.15) | collective-permute-done | bytes 786464 | tf_op jit(solution)/shard_map/ppermute | solution.py:844
  162.5 26.7 %shard_map.277 = (bf16[2048,192]{1,0:T(8,128)(2,1)}, f32[2048,192]{1,0:T(8,128)}, f32[8,8,256]{2,1,0:T(8,128)}, f32[8,256]{1,0:T(8,128)}) custom-call(s32[64]{0:T(128)} %get-tuple-element.134.refs_0_, s32[6]{0:T(128)} %refs_1_.5, bf16[2048,192]{1,0:T(8,128)(2,1)} %get-tuple-element.144.refs_1_.refs_2_, bf16[160,384]{1,0:T(8,128)(2,1)} %get-tuple-element.151.refs_3_.refs_5_, ...), custom_call_target="tpu_custom_call" | custom-call | flops 1150000000 | bytes 1000000 | tf_op jit(solution)/shard_map/pallas_call | solution.py:85
  189.2 7.8 %shard_map.278 = (bf16[4,256,1536]{2,1,0:T(8,128)(2,1)}, bf16[4,256,1536]{2,1,0:T(8,128)(2,1)}) custom-call(s32[23]{0:T(128)} %get-tuple-element.133.refs_0_, bf16[2048,192]{1,0:T(8,128)(2,1)} %get-tuple-element.155.refs_1_.refs_3_, bf16[1536,384]{1,0:T(8,128)(2,1)} %all-gather.7.cloned.1.call-done.refs_3_.refs_2_), custom_call_target="tpu_custom_call" | custom-call | flops 1150000000 | bytes 1000000 | tf_op jit(solution)/shard_map/pallas_call | solution.py:85
  200.1 8.4 %collective-permute-done.19 = bf16[128,1536]{1,0:T(8,128)(2,1)S(1)} collective-permute-done((bf16[128,1536]{1,0:T(8,128)(2,1)S(1)}, bf16[128,1536]{1,0:T(8,128)(2,1)S(1)}, u32[]{:S(2)}, u32[]{:S(2)}) %collective-permute-start.19) | collective-permute-done | bytes 393248 | tf_op jit(solution)/shard_map/ppermute | solution.py:848
  221.5 8.3 %collective-permute-done.27.refs_1_ = bf16[128,1536]{1,0:T(8,128)(2,1)} collective-permute-done((bf16[128,1536]{1,0:T(8,128)(2,1)}, bf16[128,1536]{1,0:T(8,128)(2,1)}, u32[]{:S(2)}, u32[]{:S(2)}) %collective-permute-start.27) | collective-permute-done | bytes 393248 | tf_op jit(solution)/shard_map/ppermute | solution.py:844
  229.8 12.1 %all-gather.9.cloned.1.call-done.refs_2_.refs_3_.refs_4_.refs_5_ = bf16[1536,1536]{1,0:T(8,128)(2,1)} async-done(((bf16[384,1536]{1,0:T(8,128)(2,1)}), bf16[1536,1536]{1,0:T(8,128)(2,1)}) %all-gather.9.cloned.1.call-update) | async-done | bytes 4718608 | tf_op jit(solution)/shard_map/all_gather | solution.py:1158
  266.7 16.4 %collective-permute-done.29 = bf16[256,1536]{1,0:T(8,128)(2,1)S(1)} collective-permute-done((bf16[256,1536]{1,0:T(8,128)(2,1)}, bf16[256,1536]{1,0:T(8,128)(2,1)S(1)}, u32[]{:S(2)}, u32[]{:S(2)}) %collective-permute-start.29) | collective-permute-done | bytes 786464 | tf_op jit(solution)/shard_map/ppermute | solution.py:844
  299.7 13.0 %shard_map.283 = (bf16[4,512,768]{2,1,0:T(8,128)(2,1)}, bf16[4,512,768]{2,1,0:T(8,128)(2,1)}) custom-call(s32[23]{0:T(128)} %get-tuple-element.133.refs_0_, bf16[4,256,1536]{2,1,0:T(8,128)(2,1)} %copy-done.2, bf16[4,256,1536]{2,1,0:T(8,128)(2,1)} %collective-permute-done.33.refs_2_, ...), custom_call_target="tpu_custom_call" | custom-call | flops 1150000000 | bytes 1000000 | tf_op jit(solution)/shard_map/pallas_call | solution.py:85
  312.8 12.8 %shard_map.284.refs_8_ = bf16[1536,1536]{1,0:T(8,128)(2,1)} custom-call(s32[23]{0:T(128)} %get-tuple-element.133.refs_0_, bf16[4,256,1536]{2,1,0:T(8,128)(2,1)} %copy-done, bf16[4,256,1536]{2,1,0:T(8,128)(2,1)} %collective-permute-done.21.refs_9_.refs_2_, bf16[4,512,768]{2,1,0:T(8,128)(2,1)} %get-tuple-element.168.refs_3_.refs_1_), custom_call_target="tpu_custom_call" | custom-call | flops 1150000000 | bytes 1000000 | tf_op jit(solution)/shard_map/pallas_call | solution.py:85
  331.9 20.0 %shard_map.285 = (bf16[4,256,1536]{2,1,0:T(8,128)(2,1)}, bf16[4,256,1536]{2,1,0:T(8,128)(2,1)}, bf16[4,512,768]{2,1,0:T(8,128)(2,1)}) custom-call(s32[23]{0:T(128)} %get-tuple-element.133.refs_0_, bf16[4,256,1536]{2,1,0:T(8,128)(2,1)} %copy-done, bf16[4,256,1536]{2,1,0:T(8,128)(2,1)} %collective-permute-done.21.refs_9_.refs_2_, ...), custom_call_target="tpu_custom_call" | custom-call | flops 1150000000 | bytes 1000000 | tf_op jit(solution)/shard_map/pallas_call | solution.py:85
  366.5 12.9 %shard_map.287.refs_2_ = bf16[1536,1536]{1,0:T(8,128)(2,1)} custom-call(s32[23]{0:T(128)} %get-tuple-element.133.refs_0_, bf16[4,256,1536]{2,1,0:T(8,128)(2,1)} %copy-done.2, bf16[4,256,1536]{2,1,0:T(8,128)(2,1)} %collective-permute-done.33.refs_2_, bf16[4,512,768]{2,1,0:T(8,128)(2,1)} %get-tuple-element.176.refs_3_, ...), custom_call_target="tpu_custom_call" | custom-call | flops 13799999488 | bytes 12000000 | tf_op jit(solution)/shard_map/pallas_call | solution.py:85
  387.8 11.3 %shard_map.290 = (bf16[4,256,1536]{2,1,0:T(8,128)(2,1)}, bf16[4,256,1536]{2,1,0:T(8,128)(2,1)}) custom-call(s32[23]{0:T(128)} %get-tuple-element.133.refs_0_, bf16[4,512,768]{2,1,0:T(8,128)(2,1)} %get-tuple-element.168.refs_3_.refs_1_, bf16[1536,1536]{1,0:T(8,128)(2,1)} %all-gather.11.cloned.1.call-done.refs_6_.refs_7_.refs_2_.refs_3_, ...), custom_call_target="tpu_custom_call" | custom-call | flops 28750000128 | bytes 25000000 | tf_op jit(solution)/shard_map/pallas_call | solution.py:85
  407.6 16.9 %collective-permute-done.41 = bf16[256,1536]{1,0:T(8,128)(2,1)S(1)} collective-permute-done((bf16[256,1536]{1,0:T(8,128)(2,1)}, bf16[256,1536]{1,0:T(8,128)(2,1)S(1)}, u32[]{:S(2)}, u32[]{:S(2)}) %collective-permute-start.41) | collective-permute-done | bytes 786464 | tf_op jit(solution)/shard_map/ppermute | solution.py:844
  441.1 9.0 %collective-permute-done.45.refs_2_ = bf16[4,256,1536]{2,1,0:T(8,128)(2,1)} collective-permute-done((bf16[4,256,1536]{2,1,0:T(8,128)(2,1)S(1)}, bf16[4,256,1536]{2,1,0:T(8,128)(2,1)}, u32[]{:S(2)}, u32[]{:S(2)}) %collective-permute-start.45) | collective-permute-done | bytes 3145760 | tf_op jit(solution)/shard_map/ppermute | solution.py:852
  462.4 38.6 %shard_map.296 = (bf16[2048,192]{1,0:T(8,128)(2,1)}, bf16[160,384]{1,0:T(8,128)(2,1)S(1)}, bf16[1184,384]{1,0:T(8,128)(2,1)}, f32[2048,384]{1,0:T(8,128)}, bf16[...) custom-call(s32[64]{0:T(128)} %get-tuple-element.134.refs_0_, s32[6]{0:T(128)} %refs_1_.5, ...), custom_call_target="tpu_custom_call" | custom-call | flops 1150000000 | bytes 1000000 | tf_op jit(solution)/shard_map/pallas_call | solution.py:85
  510.4 8.5 %shard_map.297.refs_7_.refs_2_.refs_0_ = bf16[1536,384]{1,0:T(8,128)(2,1)} custom-call(s32[23]{0:T(128)} %get-tuple-element.133.refs_0_, bf16[4,256,1536]{2,1,0:T(8,128)(2,1)} %copy-done.1, bf16[4,256,1536]{2,1,0:T(8,128)(2,1)} %collective-permute-done.45.refs_2_, bf16[2048,192]{1,0:T(8,128)(2,1)} %get-tuple-element.155.refs_1_.refs_3_, ...), custom_call_target="tpu_custom_call" | custom-call | flops 115000000 | bytes 100000 | tf_op jit(solution)/shard_map/pallas_call | solution.py:85
  537.9 13.3 %shard_map.301 = (bf16[4,256,1536]{2,1,0:T(8,128)(2,1)}, bf16[4,256,1536]{2,1,0:T(8,128)(2,1)}) custom-call(s32[23]{0:T(128)} %get-tuple-element.133.refs_0_, bf16[2048,576]{1,0:T(8,128)(2,1)} %shard_map.298.refs_1_.refs_3_, bf16[1536,1152]{1,0:T(8,128)(2,1)} %all-gather.5.cloned.1.call-done.refs_3_.refs_2_, bf16[128,1536]{1,0:T(8,128)(2,1)} %shard_map.299.refs_3_, ...), custom_call_target="tpu_custom_call" | custom-call | flops 115000000 | bytes 100000 | tf_op jit(solution)/shard_map/pallas_call | solution.py:85
  552.1 15.2 %shard_map.302.refs_2_ = bf16[1536,1152]{1,0:T(8,128)(2,1)} custom-call(s32[23]{0:T(128)} %get-tuple-element.133.refs_0_, bf16[4,256,1536]{2,1,0:T(8,128)(2,1)} %copy-done.7, bf16[4,256,1536]{2,1,0:T(8,128)(2,1)} %collective-permute-done.11.refs_2_, bf16[2048,576]{1,0:T(8,128)(2,1)} %shard_map.298.refs_1_.refs_3_, ...), custom_call_target="tpu_custom_call" | custom-call | flops 16099999744 | bytes 14000000 | tf_op jit(solution)/shard_map/pallas_call | solution.py:85
  604.3 7.9 %collective-permute-done.74.refs_2_ = bf16[96,384]{1,0:T(8,128)(2,1)S(1)} collective-permute-done((bf16[96,384]{1,0:T(8,128)(2,1)}, bf16[96,384]{1,0:T(8,128)(2,1)S(1)}, u32[]{:S(2)}, u32[]{:S(2)}) %collective-permute-start.74) | collective-permute-done | bytes 73760 | tf_op jit(solution)/shard_map/ppermute | solution.py:844
  616.5 12.3 %shard_map.310 = (f32[256,1536]{1,0:T(8,128)}, bf16[256,1536]{1,0:T(8,128)(2,1)}, f32[10,6,1536]{2,1,0:T(8,128)}) custom-call(s32[23]{0:T(128)} %get-tuple-element.133.refs_0_, bf16[256,1536]{1,0:T(8,128)(2,1)} %get-tuple-element.200.refs_2_.refs_1_, bf16[128,1536]{1,0:T(8,128)(2,1)} %copy-done.39, bf16[128,1536]{1,0:T(8,128)(2,1)} %copy-done.40, ...), custom_call_target="tpu_custom_call" | custom-call | flops 13799999488 | bytes 12000000 | tf_op jit(solution)/shard_map/pallas_call | solution.py:1104
  641.6 8.3 %collective-permute-done.78.refs_3_ = bf16[96,1536]{1,0:T(8,128)(2,1)} collective-permute-done((bf16[96,1536]{1,0:T(8,128)(2,1)}, bf16[96,1536]{1,0:T(8,128)(2,1)}, u32[]{:S(2)}, u32[]{:S(2)}) %collective-permute-start.78) | collective-permute-done | bytes 294944 | tf_op jit(solution)/shard_map/ppermute | solution.py:848
  677.9 14.6 %collective-permute-start.72 = (f32[61,96]{1,0:T(8,128)S(1)}, f32[61,96]{1,0:T(8,128)S(1)}, u32[]{:S(2)}, u32[]{:S(2)}) collective-permute-start(f32[61,96]{1,0:T(8,128)S(1)} %get-tuple-element.247), channel_id=1, source_target_pairs={{0,16},{8,24},{16,0},{24,8},{1,17},{9,25},{17,1},{25,9},{2,18},{10... | collective-permute-start | bytes 70280 | tf_op jit(solution)/shard_map/ppermute | solution.py:939
  (411 shorter events, 351.2 us)
Async XLA Ops:
  7.2 92.1 %all-gather.5.cloned.1.call-start = ((), (), s32[]{:S(2)}) async-start(), calls=%async_computation.4 | async-start | bytes 4423680 | tf_op jit(solution)/shard_map/all_gather | solution.py:1124
  28.6 130.3 %all-gather.7.cloned.1.call-start = ((), (), s32[]{:S(2)}) async-start(), calls=%async_computation.5 | async-start | bytes 1474560 | tf_op jit(solution)/shard_map/all_gather | solution.py:1141
  39.0 33.2 %collective-permute-start.8 = (bf16[96,3456]{1,0:T(8,128)(2,1)}, bf16[96,3456]{1,0:T(8,128)(2,1)S(1)}, u32[]{:S(2)}, u32[]{:S(2)}) collective-permute-start(bf16[96,3456]{1,0:T(8,128)(2,1)} %get-tuple-element.138), channel_id=1, source_target_pairs={{0,4},{4,0},{1,5},{5,1},{2,6},{6,2},{3,7},{7,3},{8,12},{12,8},{9,1... | collective-permute-start | bytes 1990664 | tf_op jit(solution)/shard_map/ppermute | solution.py:848
  39.5 32.6 %collective-permute-start.9 = (bf16[96,3456]{1,0:T(8,128)(2,1)}, bf16[96,3456]{1,0:T(8,128)(2,1)S(1)}, u32[]{:S(2)}, u32[]{:S(2)}) collective-permute-start(bf16[96,3456]{1,0:T(8,128)(2,1)} %get-tuple-element.139), channel_id=1, source_target_pairs={{0,6},{2,4},{4,2},{6,0},{1,7},{3,5},{5,3},{7,1},{8,14},{10,12},{12... | collective-permute-start | bytes 1990664 | tf_op jit(solution)/shard_map/ppermute | solution.py:856
  44.4 34.5 %collective-permute-start.6 = (bf16[128,1536]{1,0:T(8,128)(2,1)}, bf16[128,1536]{1,0:T(8,128)(2,1)S(1)}, u32[]{:S(2)}, u32[]{:S(2)}) collective-permute-start(bf16[128,1536]{1,0:T(8,128)(2,1)} %shard_map.265), channel_id=1, source_target_pairs={{0,4},{4,0},{1,5},{5,1},{2,6},{6,2},{3,7},{7,3},{8,12},{12,8},{9,1... | collective-permute-start | bytes 1179656 | tf_op jit(solution)/shard_map/ppermute | solution.py:848
  49.9 31.5 %collective-permute-start.10 = (bf16[128,1536]{1,0:T(8,128)(2,1)}, bf16[128,1536]{1,0:T(8,128)(2,1)S(1)}, u32[]{:S(2)}, u32[]{:S(2)}) collective-permute-start(bf16[128,1536]{1,0:T(8,128)(2,1)} %shard_map.267), channel_id=1, source_target_pairs={{0,2},{2,0},{1,3},{3,1},{4,6},{6,4},{5,7},{7,5},{8,10},{10,8},{9,1... | collective-permute-start | bytes 1179656 | tf_op jit(solution)/shard_map/ppermute | solution.py:844
  91.3 150.6 %all-gather.9.cloned.1.call-start = ((), (), s32[]{:S(2)}) async-start(), calls=%async_computation.6 | async-start | bytes 5898240 | tf_op jit(solution)/shard_map/all_gather | solution.py:1158
  115.4 31.3 %collective-permute-start.17 = (bf16[1184,384]{1,0:T(8,128)(2,1)}, bf16[1184,384]{1,0:T(8,128)(2,1)S(1)}, u32[]{:S(2)}, u32[]{:S(2)}) collective-permute-start(bf16[1184,384]{1,0:T(8,128)(2,1)} %get-tuple-element.146), channel_id=1, source_target_pairs={{0,8},{8,16},{16,24},{1,9},{9,17},{17,25},{2,10},{10,18},{18,26},{... | collective-permute-start | bytes 2727944 | tf_op jit(solution)/shard_map/ppermute | solution.py:836
  116.7 32.0 %collective-permute-start.18 = (bf16[1184,384]{1,0:T(8,128)(2,1)}, bf16[1184,384]{1,0:T(8,128)(2,1)S(1)}, u32[]{:S(2)}, u32[]{:S(2)}) collective-permute-start(bf16[1184,384]{1,0:T(8,128)(2,1)} %get-tuple-element.147), channel_id=1, source_target_pairs={{8,0},{16,8},{24,16},{9,1},{17,9},{25,17},{10,2},{18,10},{26,18},{... | collective-permute-start | bytes 2727944 | tf_op jit(solution)/shard_map/ppermute | solution.py:836
  152.1 179.8 %all-gather.11.cloned.1.call-start = ((), (), s32[]{:S(2)}) async-start(), calls=%async_computation.7 | async-start | bytes 5898240 | tf_op jit(solution)/shard_map/all_gather | solution.py:1142
  211.7 40.1 %collective-permute-start.21 = (bf16[4,256,1536]{2,1,0:T(8,128)(2,1)S(1)}, bf16[4,256,1536]{2,1,0:T(8,128)(2,1)}, u32[]{:S(2)}, u32[]{:S(2)}) collective-permute-start(bf16[4,256,1536]{2,1,0:T(8,128)(2,1)S(1)} %pad_maximum_fusion.1.refs_1_), channel_id=1, source_target_pairs={{0,1},{1,0},{2,3},{3,2},{4,5},{5,4},{6,7},{7,6},{8,9},{9,8},{10,11... | collective-permute-start | bytes 9437192 | tf_op jit(solution)/shard_map/ppermute | solution.py:852
  211.8 214.3 %reduce-scatter.5.cloned.1.call-start = ((), (), s32[]{:S(2)}) async-start(), calls=%async_computation.8 | async-start | bytes 5898240 | tf_op jit(solution)/shard_map/reduce_scatter | solution.py:860
  218.9 26.5 %collective-permute-start.25 = (bf16[128,1536]{1,0:T(8,128)(2,1)}, bf16[128,1536]{1,0:T(8,128)(2,1)S(1)}, u32[]{:S(2)}, u32[]{:S(2)}) collective-permute-start(bf16[128,1536]{1,0:T(8,128)(2,1)} %get-tuple-element.162), channel_id=1, source_target_pairs={{0,4},{4,0},{1,5},{5,1},{2,6},{6,2},{3,7},{7,3},{8,12},{12,8},{9,1... | collective-permute-start | bytes 1179656 | tf_op jit(solution)/shard_map/ppermute | solution.py:848
  219.5 32.2 %collective-permute-start.23 = (bf16[128,1536]{1,0:T(8,128)(2,1)}, bf16[128,1536]{1,0:T(8,128)(2,1)}, u32[]{:S(2)}, u32[]{:S(2)}) collective-permute-start(bf16[128,1536]{1,0:T(8,128)(2,1)} %get-tuple-element.159), channel_id=1, source_target_pairs={{0,2},{2,0},{1,3},{3,1},{4,6},{6,4},{5,7},{7,5},{8,10},{10,8},{9,1... | collective-permute-start | bytes 1179656 | tf_op jit(solution)/shard_map/ppermute | solution.py:844
  220.0 31.8 %collective-permute-start.24 = (bf16[128,1536]{1,0:T(8,128)(2,1)}, bf16[128,1536]{1,0:T(8,128)(2,1)}, u32[]{:S(2)}, u32[]{:S(2)}) collective-permute-start(bf16[128,1536]{1,0:T(8,128)(2,1)} %get-tuple-element.160), channel_id=1, source_target_pairs={{0,4},{4,0},{1,5},{5,1},{2,6},{6,2},{3,7},{7,3},{8,12},{12,8},{9,1... | collective-permute-start | bytes 1179656 | tf_op jit(solution)/shard_map/ppermute | solution.py:848
  325.6 205.3 %reduce-scatter.7.cloned.1.call-start = ((), (), s32[]{:S(2)}) async-start(), calls=%async_computation.9 | async-start | bytes 5898240 | tf_op jit(solution)/shard_map/reduce_scatter | solution.py:860
  365.4 33.7 %collective-permute-start.35 = (bf16[128,1536]{1,0:T(8,128)(2,1)}, bf16[128,1536]{1,0:T(8,128)(2,1)S(1)}, u32[]{:S(2)}, u32[]{:S(2)}) collective-permute-start(bf16[128,1536]{1,0:T(8,128)(2,1)} %get-tuple-element.172.refs_7_), channel_id=1, source_target_pairs={{0,2},{2,0},{1,3},{3,1},{4,6},{6,4},{5,7},{7,5},{8,10},{10,8},{9,1... | collective-permute-start | bytes 1179656 | tf_op jit(solution)/shard_map/ppermute | solution.py:844
  366.0 33.2 %collective-permute-start.36 = (bf16[128,1536]{1,0:T(8,128)(2,1)}, bf16[128,1536]{1,0:T(8,128)(2,1)S(1)}, u32[]{:S(2)}, u32[]{:S(2)}) collective-permute-start(bf16[128,1536]{1,0:T(8,128)(2,1)} %get-tuple-element.173.refs_10_), channel_id=1, source_target_pairs={{0,4},{4,0},{1,5},{5,1},{2,6},{6,2},{3,7},{7,3},{8,12},{12,8},{9,1... | collective-permute-start | bytes 1179656 | tf_op jit(solution)/shard_map/ppermute | solution.py:848
  379.4 215.5 %reduce-scatter.9.cloned.1.call-start = ((), (), s32[]{:S(2)}) async-start(), calls=%async_computation.10 | async-start | bytes 1474560 | tf_op jit(solution)/shard_map/reduce_scatter | solution.py:860
  521.7 29.5 %collective-permute-start.53 = (bf16[128,1536]{1,0:T(8,128)(2,1)}, bf16[128,1536]{1,0:T(8,128)(2,1)S(1)}, u32[]{:S(2)}, u32[]{:S(2)}) collective-permute-start(bf16[128,1536]{1,0:T(8,128)(2,1)} %shard_map.300.refs_4_), channel_id=1, source_target_pairs={{0,4},{4,0},{1,5},{5,1},{2,6},{6,2},{3,7},{7,3},{8,12},{12,8},{9,1... | collective-permute-start | bytes 1179656 | tf_op jit(solution)/shard_map/ppermute | solution.py:848
  530.6 130.8 %reduce-scatter.11.cloned.1.call-start = ((), (), s32[]{:S(2)}) async-start(), calls=%async_computation.11 | async-start | bytes 4423680 | tf_op jit(solution)/shard_map/reduce_scatter | solution.py:860
  602.1 31.8 %collective-permute-start.80 = (bf16[96,1536]{1,0:T(8,128)(2,1)}, bf16[96,1536]{1,0:T(8,128)(2,1)}, u32[]{:S(2)}, u32[]{:S(2)}) collective-permute-start(bf16[96,1536]{1,0:T(8,128)(2,1)} %get-tuple-element.234), channel_id=1, source_target_pairs={{0,2},{2,0},{1,3},{3,1},{4,6},{6,4},{5,7},{7,5},{8,10},{10,8},{9,1... | collective-permute-start | bytes 884744 | tf_op jit(solution)/shard_map/ppermute | solution.py:844
  602.8 31.7 %collective-permute-start.81 = (bf16[96,1536]{1,0:T(8,128)(2,1)S(1)}, bf16[96,1536]{1,0:T(8,128)(2,1)}, u32[]{:S(2)}, u32[]{:S(2)}) collective-permute-start(bf16[96,1536]{1,0:T(8,128)(2,1)S(1)} %copy-done.55), channel_id=1, source_target_pairs={{0,4},{4,0},{1,5},{5,1},{2,6},{6,2},{3,7},{7,3},{8,12},{12,8},{9,1... | collective-permute-start | bytes 884744 | tf_op jit(solution)/shard_map/ppermute | solution.py:848
  636.7 30.3 %collective-permute-start.63 = (f32[256,1536]{1,0:T(8,128)S(1)}, f32[256,1536]{1,0:T(8,128)}, u32[]{:S(2)}, u32[]{:S(2)}) collective-permute-start(f32[256,1536]{1,0:T(8,128)S(1)} %copy-done.10), channel_id=1, source_target_pairs={{0,1},{1,0},{2,3},{3,2},{4,5},{5,4},{6,7},{7,6},{8,9},{9,8},{10,11... | collective-permute-start | bytes 4718600 | tf_op jit(solution)/shard_map/ppermute | solution.py:852
  (131 other events, 1374.1 us)
Sparse Core Ops, SparseCore 0:
  28.7 70.5 all-gather.4
  101.4 35.5 all-gather.6
  152.2 89.7 all-gather.8
  244.0 87.8 all-gather.10
  334.0 83.6 reduce-scatter.4
  419.9 85.7 reduce-scatter.6
  530.7 39.0 reduce-scatter.8
  572.2 72.6 reduce-scatter.10

commit v5 on v4

--- a/solution.py
+++ b/solution.py
@@ -813,7 +813,7 @@
 
 
 def gather_grads_kernel(info, dq, d_kv, near_back, near_on, far_back, far_on, out, total):
-    total[...] = d_kv[...]
+    total[...] = d_kv[...].astype(F32)
     for start, part in ((info[TAIL_FROM], near_back), (info[EDGE_FROM], far_back)):
         place, skip = window(start, part.shape[0], total.shape[0])
         total[place, :] += moved(part[...], skip)
@@ -1297,7 +1297,7 @@
         n_tiles,
         [SMEM, SMEM, tile_spec, tile_spec, tile_spec, *source_specs, log_spec],
         (tile_spec, *(kept(s.shape) for s in sources)),
-        (rows_of(mine, BF), pair(EDGE), pair(TAIL), rows_of(2 * mine, F32), pair(TAIL), pair(EDGE)),
+        (rows_of(mine, BF), pair(EDGE), pair(TAIL), pair(group_rows), pair(TAIL), pair(EDGE)),
         [
             scratch(reach, mine),
             scratch(reach, mine),

time: 714 us -> 708 us (level)
  starting transfers between devices: 96.1 us -> 86.4 us
    ppermute x3, starting transfers between devices: 14.7 us -> 3.87 us  [sums_of_shares(): lax.ppermute(pick(shares, lax.rem(g + step, groups)), 'g', pairs)]
  transfers between devices with their start and end apart: 87 -> 87, of which waited for: 38 -> 37; matrix products, arithmetic and copies ran while one was open for 5% -> 5% of each run, Pallas kernels for 46% -> 48%
where the time goes in v5:
time: 708 us; the launch traced here: 700 us
  Pallas kernels  337 us (48%)
  waiting for transfers between devices  204 us (29%)
  starting transfers between devices  86.4 us (12%)
  local copies, waits for them, and re-layouts  37 us (5%)
  other arithmetic  19 us (3%)
  between operations  16.1 us (2%)
    pallas_call x13, Pallas kernels, stepped(): return lambda *args: run(*args, *deps)  211 us
    ppermute x27, waiting for transfers between devices, over_x(): return lax.ppermute(value, 'x', SWAP)  88.2 us
    ppermute x27, waiting for transfers between devices, over_y(): return lax.ppermute(value, 'y', SWAP)  64 us
    pallas_call x20, Pallas kernels, sum_after(): pl.pallas_call(after(body, n, len(deps)), out_shape=jax.ShapeDtypeStruct(...  38.4 us
    ppermute x27, starting transfers between devices, over_x(): return lax.ppermute(value, 'x', SWAP)  32.7 us
    ppermute x27, starting transfers between devices, over_y(): return lax.ppermute(value, 'y', SWAP)  29.3 us
    pallas_call x4, Pallas kernels, rows_kernel(): pl.pallas_call(after(body, 1 + len(args), len(deps)), out_shape=tuple((ja...  28.3 us
    ppermute x11, waiting for transfers between devices, over_core(): return lax.ppermute(value, 'c', SWAP)  20.9 us
  transfers between devices with their start and end apart: 87, of which 37 were waited for; matrix products, arithmetic and copies ran while one was open for 5% of the time, Pallas kernels for 48%

profile of v5, /device:TPU:0, one launch (start us, length us, event | category | flops | bytes accessed | tf_op | source)
XLA Modules:
  0.0 700.1 jit_solution(16343200519601261091)
XLA Ops:
  56.0 16.2 %collective-permute-done.8.refs_2_.refs_3_ = bf16[96,3456]{1,0:T(8,128)(2,1)S(1)} collective-permute-done((bf16[96,3456]{1,0:T(8,128)(2,1)}, bf16[96,3456]{1,0:T(8,128)(2,1)S(1)}, u32[]{:S(2)}, u32[]{:S(2)}) %collective-permute-start.8) | collective-permute-done | bytes 663584 | tf_op jit(solution)/shard_map/ppermute | solution.py:848
  99.3 16.0 %shard_map.271 = (bf16[2048,192]{1,0:T(8,128)(2,1)}, bf16[2048,384]{1,0:T(8,128)(2,1)}, bf16[1184,384]{1,0:T(8,128)(2,1)}, bf16[160,384]{1,0:T(8,128)(2,1)S(1)},...) custom-call(s32[23]{0:T(128)} %get-tuple-element.133.refs_0_, bf16[4,256,1536]{2,1,0:T(8,128)(2,1)} %copy-done.7, ...), custom_call_target="tpu_custom_call" | custom-call | flops 6899999744 | bytes 6000000 | tf_op jit(solution)/shard_map/pallas_call | solution.py:85
  122.9 16.5 %collective-permute-done.15.refs_3_ = bf16[256,1536]{1,0:T(8,128)(2,1)S(1)} collective-permute-done((bf16[256,1536]{1,0:T(8,128)(2,1)}, bf16[256,1536]{1,0:T(8,128)(2,1)S(1)}, u32[]{:S(2)}, u32[]{:S(2)}) %collective-permute-start.15) | collective-permute-done | bytes 786464 | tf_op jit(solution)/shard_map/ppermute | solution.py:844
  162.5 31.6 %shard_map.277 = (bf16[2048,192]{1,0:T(8,128)(2,1)}, f32[2048,192]{1,0:T(8,128)}, f32[8,8,256]{2,1,0:T(8,128)}, f32[8,256]{1,0:T(8,128)}) custom-call(s32[64]{0:T(128)} %get-tuple-element.134.refs_0_, s32[6]{0:T(128)} %refs_1_.5, bf16[2048,192]{1,0:T(8,128)(2,1)} %get-tuple-element.144.refs_1_.refs_2_, bf16[160,384]{1,0:T(8,128)(2,1)} %get-tuple-element.151.refs_3_.refs_5_, ...), custom_call_target="tpu_custom_call" | custom-call | flops 1150000000 | bytes 1000000 | tf_op jit(solution)/shard_map/pallas_call | solution.py:85
  194.1 7.5 %shard_map.278 = (bf16[4,256,1536]{2,1,0:T(8,128)(2,1)}, bf16[4,256,1536]{2,1,0:T(8,128)(2,1)}) custom-call(s32[23]{0:T(128)} %get-tuple-element.133.refs_0_, bf16[2048,192]{1,0:T(8,128)(2,1)} %get-tuple-element.155.refs_1_.refs_3_, bf16[1536,384]{1,0:T(8,128)(2,1)} %all-gather.7.cloned.1.call-done.refs_3_.refs_2_), custom_call_target="tpu_custom_call" | custom-call | flops 1150000000 | bytes 1000000 | tf_op jit(solution)/shard_map/pallas_call | solution.py:85
  204.6 8.5 %collective-permute-done.19 = bf16[128,1536]{1,0:T(8,128)(2,1)S(1)} collective-permute-done((bf16[128,1536]{1,0:T(8,128)(2,1)S(1)}, bf16[128,1536]{1,0:T(8,128)(2,1)S(1)}, u32[]{:S(2)}, u32[]{:S(2)}) %collective-permute-start.19) | collective-permute-done | bytes 393248 | tf_op jit(solution)/shard_map/ppermute | solution.py:848
  226.3 8.3 %collective-permute-done.27.refs_1_ = bf16[128,1536]{1,0:T(8,128)(2,1)} collective-permute-done((bf16[128,1536]{1,0:T(8,128)(2,1)}, bf16[128,1536]{1,0:T(8,128)(2,1)}, u32[]{:S(2)}, u32[]{:S(2)}) %collective-permute-start.27) | collective-permute-done | bytes 393248 | tf_op jit(solution)/shard_map/ppermute | solution.py:844
  266.7 16.4 %collective-permute-done.29 = bf16[256,1536]{1,0:T(8,128)(2,1)S(1)} collective-permute-done((bf16[256,1536]{1,0:T(8,128)(2,1)}, bf16[256,1536]{1,0:T(8,128)(2,1)S(1)}, u32[]{:S(2)}, u32[]{:S(2)}) %collective-permute-start.29) | collective-permute-done | bytes 786464 | tf_op jit(solution)/shard_map/ppermute | solution.py:844
  285.4 7.4 %collective-permute-done.31 = bf16[128,1536]{1,0:T(8,128)(2,1)S(1)} collective-permute-done((bf16[128,1536]{1,0:T(8,128)(2,1)S(1)}, bf16[128,1536]{1,0:T(8,128)(2,1)S(1)}, u32[]{:S(2)}, u32[]{:S(2)}) %collective-permute-start.31) | collective-permute-done | bytes 393248 | tf_op jit(solution)/shard_map/ppermute | solution.py:848
  299.7 13.0 %shard_map.283 = (bf16[4,512,768]{2,1,0:T(8,128)(2,1)}, bf16[4,512,768]{2,1,0:T(8,128)(2,1)}) custom-call(s32[23]{0:T(128)} %get-tuple-element.133.refs_0_, bf16[4,256,1536]{2,1,0:T(8,128)(2,1)} %copy-done.2, bf16[4,256,1536]{2,1,0:T(8,128)(2,1)} %collective-permute-done.33.refs_2_, ...), custom_call_target="tpu_custom_call" | custom-call | flops 1150000000 | bytes 1000000 | tf_op jit(solution)/shard_map/pallas_call | solution.py:85
  312.7 12.0 %shard_map.284.refs_8_ = bf16[1536,1536]{1,0:T(8,128)(2,1)} custom-call(s32[23]{0:T(128)} %get-tuple-element.133.refs_0_, bf16[4,256,1536]{2,1,0:T(8,128)(2,1)} %copy-done, bf16[4,256,1536]{2,1,0:T(8,128)(2,1)} %collective-permute-done.21.refs_9_.refs_2_, bf16[4,512,768]{2,1,0:T(8,128)(2,1)} %get-tuple-element.168.refs_3_.refs_1_), custom_call_target="tpu_custom_call" | custom-call | flops 1150000000 | bytes 1000000 | tf_op jit(solution)/shard_map/pallas_call | solution.py:85
  331.9 19.1 %shard_map.285 = (bf16[4,256,1536]{2,1,0:T(8,128)(2,1)}, bf16[4,256,1536]{2,1,0:T(8,128)(2,1)}, bf16[4,512,768]{2,1,0:T(8,128)(2,1)}) custom-call(s32[23]{0:T(128)} %get-tuple-element.133.refs_0_, bf16[4,256,1536]{2,1,0:T(8,128)(2,1)} %copy-done, bf16[4,256,1536]{2,1,0:T(8,128)(2,1)} %collective-permute-done.21.refs_9_.refs_2_, ...), custom_call_target="tpu_custom_call" | custom-call | flops 1150000000 | bytes 1000000 | tf_op jit(solution)/shard_map/pallas_call | solution.py:85
  365.6 12.1 %shard_map.287.refs_2_ = bf16[1536,1536]{1,0:T(8,128)(2,1)} custom-call(s32[23]{0:T(128)} %get-tuple-element.133.refs_0_, bf16[4,256,1536]{2,1,0:T(8,128)(2,1)} %copy-done.2, bf16[4,256,1536]{2,1,0:T(8,128)(2,1)} %collective-permute-done.33.refs_2_, bf16[4,512,768]{2,1,0:T(8,128)(2,1)} %get-tuple-element.176.refs_3_, ...), custom_call_target="tpu_custom_call" | custom-call | flops 13799999488 | bytes 12000000 | tf_op jit(solution)/shard_map/pallas_call | solution.py:85
  386.2 10.4 %shard_map.290 = (bf16[4,256,1536]{2,1,0:T(8,128)(2,1)}, bf16[4,256,1536]{2,1,0:T(8,128)(2,1)}) custom-call(s32[23]{0:T(128)} %get-tuple-element.133.refs_0_, bf16[4,512,768]{2,1,0:T(8,128)(2,1)} %get-tuple-element.168.refs_3_.refs_1_, bf16[1536,1536]{1,0:T(8,128)(2,1)} %all-gather.11.cloned.1.call-done.refs_6_.refs_7_.refs_2_.refs_3_, ...), custom_call_target="tpu_custom_call" | custom-call | flops 28750000128 | bytes 25000000 | tf_op jit(solution)/shard_map/pallas_call | solution.py:85
  405.0 17.0 %collective-permute-done.41 = bf16[256,1536]{1,0:T(8,128)(2,1)S(1)} collective-permute-done((bf16[256,1536]{1,0:T(8,128)(2,1)}, bf16[256,1536]{1,0:T(8,128)(2,1)S(1)}, u32[]{:S(2)}, u32[]{:S(2)}) %collective-permute-start.41) | collective-permute-done | bytes 786464 | tf_op jit(solution)/shard_map/ppermute | solution.py:844
  438.8 9.0 %collective-permute-done.45.refs_2_ = bf16[4,256,1536]{2,1,0:T(8,128)(2,1)} collective-permute-done((bf16[4,256,1536]{2,1,0:T(8,128)(2,1)S(1)}, bf16[4,256,1536]{2,1,0:T(8,128)(2,1)}, u32[]{:S(2)}, u32[]{:S(2)}) %collective-permute-start.45) | collective-permute-done | bytes 3145760 | tf_op jit(solution)/shard_map/ppermute | solution.py:852
  447.7 7.4 %shard_map.294.refs_3_ = bf16[2048,192]{1,0:T(8,128)(2,1)} custom-call(s32[23]{0:T(128)} %get-tuple-element.133.refs_0_, bf16[4,256,1536]{2,1,0:T(8,128)(2,1)} %copy-done.1, bf16[4,256,1536]{2,1,0:T(8,128)(2,1)} %collective-permute-done.45.refs_2_, bf16[1536,384]{1,0:T(8,128)(2,1)} %all-gather.7.cloned.1.call-done.refs_3_.refs_2_), custom_call_target="tpu_custom_call" | custom-call | flops 1150000000 | bytes 1000000 | tf_op jit(solution)/shard_map/pallas_call | solution.py:85
  459.8 45.6 %shard_map.296 = (bf16[2048,192]{1,0:T(8,128)(2,1)}, bf16[160,384]{1,0:T(8,128)(2,1)S(1)}, bf16[1184,384]{1,0:T(8,128)(2,1)}, bf16[2048,384]{1,0:T(8,128)(2,1)},...) custom-call(s32[64]{0:T(128)} %get-tuple-element.134.refs_0_, s32[6]{0:T(128)} %refs_1_.5, ...), custom_call_target="tpu_custom_call" | custom-call | flops 1150000000 | bytes 1000000 | tf_op jit(solution)/shard_map/pallas_call | solution.py:85
  514.7 8.1 %shard_map.297.refs_7_.refs_2_.refs_0_ = bf16[1536,384]{1,0:T(8,128)(2,1)} custom-call(s32[23]{0:T(128)} %get-tuple-element.133.refs_0_, bf16[4,256,1536]{2,1,0:T(8,128)(2,1)} %copy-done.1, bf16[4,256,1536]{2,1,0:T(8,128)(2,1)} %collective-permute-done.45.refs_2_, bf16[2048,192]{1,0:T(8,128)(2,1)} %get-tuple-element.155.refs_1_.refs_3_, ...), custom_call_target="tpu_custom_call" | custom-call | flops 115000000 | bytes 100000 | tf_op jit(solution)/shard_map/pallas_call | solution.py:85
  541.3 13.1 %shard_map.301 = (bf16[4,256,1536]{2,1,0:T(8,128)(2,1)}, bf16[4,256,1536]{2,1,0:T(8,128)(2,1)}) custom-call(s32[23]{0:T(128)} %get-tuple-element.133.refs_0_, bf16[2048,576]{1,0:T(8,128)(2,1)} %shard_map.298.refs_1_.refs_3_, bf16[1536,1152]{1,0:T(8,128)(2,1)} %all-gather.5.cloned.1.call-done.refs_3_.refs_2_, bf16[128,1536]{1,0:T(8,128)(2,1)} %shard_map.299.refs_3_, ...), custom_call_target="tpu_custom_call" | custom-call | flops 115000000 | bytes 100000 | tf_op jit(solution)/shard_map/pallas_call | solution.py:85
  555.3 14.7 %shard_map.302.refs_2_ = bf16[1536,1152]{1,0:T(8,128)(2,1)} custom-call(s32[23]{0:T(128)} %get-tuple-element.133.refs_0_, bf16[4,256,1536]{2,1,0:T(8,128)(2,1)} %copy-done.7, bf16[4,256,1536]{2,1,0:T(8,128)(2,1)} %collective-permute-done.11.refs_2_, bf16[2048,576]{1,0:T(8,128)(2,1)} %shard_map.298.refs_1_.refs_3_, ...), custom_call_target="tpu_custom_call" | custom-call | flops 16099999744 | bytes 14000000 | tf_op jit(solution)/shard_map/pallas_call | solution.py:85
  607.0 7.9 %collective-permute-done.74.refs_2_ = bf16[96,384]{1,0:T(8,128)(2,1)S(1)} collective-permute-done((bf16[96,384]{1,0:T(8,128)(2,1)}, bf16[96,384]{1,0:T(8,128)(2,1)S(1)}, u32[]{:S(2)}, u32[]{:S(2)}) %collective-permute-start.74) | collective-permute-done | bytes 73760 | tf_op jit(solution)/shard_map/ppermute | solution.py:844
  619.5 12.3 %shard_map.310 = (f32[256,1536]{1,0:T(8,128)}, bf16[256,1536]{1,0:T(8,128)(2,1)}, f32[10,6,1536]{2,1,0:T(8,128)}) custom-call(s32[23]{0:T(128)} %get-tuple-element.133.refs_0_, bf16[256,1536]{1,0:T(8,128)(2,1)} %get-tuple-element.200.refs_2_.refs_1_, bf16[128,1536]{1,0:T(8,128)(2,1)} %copy-done.39, bf16[128,1536]{1,0:T(8,128)(2,1)} %copy-done.40, ...), custom_call_target="tpu_custom_call" | custom-call | flops 13799999488 | bytes 12000000 | tf_op jit(solution)/shard_map/pallas_call | solution.py:1104
  644.3 8.3 %collective-permute-done.78.refs_3_ = bf16[96,1536]{1,0:T(8,128)(2,1)} collective-permute-done((bf16[96,1536]{1,0:T(8,128)(2,1)}, bf16[96,1536]{1,0:T(8,128)(2,1)}, u32[]{:S(2)}, u32[]{:S(2)}) %collective-permute-start.78) | collective-permute-done | bytes 294944 | tf_op jit(solution)/shard_map/ppermute | solution.py:848
  (411 shorter events, 348.2 us)
Async XLA Ops:
  7.2 92.1 %all-gather.5.cloned.1.call-start = ((), (), s32[]{:S(2)}) async-start(), calls=%async_computation.4 | async-start | bytes 4423680 | tf_op jit(solution)/shard_map/all_gather | solution.py:1124
  28.6 130.3 %all-gather.7.cloned.1.call-start = ((), (), s32[]{:S(2)}) async-start(), calls=%async_computation.5 | async-start | bytes 1474560 | tf_op jit(solution)/shard_map/all_gather | solution.py:1141
  39.0 33.2 %collective-permute-start.8 = (bf16[96,3456]{1,0:T(8,128)(2,1)}, bf16[96,3456]{1,0:T(8,128)(2,1)S(1)}, u32[]{:S(2)}, u32[]{:S(2)}) collective-permute-start(bf16[96,3456]{1,0:T(8,128)(2,1)} %get-tuple-element.138), channel_id=1, source_target_pairs={{0,4},{4,0},{1,5},{5,1},{2,6},{6,2},{3,7},{7,3},{8,12},{12,8},{9,1... | collective-permute-start | bytes 1990664 | tf_op jit(solution)/shard_map/ppermute | solution.py:848
  39.5 32.6 %collective-permute-start.9 = (bf16[96,3456]{1,0:T(8,128)(2,1)}, bf16[96,3456]{1,0:T(8,128)(2,1)S(1)}, u32[]{:S(2)}, u32[]{:S(2)}) collective-permute-start(bf16[96,3456]{1,0:T(8,128)(2,1)} %get-tuple-element.139), channel_id=1, source_target_pairs={{0,6},{2,4},{4,2},{6,0},{1,7},{3,5},{5,3},{7,1},{8,14},{10,12},{12... | collective-permute-start | bytes 1990664 | tf_op jit(solution)/shard_map/ppermute | solution.py:856
  44.4 34.5 %collective-permute-start.6 = (bf16[128,1536]{1,0:T(8,128)(2,1)}, bf16[128,1536]{1,0:T(8,128)(2,1)S(1)}, u32[]{:S(2)}, u32[]{:S(2)}) collective-permute-start(bf16[128,1536]{1,0:T(8,128)(2,1)} %shard_map.265), channel_id=1, source_target_pairs={{0,4},{4,0},{1,5},{5,1},{2,6},{6,2},{3,7},{7,3},{8,12},{12,8},{9,1... | collective-permute-start | bytes 1179656 | tf_op jit(solution)/shard_map/ppermute | solution.py:848
  49.9 31.5 %collective-permute-start.10 = (bf16[128,1536]{1,0:T(8,128)(2,1)}, bf16[128,1536]{1,0:T(8,128)(2,1)S(1)}, u32[]{:S(2)}, u32[]{:S(2)}) collective-permute-start(bf16[128,1536]{1,0:T(8,128)(2,1)} %shard_map.267), channel_id=1, source_target_pairs={{0,2},{2,0},{1,3},{3,1},{4,6},{6,4},{5,7},{7,5},{8,10},{10,8},{9,1... | collective-permute-start | bytes 1179656 | tf_op jit(solution)/shard_map/ppermute | solution.py:844
  91.3 150.6 %all-gather.9.cloned.1.call-start = ((), (), s32[]{:S(2)}) async-start(), calls=%async_computation.6 | async-start | bytes 5898240 | tf_op jit(solution)/shard_map/all_gather | solution.py:1158
  115.3 31.4 %collective-permute-start.17 = (bf16[1184,384]{1,0:T(8,128)(2,1)}, bf16[1184,384]{1,0:T(8,128)(2,1)S(1)}, u32[]{:S(2)}, u32[]{:S(2)}) collective-permute-start(bf16[1184,384]{1,0:T(8,128)(2,1)} %get-tuple-element.146), channel_id=1, source_target_pairs={{0,8},{8,16},{16,24},{1,9},{9,17},{17,25},{2,10},{10,18},{18,26},{... | collective-permute-start | bytes 2727944 | tf_op jit(solution)/shard_map/ppermute | solution.py:836
  116.6 32.1 %collective-permute-start.18 = (bf16[1184,384]{1,0:T(8,128)(2,1)}, bf16[1184,384]{1,0:T(8,128)(2,1)S(1)}, u32[]{:S(2)}, u32[]{:S(2)}) collective-permute-start(bf16[1184,384]{1,0:T(8,128)(2,1)} %get-tuple-element.147), channel_id=1, source_target_pairs={{8,0},{16,8},{24,16},{9,1},{17,9},{25,17},{10,2},{18,10},{26,18},{... | collective-permute-start | bytes 2727944 | tf_op jit(solution)/shard_map/ppermute | solution.py:836
  152.1 179.8 %all-gather.11.cloned.1.call-start = ((), (), s32[]{:S(2)}) async-start(), calls=%async_computation.7 | async-start | bytes 5898240 | tf_op jit(solution)/shard_map/all_gather | solution.py:1142
  216.5 35.3 %collective-permute-start.21 = (bf16[4,256,1536]{2,1,0:T(8,128)(2,1)S(1)}, bf16[4,256,1536]{2,1,0:T(8,128)(2,1)}, u32[]{:S(2)}, u32[]{:S(2)}) collective-permute-start(bf16[4,256,1536]{2,1,0:T(8,128)(2,1)S(1)} %pad_maximum_fusion.1.refs_1_), channel_id=1, source_target_pairs={{0,1},{1,0},{2,3},{3,2},{4,5},{5,4},{6,7},{7,6},{8,9},{9,8},{10,11... | collective-permute-start | bytes 9437192 | tf_op jit(solution)/shard_map/ppermute | solution.py:852
  216.6 207.0 %reduce-scatter.5.cloned.1.call-start = ((), (), s32[]{:S(2)}) async-start(), calls=%async_computation.8 | async-start | bytes 5898240 | tf_op jit(solution)/shard_map/reduce_scatter | solution.py:860
  224.3 27.5 %collective-permute-start.23 = (bf16[128,1536]{1,0:T(8,128)(2,1)}, bf16[128,1536]{1,0:T(8,128)(2,1)}, u32[]{:S(2)}, u32[]{:S(2)}) collective-permute-start(bf16[128,1536]{1,0:T(8,128)(2,1)} %get-tuple-element.159), channel_id=1, source_target_pairs={{0,2},{2,0},{1,3},{3,1},{4,6},{6,4},{5,7},{7,5},{8,10},{10,8},{9,1... | collective-permute-start | bytes 1179656 | tf_op jit(solution)/shard_map/ppermute | solution.py:844
  224.6 27.1 %collective-permute-start.24 = (bf16[128,1536]{1,0:T(8,128)(2,1)}, bf16[128,1536]{1,0:T(8,128)(2,1)}, u32[]{:S(2)}, u32[]{:S(2)}) collective-permute-start(bf16[128,1536]{1,0:T(8,128)(2,1)} %get-tuple-element.160), channel_id=1, source_target_pairs={{0,4},{4,0},{1,5},{5,1},{2,6},{6,2},{3,7},{7,3},{8,12},{12,8},{9,1... | collective-permute-start | bytes 1179656 | tf_op jit(solution)/shard_map/ppermute | solution.py:848
  324.8 210.0 %reduce-scatter.7.cloned.1.call-start = ((), (), s32[]{:S(2)}) async-start(), calls=%async_computation.9 | async-start | bytes 5898240 | tf_op jit(solution)/shard_map/reduce_scatter | solution.py:860
  364.6 32.0 %collective-permute-start.35 = (bf16[128,1536]{1,0:T(8,128)(2,1)}, bf16[128,1536]{1,0:T(8,128)(2,1)S(1)}, u32[]{:S(2)}, u32[]{:S(2)}) collective-permute-start(bf16[128,1536]{1,0:T(8,128)(2,1)} %get-tuple-element.172.refs_7_), channel_id=1, source_target_pairs={{0,2},{2,0},{1,3},{3,1},{4,6},{6,4},{5,7},{7,5},{8,10},{10,8},{9,1... | collective-permute-start | bytes 1179656 | tf_op jit(solution)/shard_map/ppermute | solution.py:844
  365.1 31.4 %collective-permute-start.36 = (bf16[128,1536]{1,0:T(8,128)(2,1)}, bf16[128,1536]{1,0:T(8,128)(2,1)S(1)}, u32[]{:S(2)}, u32[]{:S(2)}) collective-permute-start(bf16[128,1536]{1,0:T(8,128)(2,1)} %get-tuple-element.173.refs_10_), channel_id=1, source_target_pairs={{0,4},{4,0},{1,5},{5,1},{2,6},{6,2},{3,7},{7,3},{8,12},{12,8},{9,1... | collective-permute-start | bytes 1179656 | tf_op jit(solution)/shard_map/ppermute | solution.py:848
  377.7 220.6 %reduce-scatter.9.cloned.1.call-start = ((), (), s32[]{:S(2)}) async-start(), calls=%async_computation.10 | async-start | bytes 1474560 | tf_op jit(solution)/shard_map/reduce_scatter | solution.py:860
  525.5 28.9 %collective-permute-start.53 = (bf16[128,1536]{1,0:T(8,128)(2,1)}, bf16[128,1536]{1,0:T(8,128)(2,1)S(1)}, u32[]{:S(2)}, u32[]{:S(2)}) collective-permute-start(bf16[128,1536]{1,0:T(8,128)(2,1)} %shard_map.300.refs_4_), channel_id=1, source_target_pairs={{0,4},{4,0},{1,5},{5,1},{2,6},{6,2},{3,7},{7,3},{8,12},{12,8},{9,1... | collective-permute-start | bytes 1179656 | tf_op jit(solution)/shard_map/ppermute | solution.py:848
  529.4 25.0 %collective-permute-start.52 = (bf16[128,1536]{1,0:T(8,128)(2,1)}, bf16[128,1536]{1,0:T(8,128)(2,1)S(1)}, u32[]{:S(2)}, u32[]{:S(2)}) collective-permute-start(bf16[128,1536]{1,0:T(8,128)(2,1)} %shard_map.299.refs_3_), channel_id=1, source_target_pairs={{0,2},{2,0},{1,3},{3,1},{4,6},{6,4},{5,7},{7,5},{8,10},{10,8},{9,1... | collective-permute-start | bytes 1179656 | tf_op jit(solution)/shard_map/ppermute | solution.py:844
  534.5 129.6 %reduce-scatter.11.cloned.1.call-start = ((), (), s32[]{:S(2)}) async-start(), calls=%async_computation.11 | async-start | bytes 4423680 | tf_op jit(solution)/shard_map/reduce_scatter | solution.py:860
  604.9 31.8 %collective-permute-start.80 = (bf16[96,1536]{1,0:T(8,128)(2,1)}, bf16[96,1536]{1,0:T(8,128)(2,1)}, u32[]{:S(2)}, u32[]{:S(2)}) collective-permute-start(bf16[96,1536]{1,0:T(8,128)(2,1)} %get-tuple-element.234), channel_id=1, source_target_pairs={{0,2},{2,0},{1,3},{3,1},{4,6},{6,4},{5,7},{7,5},{8,10},{10,8},{9,1... | collective-permute-start | bytes 884744 | tf_op jit(solution)/shard_map/ppermute | solution.py:844
  606.1 31.8 %collective-permute-start.81 = (bf16[96,1536]{1,0:T(8,128)(2,1)S(1)}, bf16[96,1536]{1,0:T(8,128)(2,1)}, u32[]{:S(2)}, u32[]{:S(2)}) collective-permute-start(bf16[96,1536]{1,0:T(8,128)(2,1)S(1)} %copy-done.55), channel_id=1, source_target_pairs={{0,4},{4,0},{1,5},{5,1},{2,6},{6,2},{3,7},{7,3},{8,12},{12,8},{9,1... | collective-permute-start | bytes 884744 | tf_op jit(solution)/shard_map/ppermute | solution.py:848
  639.7 30.0 %collective-permute-start.63 = (f32[256,1536]{1,0:T(8,128)S(1)}, f32[256,1536]{1,0:T(8,128)}, u32[]{:S(2)}, u32[]{:S(2)}) collective-permute-start(f32[256,1536]{1,0:T(8,128)S(1)} %copy-done.10), channel_id=1, source_target_pairs={{0,1},{1,0},{2,3},{3,2},{4,5},{5,4},{6,7},{7,6},{8,9},{9,8},{10,11... | collective-permute-start | bytes 4718600 | tf_op jit(solution)/shard_map/ppermute | solution.py:852
  (131 other events, 1359.2 us)
Sparse Core Ops, SparseCore 0:
  28.7 70.5 all-gather.4
  101.4 35.6 all-gather.6
  152.2 89.7 all-gather.8
  244.0 87.8 all-gather.10
  334.0 83.6 reduce-scatter.4
  419.9 85.7 reduce-scatter.6
  534.6 27.9 reduce-scatter.8
  570.2 65.9 reduce-scatter.10
